TPU v7x, 512 devices: a whole 4x8x8 slice. The times are simulated.
512 devices in a mesh: hist: 4 (over y_hi, core), seq: 128 (over z, y_lo, x).
Axes of the slice: x: 4, y: 8 (y_hi: 2, y_lo: 4; y = y_hi * 4 + y_lo), z: 8, core: 2. Of those that a mesh axis runs over, the one named last changes fastest.
Arguments:
- queries: bfloat16 [131072, 1600], P(('hist', 'seq')), parts along dimension 0, may hold values from -6 to 6, as said below
- keys: bfloat16 [131072, 1600], P(('hist', 'seq')), parts along dimension 0, may hold values from -6 to 6, as said below
- values: bfloat16 [131072, 1600], P(('hist', 'seq')), parts along dimension 0, may hold values from -6 to 6
Outputs:
- attended: bfloat16 [131072, 1600], P(('hist', 'seq')), parts along dimension 0
There are 4 independent parts, one for each index of `hist`. A program takes and returns all parts, laid end to end along the dimension named above; each array names one. Nothing has to cross between parts.
Inputs may be any that keep to these rules, and one draw needn't show every extreme that they name: `queries`: entries of the query and key projections. `keys`: entries of the query and key projections.
All inputs are finite; a program needn't handle non-finite values.
Results may differ from a plain program's by a relative error of at most 0.009.
Values may be sent and summed in bfloat16 or wider, within the bound.
No kernel may reach another device: no remote copies, remote signals or barrier semaphores. Data moves between devices by JAX's collectives and lax.ppermute only.
A program may use at most 64 MiB of HBM per device.

v0:
```python
import jax
import jax.numpy as jnp
from jax import lax
from jax.sharding import PartitionSpec as P

HEADS = 25
WIN = 3


neg_large = -1e30


def from_behind(shard, axis, by):
    length = lax.axis_size(axis)
    pairs = [(i, i + by) for i in range(length) if 0 <= i + by < length]
    return lax.ppermute(shard, axis, pairs)


def block_partial(query_rows, key_rows, value_rows, allowed):
    rows = query_rows.shape[0]
    span = key_rows.shape[0]
    heads = HEADS
    width = query_rows.shape[1] // heads
    qsplit = query_rows.reshape(rows, heads, width)
    ksplit = key_rows.reshape(span, heads, width)
    vsplit = value_rows.reshape(span, heads, width)
    score = jnp.einsum(
        "qhd,khd->hqk", qsplit, ksplit, preferred_element_type=jnp.float32
    ) * width ** (-0.5)
    score = jnp.where(allowed[None], score, neg_large)
    top = jnp.max(score, axis=-1)
    expo = jnp.where(allowed[None], jnp.exp(score - top[..., None]), 0.0)
    total = jnp.sum(expo, axis=-1)
    low_weight = expo.astype(jnp.bfloat16)
    summed = jnp.einsum("hqk,khd->hqd", low_weight, vsplit, preferred_element_type=jnp.float32)
    return (top, total, summed)


def merge_state(state, other):
    top_a, total_a, summed_a = state
    top_b, total_b, summed_b = other
    top_new = jnp.maximum(top_a, top_b)
    factor_a = jnp.exp(top_a - top_new)
    factor_b = jnp.exp(top_b - top_new)
    total_new = total_a * factor_a + total_b * factor_b
    summed_new = summed_a * factor_a[..., None] + summed_b * factor_b[..., None]
    return (top_new, total_new, summed_new)


def earlier_block(state, queries, pair, distance, position):
    rows = queries.shape[0]
    valid = position >= distance
    allowed = jnp.broadcast_to(valid, (rows, rows))
    return merge_state(state, block_partial(queries, pair[0], pair[1], allowed))


def shards(queries, keys, values):
    rows = queries.shape[0]
    position = lax.axis_index("seq")
    local = jnp.arange(rows, dtype=jnp.int32)
    causal = local[None, :] <= local[:, None]
    state = block_partial(queries, keys, values, causal)
    pair = (keys, values)
    for distance in range(1, WIN + 1):
        pair = from_behind((pair[0], pair[1]), "seq", 1)
        state = earlier_block(state, queries, pair, distance, position)
    top, total, summed = state
    mixed = summed / total[..., None]
    return jnp.transpose(mixed, (1, 0, 2)).reshape(rows, -1).astype(jnp.bfloat16)


def solution(mesh):
    return jax.shard_map(
        shards,
        mesh=mesh,
        in_specs=(P(("hist", "seq"), None), P(("hist", "seq"), None), P(("hist", "seq"), None)),
        out_specs=P(("hist", "seq"), None),
        check_vma=False,
    )
```

profile of v0, /device:TPU:288, one launch (start us, length us, event | category | flops | bytes accessed | tf_op | source)
XLA Modules:
  0.0 119.0 jit_solution(9946403082120205982)
XLA Ops:
  0.0 0.0 copy-start
  0.0 0.0 copy-start.1
  0.0 3.5 %collective-permute-start = (bf16[256,1600]{0,1:T(8,128)(2,1)}, bf16[256,1600]{0,1:T(8,128)(2,1)S(1)}, u32[]{:S(2)}, u32[]{:S(2)}) collective-permute-start(bf16[256,1600]{0,1:T(8,128)(2,1)} %param.4), channel_id=1, source_target_pairs={{0,1},{1,2},{2,3},{3,4},{4,5},{5,6},{6,7},{7,8},{8,9},{9,10},{10,1... | collective-permute-start | bytes 2457608 | tf_op jit(solution)/shard_map/ppermute | solution.py:16
  3.5 3.4 %collective-permute-start.1 = (bf16[256,1600]{0,1:T(8,128)(2,1)}, bf16[256,1600]{0,1:T(8,128)(2,1)S(1)}, u32[]{:S(2)}, u32[]{:S(2)}) collective-permute-start(bf16[256,1600]{0,1:T(8,128)(2,1)} %param.5), channel_id=1, source_target_pairs={{0,1},{1,2},{2,3},{3,4},{4,5},{5,6},{6,7},{7,8},{8,9},{9,10},{10,1... | collective-permute-start | bytes 2457608 | tf_op jit(solution)/shard_map/ppermute | solution.py:16
  7.0 0.0 copy-done
  7.0 5.1 %fusion = (f32[25,256]{1,0:T(8,128)S(1)}, f32[25,256,256]{1,2,0:T(8,128)}) fusion(pred[256,256]{0,1:T(8,128)(4,1)S(1)} %iota_compare_fusion, bf16[256,25,64]{0,2,1:T(8,128)(2,1)S(1)} %bitcast.119, bf16[256,25,64]{0,2,1:T(8,128)(2,1)} %bitcast.126), kind=kOutput, calls=%fused_computation.8 | convolution fusion | flops 214624000 | bytes 8283136 | tf_op jit(solution)/shard_map/qhd,khd->hqk/dot_general | solution.py:27
  12.1 0.0 slice-start
  12.1 0.0 copy-done.1
  12.1 0.0 slice-start.1
  12.1 4.6 %fusion.18 = f32[25,256,64]{1,2,0:T(8,128)S(1)} fusion(bf16[256,25,64]{0,2,1:T(8,128)(2,1)S(1)} %bitcast.127, f32[25,256,256]{1,2,0:T(8,128)} %get-tuple-element.17, f32[25,256]{1,0:T(8,128)S(1)} %get-tuple-element.16, pred[256,256]{0,1:T(8,128)(4,1)S(1)} %iota_compare_fusion), kind=kOutput, calls=%fused_computation.23 | convolution fusion | flops 217907200 | bytes 9102336 | tf_op jit(solution)/shard_map/hqk,khd->hqd/dot_general | solution.py:35
  16.7 12.7 %collective-permute-done = bf16[256,1600]{0,1:T(8,128)(2,1)S(1)} collective-permute-done((bf16[256,1600]{0,1:T(8,128)(2,1)}, bf16[256,1600]{0,1:T(8,128)(2,1)S(1)}, u32[]{:S(2)}, u32[]{:S(2)}) %collective-permute-start) | collective-permute-done | bytes 819232 | tf_op jit(solution)/shard_map/ppermute | solution.py:16
  29.4 1.1 fusion.1
  30.5 1.9 %collective-permute-start.2 = (bf16[256,1600]{0,1:T(8,128)(2,1)S(1)}, bf16[256,1600]{0,1:T(8,128)(2,1)S(1)}, u32[]{:S(2)}, u32[]{:S(2)}) collective-permute-start(bf16[256,1600]{0,1:T(8,128)(2,1)S(1)} %collective-permute-done), channel_id=1, source_target_pairs={{0,1},{1,2},{2,3},{3,4},{4,5},{5,6},{6,7},{7,8},{8,9},{9,10},{10,1... | collective-permute-start | bytes 2457608 | tf_op jit(solution)/shard_map/ppermute | solution.py:16
  32.4 0.0 slice-done
  32.4 0.0 slice-done.1
  32.5 3.3 %fusion.4 = (f32[25,256]{1,0:T(8,128)S(1)}, f32[25,256]{1,0:T(8,128)S(1)}) fusion(f32[25,256,256]{1,2,0:T(8,128)S(1)} %bitcast.122, f32[25,256]{1,0:T(8,128)S(1)} %get-tuple-element.16, pred[256,256]{0,1:T(8,128)(4,1)S(1)} %iota_compare_fusion, f32[25,256]{1,0:T(8,128)S(1)} %get-tuple-element.14, f32[25,256,256]{1,2,0:T(8,128)S(1)} %get-tuple-element.15, ...), kind=kLoop, calls=%fused_computation.12 | loop fusion | flops 16371200 | bytes 13275137 | tf_op jit(solution)/shard_map/reduce_sum | solution.py:33
  35.8 11.2 %collective-permute-done.1 = bf16[256,1600]{0,1:T(8,128)(2,1)S(1)} collective-permute-done((bf16[256,1600]{0,1:T(8,128)(2,1)}, bf16[256,1600]{0,1:T(8,128)(2,1)S(1)}, u32[]{:S(2)}, u32[]{:S(2)}) %collective-permute-start.1) | collective-permute-done | bytes 819232 | tf_op jit(solution)/shard_map/ppermute | solution.py:16
  46.9 1.9 %collective-permute-start.3 = (bf16[256,1600]{0,1:T(8,128)(2,1)S(1)}, bf16[256,1600]{0,1:T(8,128)(2,1)S(1)}, u32[]{:S(2)}, u32[]{:S(2)}) collective-permute-start(bf16[256,1600]{0,1:T(8,128)(2,1)S(1)} %collective-permute-done.1), channel_id=1, source_target_pairs={{0,1},{1,2},{2,3},{3,4},{4,5},{5,6},{6,7},{7,8},{8,9},{9,10},{10,1... | collective-permute-start | bytes 2457608 | tf_op jit(solution)/shard_map/ppermute | solution.py:16
  48.9 1.4 %fusion.16 = f32[25,256,64]{1,2,0:T(8,128)S(1)} fusion(bf16[256,25,64]{0,2,1:T(8,128)(2,1)S(1)} %bitcast.128, f32[25,256,256]{1,2,0:T(8,128)S(1)} %get-tuple-element.15, f32[25,256]{1,0:T(8,128)S(1)} %get-tuple-element.14, pred[]{:T(512)S(6)} %ge.9), kind=kOutput, calls=%fused_computation.22 | convolution fusion | flops 217907200 | bytes 9036801 | tf_op jit(solution)/shard_map/hqk,khd->hqd/dot_general | solution.py:35
  50.3 14.2 %collective-permute-done.2 = bf16[256,1600]{0,1:T(8,128)(2,1)S(1)} collective-permute-done((bf16[256,1600]{0,1:T(8,128)(2,1)S(1)}, bf16[256,1600]{0,1:T(8,128)(2,1)S(1)}, u32[]{:S(2)}, u32[]{:S(2)}) %collective-permute-start.2) | collective-permute-done | bytes 819232 | tf_op jit(solution)/shard_map/ppermute | solution.py:16
  64.5 1.9 %collective-permute-start.4 = (bf16[256,1600]{0,1:T(8,128)(2,1)S(1)}, bf16[256,1600]{0,1:T(8,128)(2,1)S(1)}, u32[]{:S(2)}, u32[]{:S(2)}) collective-permute-start(bf16[256,1600]{0,1:T(8,128)(2,1)S(1)} %collective-permute-done.2), channel_id=1, source_target_pairs={{0,1},{1,2},{2,3},{3,4},{4,5},{5,6},{6,7},{7,8},{8,9},{9,10},{10,1... | collective-permute-start | bytes 2457608 | tf_op jit(solution)/shard_map/ppermute | solution.py:16
  66.4 1.1 fusion.2
  67.5 14.5 %collective-permute-done.3 = bf16[256,1600]{0,1:T(8,128)(2,1)S(1)} collective-permute-done((bf16[256,1600]{0,1:T(8,128)(2,1)S(1)}, bf16[256,1600]{0,1:T(8,128)(2,1)S(1)}, u32[]{:S(2)}, u32[]{:S(2)}) %collective-permute-start.3) | collective-permute-done | bytes 819232 | tf_op jit(solution)/shard_map/ppermute | solution.py:16
  82.0 2.1 %collective-permute-start.5 = (bf16[256,1600]{0,1:T(8,128)(2,1)S(1)}, bf16[256,1600]{0,1:T(8,128)(2,1)S(1)}, u32[]{:S(2)}, u32[]{:S(2)}) collective-permute-start(bf16[256,1600]{0,1:T(8,128)(2,1)S(1)} %collective-permute-done.3), channel_id=1, source_target_pairs={{0,1},{1,2},{2,3},{3,4},{4,5},{5,6},{6,7},{7,8},{8,9},{9,10},{10,1... | collective-permute-start | bytes 2457608 | tf_op jit(solution)/shard_map/ppermute | solution.py:16
  84.1 1.5 %fusion.14 = f32[25,256,64]{1,2,0:T(8,128)S(1)} fusion(bf16[256,25,64]{0,2,1:T(8,128)(2,1)S(1)} %bitcast.129, f32[25,256,256]{1,2,0:T(8,128)S(1)} %get-tuple-element.13, f32[25,256]{1,0:T(8,128)S(1)} %get-tuple-element.12, pred[]{:T(512)S(6)} %ge.10), kind=kOutput, calls=%fused_computation.21 | convolution fusion | flops 217907200 | bytes 9036801 | tf_op jit(solution)/shard_map/hqk,khd->hqd/dot_general | solution.py:35
  85.6 14.0 %collective-permute-done.4 = bf16[256,1600]{0,1:T(8,128)(2,1)S(1)} collective-permute-done((bf16[256,1600]{0,1:T(8,128)(2,1)S(1)}, bf16[256,1600]{0,1:T(8,128)(2,1)S(1)}, u32[]{:S(2)}, u32[]{:S(2)}) %collective-permute-start.4) | collective-permute-done | bytes 819232 | tf_op jit(solution)/shard_map/ppermute | solution.py:16
  99.6 1.1 fusion.3
  100.7 3.3 %fusion.8 = (f32[25,256]{1,0:T(8,128)S(1)}, f32[25,256]{1,0:T(8,128)S(1)}) fusion(f32[25,256,256]{1,2,0:T(8,128)S(1)} %get-tuple-element.13, f32[25,256]{1,0:T(8,128)S(1)} %get-tuple-element.12, pred[]{:T(512)S(6)} %ge.10, f32[25,256]{1,0:T(8,128)S(1)} %get-tuple-element.18, f32[25,256,256]{1,2,0:T(8,128)S(1)} %get-tuple-element.19, pred[]{:T(512)S(6)} %ge.11), kind=kLoop, calls=%fused_computation.16 | loop fusion | flops 16371200 | bytes 13209602 | tf_op jit(solution)/shard_map/reduce_sum | solution.py:33
  104.1 11.9 %collective-permute-done.5 = bf16[256,1600]{0,1:T(8,128)(2,1)S(1)} collective-permute-done((bf16[256,1600]{0,1:T(8,128)(2,1)S(1)}, bf16[256,1600]{0,1:T(8,128)(2,1)S(1)}, u32[]{:S(2)}, u32[]{:S(2)}) %collective-permute-start.5) | collective-permute-done | bytes 819232 | tf_op jit(solution)/shard_map/ppermute | solution.py:16
  116.0 3.0 %fusion.26 = bf16[256,25,64]{0,2,1:T(8,128)(2,1)} fusion(f32[25,256,64]{1,2,0:T(8,128)S(1)} %fusion.14, f32[25,256,64]{1,2,0:T(8,128)S(1)} %fusion.16, f32[25,256,64]{1,2,0:T(8,128)S(1)} %fusion.18, bf16[256,25,64]{0,2,1:T(8,128)(2,1)S(1)} %bitcast.130, f32[25,256,256]{1,2,0:T(8,128)S(1)} %get-tuple-element.19, f32[25,256]{1,0:T(8,128)S(1)} %get-tuple-element.18, ...), kind=kOutput, calls=%fused_computation.31 | convolution fusion | flops 222412800 | bytes 13312001 | tf_op jit(solution)/shard_map/hqk,khd->hqd/dot_general | solution.py:35
  (3 shorter events, 0.1 us)
Async XLA Ops:
  0.0 7.0 %copy-start = (bf16[256,1600]{0,1:T(8,128)(2,1)S(1)}, bf16[256,1600]{0,1:T(8,128)(2,1)}, u32[]{:S(2)}) copy-start(bf16[256,1600]{0,1:T(8,128)(2,1)} %param.3) | copy-start | bytes 2457604
  0.0 12.1 %copy-start.1 = (bf16[256,1600]{0,1:T(8,128)(2,1)S(1)}, bf16[256,1600]{0,1:T(8,128)(2,1)}, u32[]{:S(2)}) copy-start(bf16[256,1600]{0,1:T(8,128)(2,1)} %param.5) | copy-start | bytes 2457604
  0.0 29.4 %collective-permute-start = (bf16[256,1600]{0,1:T(8,128)(2,1)}, bf16[256,1600]{0,1:T(8,128)(2,1)S(1)}, u32[]{:S(2)}, u32[]{:S(2)}) collective-permute-start(bf16[256,1600]{0,1:T(8,128)(2,1)} %param.4), channel_id=1, source_target_pairs={{0,1},{1,2},{2,3},{3,4},{4,5},{5,6},{6,7},{7,8},{8,9},{9,10},{10,1... | collective-permute-start | bytes 2457608 | tf_op jit(solution)/shard_map/ppermute | solution.py:16
  3.5 43.4 %collective-permute-start.1 = (bf16[256,1600]{0,1:T(8,128)(2,1)}, bf16[256,1600]{0,1:T(8,128)(2,1)S(1)}, u32[]{:S(2)}, u32[]{:S(2)}) collective-permute-start(bf16[256,1600]{0,1:T(8,128)(2,1)} %param.5), channel_id=1, source_target_pairs={{0,1},{1,2},{2,3},{3,4},{4,5},{5,6},{6,7},{7,8},{8,9},{9,10},{10,1... | collective-permute-start | bytes 2457608 | tf_op jit(solution)/shard_map/ppermute | solution.py:16
  12.1 20.4 %slice-start = ((s8[6553600]{0:T(1024)(128)(4,1)}), s8[4194304]{0:T(1024)(128)(4,1)S(1)}, s32[]{:S(2)}) async-start(s8[6553600]{0:T(1024)(128)(4,1)} %bitcast.121), calls=%async_computation | async-start | bytes 8388608
  12.1 20.4 %slice-start.1 = ((s8[6553600]{0:T(1024)(128)(4,1)}), s8[2359296]{0:T(1024)(128)(4,1)S(1)}, s32[]{:S(2)}) async-start(s8[6553600]{0:T(1024)(128)(4,1)} %bitcast.121), calls=%async_computation.1 | async-start | bytes 4718592
  30.5 34.0 %collective-permute-start.2 = (bf16[256,1600]{0,1:T(8,128)(2,1)S(1)}, bf16[256,1600]{0,1:T(8,128)(2,1)S(1)}, u32[]{:S(2)}, u32[]{:S(2)}) collective-permute-start(bf16[256,1600]{0,1:T(8,128)(2,1)S(1)} %collective-permute-done), channel_id=1, source_target_pairs={{0,1},{1,2},{2,3},{3,4},{4,5},{5,6},{6,7},{7,8},{8,9},{9,10},{10,1... | collective-permute-start | bytes 2457608 | tf_op jit(solution)/shard_map/ppermute | solution.py:16
  46.9 35.1 %collective-permute-start.3 = (bf16[256,1600]{0,1:T(8,128)(2,1)S(1)}, bf16[256,1600]{0,1:T(8,128)(2,1)S(1)}, u32[]{:S(2)}, u32[]{:S(2)}) collective-permute-start(bf16[256,1600]{0,1:T(8,128)(2,1)S(1)} %collective-permute-done.1), channel_id=1, source_target_pairs={{0,1},{1,2},{2,3},{3,4},{4,5},{5,6},{6,7},{7,8},{8,9},{9,10},{10,1... | collective-permute-start | bytes 2457608 | tf_op jit(solution)/shard_map/ppermute | solution.py:16
  64.5 35.1 %collective-permute-start.4 = (bf16[256,1600]{0,1:T(8,128)(2,1)S(1)}, bf16[256,1600]{0,1:T(8,128)(2,1)S(1)}, u32[]{:S(2)}, u32[]{:S(2)}) collective-permute-start(bf16[256,1600]{0,1:T(8,128)(2,1)S(1)} %collective-permute-done.2), channel_id=1, source_target_pairs={{0,1},{1,2},{2,3},{3,4},{4,5},{5,6},{6,7},{7,8},{8,9},{9,10},{10,1... | collective-permute-start | bytes 2457608 | tf_op jit(solution)/shard_map/ppermute | solution.py:16
  82.0 34.0 %collective-permute-start.5 = (bf16[256,1600]{0,1:T(8,128)(2,1)S(1)}, bf16[256,1600]{0,1:T(8,128)(2,1)S(1)}, u32[]{:S(2)}, u32[]{:S(2)}) collective-permute-start(bf16[256,1600]{0,1:T(8,128)(2,1)S(1)} %collective-permute-done.3), channel_id=1, source_target_pairs={{0,1},{1,2},{2,3},{3,4},{4,5},{5,6},{6,7},{7,8},{8,9},{9,10},{10,1... | collective-permute-start | bytes 2457608 | tf_op jit(solution)/shard_map/ppermute | solution.py:16
where the time goes:
time: 119 us
  waiting for transfers between devices  78.5 us (66%)
  matrix products  18.9 us (16%)
  starting transfers between devices  14.7 us (12%)
  other arithmetic  6.67 us (6%)
    ppermute x6, waiting for transfers between devices, from_behind(): return lax.ppermute(shard, axis, pairs)  78.5 us
    ppermute x6, starting transfers between devices, from_behind(): return lax.ppermute(shard, axis, pairs)  14.7 us
    dot_general x4, matrix products, block_partial(): jnp.einsum('hqk,khd->hqd', low_weight, vsplit, preferred_element_type=jnp...  10.5 us
    dot_general x4, matrix products, block_partial(): jnp.einsum('qhd,khd->hqk', qsplit, ksplit, preferred_element_type=jnp.flo...  8.43 us
    reduce_sum x2, other arithmetic, block_partial(): total = jnp.sum(expo, axis=-1)  6.6 us
  transfers between devices with their start and end apart: 6, of which 6 were waited for; matrix products, arithmetic and copies ran while one was open for 19% of the time, Pallas kernels for 0%

commit v1 on v0

v1 whole, which is shorter than its diff:
```python
import jax
import jax.numpy as jnp
from jax import lax
from jax.experimental import pallas as pl
from jax.experimental.pallas import tpu as pltpu
from jax.sharding import PartitionSpec as P

HEADS = 25
WIDTH = 64
SPLIT = 13
STAT = 16
SCALE = WIDTH ** -0.5 * 1.4426950408889634
NEG = -1e30
BIG = 1e30


def scores(key_cols, query_cols):
    return lax.dot_general(key_cols, query_cols, (((0,), (0,)), ((), ())), preferred_element_type=jnp.float32)


def attend_kernel(first, heads, flags, q_own, q_mate, k_own, v_own, r1, r3, y1, y3, part, part_lse, msg, s_own, s_mate, mate_lse):
    even, ok_x, ok_z, is0 = [flags[i] > 0 for i in range(4)]
    rows = q_own.shape[1]
    causal = lax.broadcasted_iota(jnp.int32, (rows, rows), 0) <= lax.broadcasted_iota(jnp.int32, (rows, rows), 1)

    def here(h):
        return pl.ds(pl.multiple_of(h * WIDTH, WIDTH), WIDTH)

    def there(h):
        return pl.ds(pl.multiple_of((first + h) * WIDTH, WIDTH), WIDTH)

    def own_scores(h):
        query = q_own[there(h)]
        s_own[:rows] = jnp.where(causal, scores(k_own[there(h)], query), NEG)
        s_own[rows:] = scores(jnp.where(is0, r3[here(h)], r1[here(h)]), query)

    def mate_scores(h):
        query = q_mate[there(h)]
        s_mate[:rows] = scores(jnp.where(even, k_own[there(h)], y1[here(h)]), query)
        s_mate[rows:] = scores(jnp.where(is0, r3[here(h)], r1[here(h)]), query)

    def softmax(s, ok):
        top_z = jnp.max(s[:rows], axis=0, keepdims=True) * SCALE
        if ok is not None:
            top_z = jnp.where(ok, top_z, NEG)
        top_x = jnp.where(ok_x, jnp.max(s[rows:], axis=0, keepdims=True) * SCALE, NEG)
        top = jnp.maximum(top_z, top_x)
        shift_z = top if ok is None else jnp.where(ok, top, BIG)
        expo_z = jnp.exp2(s[:rows] * SCALE - shift_z)
        expo_x = jnp.exp2(s[rows:] * SCALE - jnp.where(ok_x, top, BIG))
        total = jnp.sum(expo_z, axis=0, keepdims=True) + jnp.sum(expo_x, axis=0, keepdims=True)
        total = jnp.maximum(total, 1e-30)
        weight = jnp.concatenate([expo_z.astype(jnp.bfloat16), expo_x.astype(jnp.bfloat16)], axis=0)
        return weight, 1.0 / total, top + jnp.log2(total)

    own_scores(0)

    def one_head(h, carry):
        v_x = jnp.where(is0, y3[here(h)], r3[here(h)])
        mate_scores(h)
        weight, inverse, lse = softmax(s_own, None)
        value = jnp.concatenate([v_own[there(h)], v_x], axis=1)
        part[here(h)] = jnp.dot(value, weight, preferred_element_type=jnp.float32) * inverse
        part_lse[pl.ds(h, 1)] = lse
        own_scores(jnp.minimum(h + 1, heads - 1))
        weight, inverse, lse = softmax(s_mate, ok_z)
        value = jnp.concatenate([jnp.where(even, v_own[there(h)], y3[here(h)]), v_x], axis=1)
        msg[here(h)] = (jnp.dot(value, weight, preferred_element_type=jnp.float32) * inverse).astype(jnp.bfloat16)
        mate_lse[pl.ds(h, 1)] = lse
        return carry

    mate_lse[...] = jnp.zeros(mate_lse.shape, jnp.float32)
    part_lse[...] = jnp.zeros(part_lse.shape, jnp.float32)
    lax.fori_loop(0, heads, one_head, 0)
    stat = mate_lse[...]
    high = stat.astype(jnp.bfloat16).astype(jnp.float32)
    mid = (stat - high).astype(jnp.bfloat16).astype(jnp.float32)
    stat = jnp.concatenate([high, mid, stat - high - mid], axis=0)
    msg[pl.ds(heads * WIDTH, 3 * STAT)] = stat.astype(jnp.bfloat16)


VMEM = pl.BlockSpec(memory_space=pltpu.VMEM)


def attend(flags, q_own, q_mate, k_own, v_own, r1, r3, y1, y3, first):
    rows = q_own.shape[1]
    heads = r1.shape[0] // WIDTH
    return pl.pallas_call(
        lambda *refs: attend_kernel(first, heads, *refs),
        in_specs=[pl.BlockSpec(memory_space=pltpu.SMEM)] + [VMEM] * 8,
        out_specs=[VMEM] * 3,
        out_shape=[
            jax.ShapeDtypeStruct((heads * WIDTH, rows), jnp.float32),
            jax.ShapeDtypeStruct((STAT, rows), jnp.float32),
            jax.ShapeDtypeStruct((heads * WIDTH + 3 * STAT, rows), jnp.bfloat16),
        ],
        scratch_shapes=[
            pltpu.VMEM((2 * rows, rows), jnp.float32),
            pltpu.VMEM((2 * rows, rows), jnp.float32),
            pltpu.VMEM((STAT, rows), jnp.float32),
        ],
        compiler_params=pltpu.CompilerParams(vmem_limit_bytes=24 * 2**20),
        cost_estimate=pl.CostEstimate(
            flops=heads * 4 * 4 * rows * rows * WIDTH,
            bytes_accessed=heads * WIDTH * rows * 24,
            transcendentals=heads * 4 * rows * rows,
        ),
        name="attend",
    )(flags, q_own, q_mate, k_own, v_own, r1, r3, y1, y3)


def merge_kernel(heads, part, part_lse, msg, *rest):
    out = rest[-1]
    at = 0
    if len(rest) > 1:
        at = rest[0].shape[0]
        out[:at] = rest[0][...]
    stat = msg[pl.ds(heads * WIDTH, 3 * STAT)].astype(jnp.float32)
    gap = stat[:STAT] + stat[STAT : 2 * STAT] + stat[2 * STAT :] - part_lse[...]
    mine, theirs = 1.0 / (1.0 + jnp.exp2(gap)), 1.0 / (1.0 + jnp.exp2(-gap))
    for h in range(heads):
        src = pl.ds(h * WIDTH, WIDTH)
        both = part[src] * mine[h : h + 1] + msg[src].astype(jnp.float32) * theirs[h : h + 1]
        out[pl.ds(at + h * WIDTH, WIDTH)] = both.astype(jnp.bfloat16)


def merge(part, part_lse, msg, *before):
    size, rows = part.shape
    done = sum(b.shape[0] for b in before)
    return pl.pallas_call(
        lambda *refs: merge_kernel(size // WIDTH, *refs),
        in_specs=[VMEM] * (3 + len(before)),
        out_specs=VMEM,
        out_shape=jax.ShapeDtypeStruct((done + size, rows), jnp.bfloat16),
        compiler_params=pltpu.CompilerParams(vmem_limit_bytes=24 * 2**20),
        cost_estimate=pl.CostEstimate(flops=size * rows * 4, bytes_accessed=size * rows * 8, transcendentals=0),
        name="merge",
    )(part, part_lse, msg, *before)


def shards(queries, keys, values):
    length = lax.axis_size("seq")
    position = lax.axis_index("seq")
    column = position % 4
    even = column % 2 == 0
    q, k, v = queries.T, keys.T, values.T
    cut = SPLIT * WIDTH
    k1, k2, v1, v2 = k[:cut], k[cut:], v[:cut], v[cut:]
    swap = [(i, i ^ 1) for i in range(length)]
    to_x = [(i, i + (3, 1, 3, -3)[i % 4]) for i in range(length)]
    to_x = [(i, j) for i, j in to_x if j < length]
    to_y = [(i, i + 4) for i in range(length - 4) if i % 2]
    to_y0 = [(i, i + 4) for i in range(length - 4) if i % 4 != 2]

    def send_x(most, from3):
        return lax.ppermute(jnp.where(column == 3, from3, most), "seq", to_x)

    def send_y0(most, from0):
        return lax.ppermute(jnp.where(column == 0, from0, most), "seq", to_y0)

    r1, y1 = send_x(k1, v1), lax.ppermute(k1, "seq", to_y)
    q_mate = lax.ppermute(q, "seq", swap)
    r2, y2 = send_x(k2, v2), lax.ppermute(k2, "seq", to_y)
    r3, y3 = send_x(v1, y1), send_y0(v1, r1)
    r4, y4 = send_x(v2, y2), send_y0(v2, r2)
    ok_x = jnp.where(even, position >= 1, position >= 3)
    ok_z = jnp.where(even, position >= 0, position >= 4)
    flags = jnp.stack([even, ok_x, ok_z, column == 0]).astype(jnp.int32)
    part1, lse1, msg1 = attend(flags, q, q_mate, k, v, r1, r3, y1, y3, 0)
    flags, msg1 = lax.optimization_barrier((flags, msg1))
    msg1 = lax.ppermute(msg1, "seq", swap)
    part2, lse2, msg2 = attend(flags, q, q_mate, k, v, r2, r4, y2, y4, SPLIT)
    msg2 = lax.ppermute(msg2, "seq", swap)
    return merge(part2, lse2, msg2, merge(part1, lse1, msg1)).T


def solution(mesh):
    return jax.shard_map(
        shards,
        mesh=mesh,
        in_specs=(P(("hist", "seq"), None), P(("hist", "seq"), None), P(("hist", "seq"), None)),
        out_specs=P(("hist", "seq"), None),
        check_vma=False,
    )
```

time: 119 us -> 77.1 us (0.65)
  the two profiles are of different devices: /device:TPU:288 before, /device:TPU:250 now
where the time goes in v1:
time: 77.1 us; the launch traced here: 76.7 us
  starting transfers between devices  39.9 us (52%)
  Pallas kernels  19.2 us (25%)
  waiting for transfers between devices  12.2 us (16%)
  other arithmetic  5.17 us (7%)
    pallas_call x2, Pallas kernels, attend(): pl.pallas_call(lambda *refs: attend_kernel(first, heads, *refs), in_specs...  17.9 us
    ppermute x2, starting transfers between devices, send_y0(): return lax.ppermute(jnp.where(column == 0, from0, most), 'seq', to_y0)  11.3 us
    ppermute x4, starting transfers between devices, send_x(): return lax.ppermute(jnp.where(column == 3, from3, most), 'seq', to_x)  10.1 us
    ppermute x1, waiting for transfers between devices, shards(): msg2 = lax.ppermute(msg2, 'seq', swap)  9.03 us
    ppermute x1, starting transfers between devices, shards(): r1, y1 = (send_x(k1, v1), lax.ppermute(k1, 'seq', to_y))  7.85 us
    ppermute x1, starting transfers between devices, shards(): msg1 = lax.ppermute(msg1, 'seq', swap)  3.9 us
    slice x2, other arithmetic, shards(): k1, k2, v1, v2 = (k[:cut], k[cut:], v[:cut], v[cut:])  3.18 us
    ppermute x1, waiting for transfers between devices, shards(): r1, y1 = (send_x(k1, v1), lax.ppermute(k1, 'seq', to_y))  2.77 us
  transfers between devices with their start and end apart: 11, of which 3 were waited for; matrix products, arithmetic and copies ran while one was open for 4% of the time, Pallas kernels for 24%

profile of v1, /device:TPU:250, one launch (start us, length us, event | category | flops | bytes accessed | tf_op | source)
XLA Modules:
  0.0 76.7 jit_solution(11160087789933655697)
XLA Ops:
  0.0 2.2 %fusion.1 = (bf16[832,256]{1,0:T(8,128)(2,1)}, bf16[832,256]{1,0:T(8,128)(2,1)}) fusion(bf16[1600,256]{1,0:T(8,128)(2,1)} %bitcast.14, bf16[1600,256]{1,0:T(8,128)(2,1)} %bitcast.8, pred[]{:T(512)S(6)} %eq.19), kind=kLoop, calls=%fused_computation.8 | loop fusion | flops 212992 | bytes 1703937 | tf_op jit(solution)/shard_map/slice | solution.py:148
  2.2 3.4 %collective-permute-start.1 = (bf16[832,256]{1,0:T(8,128)(2,1)}, bf16[832,256]{1,0:T(8,128)(2,1)S(1)}, u32[]{:S(2)}, u32[]{:S(2)}) collective-permute-start(bf16[832,256]{1,0:T(8,128)(2,1)} %get-tuple-element.28), channel_id=1, source_target_pairs={{0,3},{1,2},{2,5},{3,0},{4,7},{5,6},{6,9},{7,4},{8,11},{9,10},{10,... | collective-permute-start | bytes 1277960 | tf_op jit(solution)/shard_map/ppermute | solution.py:156
  5.6 7.8 %collective-permute-start.2 = (bf16[832,256]{1,0:T(8,128)(2,1)}, bf16[832,256]{1,0:T(8,128)(2,1)S(1)}, u32[]{:S(2)}, u32[]{:S(2)}) collective-permute-start(bf16[832,256]{1,0:T(8,128)(2,1)} %get-tuple-element.27), channel_id=1, source_target_pairs={{1,5},{3,7},{5,9},{7,11},{9,13},{11,15},{13,17},{15,19},{17,21},{1... | collective-permute-start | bytes 1277960 | tf_op jit(solution)/shard_map/ppermute | solution.py:161
  13.5 0.0 copy-done
  13.5 0.9 %fusion = (bf16[768,256]{1,0:T(8,128)(2,1)}, bf16[768,256]{1,0:T(8,128)(2,1)}) fusion(bf16[1600,256]{1,0:T(8,128)(2,1)S(1)} %bitcast.15, bf16[1600,256]{1,0:T(8,128)(2,1)S(1)} %bitcast.9, pred[]{:T(512)S(6)} %eq.19), kind=kLoop, calls=%fused_computation.7 | loop fusion | flops 196608 | bytes 1572865 | tf_op jit(solution)/shard_map/slice | solution.py:148
  14.4 1.9 %collective-permute-start.5 = (bf16[768,256]{1,0:T(8,128)(2,1)}, bf16[768,256]{1,0:T(8,128)(2,1)S(1)}, u32[]{:S(2)}, u32[]{:S(2)}) collective-permute-start(bf16[768,256]{1,0:T(8,128)(2,1)} %get-tuple-element.24), channel_id=1, source_target_pairs={{0,3},{1,2},{2,5},{3,0},{4,7},{5,6},{6,9},{7,4},{8,11},{9,10},{10,... | collective-permute-start | bytes 1179656 | tf_op jit(solution)/shard_map/ppermute | solution.py:156
  16.4 2.6 %collective-permute-start.6 = (bf16[768,256]{1,0:T(8,128)(2,1)}, bf16[768,256]{1,0:T(8,128)(2,1)S(1)}, u32[]{:S(2)}, u32[]{:S(2)}) collective-permute-start(bf16[768,256]{1,0:T(8,128)(2,1)} %get-tuple-element.23), channel_id=1, source_target_pairs={{1,5},{3,7},{5,9},{7,11},{9,13},{11,15},{13,17},{15,19},{17,21},{1... | collective-permute-start | bytes 1179656 | tf_op jit(solution)/shard_map/ppermute | solution.py:163
  19.0 2.3 %collective-permute-start = (bf16[1600,256]{1,0:T(8,128)(2,1)}, bf16[1600,256]{1,0:T(8,128)(2,1)}, u32[]{:S(2)}, u32[]{:S(2)}) collective-permute-start(bf16[1600,256]{1,0:T(8,128)(2,1)} %bitcast.4.refs_1_), channel_id=1, source_target_pairs={{0,1},{1,0},{2,3},{3,2},{4,5},{5,4},{6,7},{7,6},{8,9},{9,8},{10,11... | collective-permute-start | bytes 2457608 | tf_op jit(solution)/shard_map/ppermute | solution.py:162
  21.3 0.0 collective-permute-done.1.refs_5_
  21.3 2.8 %collective-permute-done.2.refs_7_ = bf16[832,256]{1,0:T(8,128)(2,1)S(1)} collective-permute-done((bf16[832,256]{1,0:T(8,128)(2,1)}, bf16[832,256]{1,0:T(8,128)(2,1)S(1)}, u32[]{:S(2)}, u32[]{:S(2)}) %collective-permute-start.2) | collective-permute-done | bytes 426016 | tf_op jit(solution)/shard_map/ppermute | solution.py:161
  24.0 1.0 %broadcast_select_fusion = (bf16[832,256]{1,0:T(8,128)(2,1)}, bf16[832,256]{1,0:T(8,128)(2,1)}) fusion(bf16[832,256]{1,0:T(8,128)(2,1)S(1)} %collective-permute-done.1.refs_5_, pred[]{:T(512)} %eq.18, bf16[1600,256]{1,0:T(8,128)(2,1)S(1)} %bitcast.10, bf16[832,256]{1,0:T(8,128)(2,1)S(1)} %collective-permute-done.2.refs_7_, pred[]{:T(512)S(6)} %eq.19), kind=kLoop, calls=%fused_computation | loop fusion | flops 425984 | bytes 2129922 | tf_op jit(solution)/shard_map/jit(_where)/select_n | solution.py:159
  25.0 1.9 %collective-permute-start.3 = (bf16[832,256]{1,0:T(8,128)(2,1)}, bf16[832,256]{1,0:T(8,128)(2,1)}, u32[]{:S(2)}, u32[]{:S(2)}) collective-permute-start(bf16[832,256]{1,0:T(8,128)(2,1)} %get-tuple-element.26), channel_id=1, source_target_pairs={{0,3},{1,2},{2,5},{3,0},{4,7},{5,6},{6,9},{7,4},{8,11},{9,10},{10,... | collective-permute-start | bytes 1277960 | tf_op jit(solution)/shard_map/ppermute | solution.py:156
  26.9 8.2 %collective-permute-start.4 = (bf16[832,256]{1,0:T(8,128)(2,1)}, bf16[832,256]{1,0:T(8,128)(2,1)}, u32[]{:S(2)}, u32[]{:S(2)}) collective-permute-start(bf16[832,256]{1,0:T(8,128)(2,1)} %get-tuple-element.25), channel_id=1, source_target_pairs={{0,4},{1,5},{3,7},{4,8},{5,9},{7,11},{8,12},{9,13},{11,15},{12,16}... | collective-permute-start | bytes 1277960 | tf_op jit(solution)/shard_map/ppermute | solution.py:159
  35.1 0.0 collective-permute-done.5.refs_5_
  35.1 0.0 collective-permute-done.6.refs_7_
  35.2 0.9 %broadcast_select_fusion.3 = (bf16[768,256]{1,0:T(8,128)(2,1)}, bf16[768,256]{1,0:T(8,128)(2,1)}) fusion(bf16[768,256]{1,0:T(8,128)(2,1)S(1)} %collective-permute-done.5.refs_5_, pred[]{:T(512)} %eq.18, bf16[1600,256]{1,0:T(8,128)(2,1)S(1)} %bitcast.11, bf16[768,256]{1,0:T(8,128)(2,1)S(1)} %collective-permute-done.6.refs_7_, pred[]{:T(512)S(6)} %eq.19), kind=kLoop, calls=%fused_computation.3 | loop fusion | flops 393216 | bytes 1966082 | tf_op jit(solution)/shard_map/jit(_where)/select_n | solution.py:159
  36.1 2.9 %collective-permute-start.7 = (bf16[768,256]{1,0:T(8,128)(2,1)}, bf16[768,256]{1,0:T(8,128)(2,1)}, u32[]{:S(2)}, u32[]{:S(2)}) collective-permute-start(bf16[768,256]{1,0:T(8,128)(2,1)} %get-tuple-element.22), channel_id=1, source_target_pairs={{0,3},{1,2},{2,5},{3,0},{4,7},{5,6},{6,9},{7,4},{8,11},{9,10},{10,... | collective-permute-start | bytes 1179656 | tf_op jit(solution)/shard_map/ppermute | solution.py:156
  39.0 3.1 %collective-permute-start.8 = (bf16[768,256]{1,0:T(8,128)(2,1)}, bf16[768,256]{1,0:T(8,128)(2,1)}, u32[]{:S(2)}, u32[]{:S(2)}) collective-permute-start(bf16[768,256]{1,0:T(8,128)(2,1)} %get-tuple-element.21), channel_id=1, source_target_pairs={{0,4},{1,5},{3,7},{4,8},{5,9},{7,11},{8,12},{9,13},{11,15},{12,16}... | collective-permute-start | bytes 1179656 | tf_op jit(solution)/shard_map/ppermute | solution.py:159
  42.1 0.1 add_convert_fusion.refs_0_
  42.2 0.0 collective-permute-done.refs_2_
  42.2 0.0 collective-permute-done.3.refs_6_
  42.2 0.4 collective-permute-done.4.refs_8_
  42.5 9.3 %attend.2 = (f32[832,256]{1,0:T(8,128)S(1)}, f32[16,256]{1,0:T(8,128)S(1)}, bf16[880,256]{1,0:T(8,128)(2,1)S(1)}) custom-call(s32[4]{0:T(128)S(1)} %add_convert_fusion.refs_0_, bf16[1600,256]{1,0:T(8,128)(2,1)} %bitcast.4.refs_1_, bf16[1600,256]{1,0:T(8,128)(2,1)} %collective-permute-done.refs_2_, bf16[1600,256]{1,0:T(8,128)(2,1)S(1)} %bitcast.16, ...), custom_call_target="tpu_custom_call" | custom-call | flops 872415232 | bytes 5111808 | tf_op jit(solution)/shard_map/attend/pallas_call | solution.py:88
  51.8 3.9 %collective-permute-start.10 = (bf16[880,256]{1,0:T(8,128)(2,1)S(1)}, bf16[880,256]{1,0:T(8,128)(2,1)S(1)}, u32[]{:S(2)}, u32[]{:S(2)}) collective-permute-start(bf16[880,256]{1,0:T(8,128)(2,1)S(1)} %get-tuple-element.20), channel_id=1, source_target_pairs={{0,1},{1,0},{2,3},{3,2},{4,5},{5,4},{6,7},{7,6},{8,9},{9,8},{10,11... | collective-permute-start | bytes 1351688 | tf_op jit(solution)/shard_map/ppermute | solution.py:171
  55.7 0.0 collective-permute-done.7.refs_6_
  55.7 0.0 collective-permute-done.8.refs_8_
  55.7 8.6 %attend.3 = (f32[768,256]{1,0:T(8,128)S(1)}, f32[16,256]{1,0:T(8,128)S(1)}, bf16[816,256]{1,0:T(8,128)(2,1)S(1)}) custom-call(s32[4]{0:T(128)S(1)} %add_convert_fusion.refs_0_, bf16[1600,256]{1,0:T(8,128)(2,1)} %bitcast.4.refs_1_, bf16[1600,256]{1,0:T(8,128)(2,1)} %collective-permute-done.refs_2_, bf16[1600,256]{1,0:T(8,128)(2,1)S(1)} %bitcast.17, ...), custom_call_target="tpu_custom_call" | custom-call | flops 805306368 | bytes 4718592 | tf_op jit(solution)/shard_map/attend/pallas_call | solution.py:88
  64.4 2.0 %collective-permute-start.9 = (bf16[816,256]{1,0:T(8,128)(2,1)S(1)}, bf16[816,256]{1,0:T(8,128)(2,1)S(1)}, u32[]{:S(2)}, u32[]{:S(2)}) collective-permute-start(bf16[816,256]{1,0:T(8,128)(2,1)S(1)} %get-tuple-element.17), channel_id=1, source_target_pairs={{0,1},{1,0},{2,3},{3,2},{4,5},{5,4},{6,7},{7,6},{8,9},{9,8},{10,11... | collective-permute-start | bytes 1253384 | tf_op jit(solution)/shard_map/ppermute | solution.py:173
  66.4 0.0 collective-permute-done.10.refs_2_
  66.4 0.2 merge.2.refs_3_
  66.6 9.0 %collective-permute-done.9.refs_2_ = bf16[816,256]{1,0:T(8,128)(2,1)S(1)} collective-permute-done((bf16[816,256]{1,0:T(8,128)(2,1)S(1)}, bf16[816,256]{1,0:T(8,128)(2,1)S(1)}, u32[]{:S(2)}, u32[]{:S(2)}) %collective-permute-start.9) | collective-permute-done | bytes 417824 | tf_op jit(solution)/shard_map/ppermute | solution.py:173
  75.6 1.1 %merge.3 = bf16[1600,256]{1,0:T(8,128)(2,1)} custom-call(f32[768,256]{1,0:T(8,128)S(1)} %get-tuple-element.15.refs_0_, f32[16,256]{1,0:T(8,128)S(1)} %get-tuple-element.16.refs_1_, bf16[816,256]{1,0:T(8,128)(2,1)S(1)} %collective-permute-done.9.refs_2_, bf16[832,256]{1,0:T(8,128)(2,1)S(1)} %merge.2.refs_3_), custom_call_target="tpu_custom_call" | custom-call | flops 786432 | bytes 1572864 | tf_op jit(solution)/shard_map/merge/pallas_call | solution.py:130
  (3 shorter events, 0.0 us)
Async XLA Ops:
  0.0 13.5 %copy-start = (bf16[256,1600]{0,1:T(8,128)(2,1)S(1)}, bf16[256,1600]{0,1:T(8,128)(2,1)}, u32[]{:S(2)}) copy-start(bf16[256,1600]{0,1:T(8,128)(2,1)} %param.5) | copy-start | bytes 2457604
  0.0 13.5 %copy-start.1 = (bf16[256,1600]{0,1:T(8,128)(2,1)S(1)}, bf16[256,1600]{0,1:T(8,128)(2,1)}, u32[]{:S(2)}) copy-start(bf16[256,1600]{0,1:T(8,128)(2,1)} %param.4) | copy-start | bytes 2457604
  2.2 19.0 %collective-permute-start.1 = (bf16[832,256]{1,0:T(8,128)(2,1)}, bf16[832,256]{1,0:T(8,128)(2,1)S(1)}, u32[]{:S(2)}, u32[]{:S(2)}) collective-permute-start(bf16[832,256]{1,0:T(8,128)(2,1)} %get-tuple-element.28), channel_id=1, source_target_pairs={{0,3},{1,2},{2,5},{3,0},{4,7},{5,6},{6,9},{7,4},{8,11},{9,10},{10,... | collective-permute-start | bytes 1277960 | tf_op jit(solution)/shard_map/ppermute | solution.py:156
  5.6 18.4 %collective-permute-start.2 = (bf16[832,256]{1,0:T(8,128)(2,1)}, bf16[832,256]{1,0:T(8,128)(2,1)S(1)}, u32[]{:S(2)}, u32[]{:S(2)}) collective-permute-start(bf16[832,256]{1,0:T(8,128)(2,1)} %get-tuple-element.27), channel_id=1, source_target_pairs={{1,5},{3,7},{5,9},{7,11},{9,13},{11,15},{13,17},{15,19},{17,21},{1... | collective-permute-start | bytes 1277960 | tf_op jit(solution)/shard_map/ppermute | solution.py:161
  14.4 20.7 %collective-permute-start.5 = (bf16[768,256]{1,0:T(8,128)(2,1)}, bf16[768,256]{1,0:T(8,128)(2,1)S(1)}, u32[]{:S(2)}, u32[]{:S(2)}) collective-permute-start(bf16[768,256]{1,0:T(8,128)(2,1)} %get-tuple-element.24), channel_id=1, source_target_pairs={{0,3},{1,2},{2,5},{3,0},{4,7},{5,6},{6,9},{7,4},{8,11},{9,10},{10,... | collective-permute-start | bytes 1179656 | tf_op jit(solution)/shard_map/ppermute | solution.py:156
  16.4 18.8 %collective-permute-start.6 = (bf16[768,256]{1,0:T(8,128)(2,1)}, bf16[768,256]{1,0:T(8,128)(2,1)S(1)}, u32[]{:S(2)}, u32[]{:S(2)}) collective-permute-start(bf16[768,256]{1,0:T(8,128)(2,1)} %get-tuple-element.23), channel_id=1, source_target_pairs={{1,5},{3,7},{5,9},{7,11},{9,13},{11,15},{13,17},{15,19},{17,21},{1... | collective-permute-start | bytes 1179656 | tf_op jit(solution)/shard_map/ppermute | solution.py:163
  19.0 23.2 %collective-permute-start = (bf16[1600,256]{1,0:T(8,128)(2,1)}, bf16[1600,256]{1,0:T(8,128)(2,1)}, u32[]{:S(2)}, u32[]{:S(2)}) collective-permute-start(bf16[1600,256]{1,0:T(8,128)(2,1)} %bitcast.4.refs_1_), channel_id=1, source_target_pairs={{0,1},{1,0},{2,3},{3,2},{4,5},{5,4},{6,7},{7,6},{8,9},{9,8},{10,11... | collective-permute-start | bytes 2457608 | tf_op jit(solution)/shard_map/ppermute | solution.py:162
  25.0 17.2 %collective-permute-start.3 = (bf16[832,256]{1,0:T(8,128)(2,1)}, bf16[832,256]{1,0:T(8,128)(2,1)}, u32[]{:S(2)}, u32[]{:S(2)}) collective-permute-start(bf16[832,256]{1,0:T(8,128)(2,1)} %get-tuple-element.26), channel_id=1, source_target_pairs={{0,3},{1,2},{2,5},{3,0},{4,7},{5,6},{6,9},{7,4},{8,11},{9,10},{10,... | collective-permute-start | bytes 1277960 | tf_op jit(solution)/shard_map/ppermute | solution.py:156
  26.9 15.6 %collective-permute-start.4 = (bf16[832,256]{1,0:T(8,128)(2,1)}, bf16[832,256]{1,0:T(8,128)(2,1)}, u32[]{:S(2)}, u32[]{:S(2)}) collective-permute-start(bf16[832,256]{1,0:T(8,128)(2,1)} %get-tuple-element.25), channel_id=1, source_target_pairs={{0,4},{1,5},{3,7},{4,8},{5,9},{7,11},{8,12},{9,13},{11,15},{12,16}... | collective-permute-start | bytes 1277960 | tf_op jit(solution)/shard_map/ppermute | solution.py:159
  36.1 19.6 %collective-permute-start.7 = (bf16[768,256]{1,0:T(8,128)(2,1)}, bf16[768,256]{1,0:T(8,128)(2,1)}, u32[]{:S(2)}, u32[]{:S(2)}) collective-permute-start(bf16[768,256]{1,0:T(8,128)(2,1)} %get-tuple-element.22), channel_id=1, source_target_pairs={{0,3},{1,2},{2,5},{3,0},{4,7},{5,6},{6,9},{7,4},{8,11},{9,10},{10,... | collective-permute-start | bytes 1179656 | tf_op jit(solution)/shard_map/ppermute | solution.py:156
  39.0 16.8 %collective-permute-start.8 = (bf16[768,256]{1,0:T(8,128)(2,1)}, bf16[768,256]{1,0:T(8,128)(2,1)}, u32[]{:S(2)}, u32[]{:S(2)}) collective-permute-start(bf16[768,256]{1,0:T(8,128)(2,1)} %get-tuple-element.21), channel_id=1, source_target_pairs={{0,4},{1,5},{3,7},{4,8},{5,9},{7,11},{8,12},{9,13},{11,15},{12,16}... | collective-permute-start | bytes 1179656 | tf_op jit(solution)/shard_map/ppermute | solution.py:159
  51.8 14.5 %collective-permute-start.10 = (bf16[880,256]{1,0:T(8,128)(2,1)S(1)}, bf16[880,256]{1,0:T(8,128)(2,1)S(1)}, u32[]{:S(2)}, u32[]{:S(2)}) collective-permute-start(bf16[880,256]{1,0:T(8,128)(2,1)S(1)} %get-tuple-element.20), channel_id=1, source_target_pairs={{0,1},{1,0},{2,3},{3,2},{4,5},{5,4},{6,7},{7,6},{8,9},{9,8},{10,11... | collective-permute-start | bytes 1351688 | tf_op jit(solution)/shard_map/ppermute | solution.py:171
  64.4 11.2 %collective-permute-start.9 = (bf16[816,256]{1,0:T(8,128)(2,1)S(1)}, bf16[816,256]{1,0:T(8,128)(2,1)S(1)}, u32[]{:S(2)}, u32[]{:S(2)}) collective-permute-start(bf16[816,256]{1,0:T(8,128)(2,1)S(1)} %get-tuple-element.17), channel_id=1, source_target_pairs={{0,1},{1,0},{2,3},{3,2},{4,5},{5,4},{6,7},{7,6},{8,9},{9,8},{10,11... | collective-permute-start | bytes 1253384 | tf_op jit(solution)/shard_map/ppermute | solution.py:173

commit v2 on v1

v2 whole, which is shorter than its diff:
```python
import jax
import jax.numpy as jnp
from jax import lax
from jax.experimental import pallas as pl
from jax.experimental.pallas import tpu as pltpu
from jax.sharding import PartitionSpec as P

HEADS = 25
WIDTH = 64
GROUP = 5
CHUNKS = (3, 2)
STEP = GROUP * WIDTH
ONES = 16
STAT = 16
MSG = STEP + STAT
SCALE = WIDTH ** -0.5 * 1.4426950408889634
NEG = -1e30


def scores(key_cols, query_cols):
    return lax.dot_general(key_cols, query_cols, (((0,), (0,)), ((), ())), preferred_element_type=jnp.float32)


def fold_max(tile):
    return jnp.max(tile.reshape(tile.shape[0] // 8, 8, tile.shape[1]), axis=0)


def top_of(folded):
    return jnp.max(folded, axis=0, keepdims=True) * SCALE


def with_ones(value):
    return jnp.concatenate([value, jnp.ones((ONES, value.shape[1]), value.dtype)], axis=0)


def weights(score, top):
    return jnp.exp2(score * SCALE - top).astype(jnp.bfloat16)


def pipelined(units):
    results, depth = [[] for _ in units], len(units[0])
    for i in range(len(units) + depth - 1):
        for stage in range(depth):
            if 0 <= i - stage < len(units):
                done = results[i - stage]
                done.append(units[i - stage][stage](*done))
    return results


def stack_rows(rows, size):
    fill = [jnp.zeros_like(rows[0])] * (size - len(rows))
    return jnp.concatenate(list(rows) + fill, axis=0)


def diag_kernel(q_any, k_any, v_any, query, key, value, acc, stats, sems):
    rows = query.shape[1]
    half = rows // 2
    later = lax.broadcasted_iota(jnp.int32, (half, half), 0) > lax.broadcasted_iota(jnp.int32, (half, half), 1)

    def copies(i):
        at = pl.ds(pl.multiple_of(i * STEP, STEP), STEP)
        pairs = (q_any, query), (k_any, key), (v_any, value)
        return [pltpu.make_async_copy(src.at[at], dst.at[at], sems.at[i, j]) for j, (src, dst) in enumerate(pairs)]

    for i in range(HEADS // GROUP):
        for copy in copies(i):
            copy.start()

    def one_group(i, carry):
        for copy in copies(i):
            copy.wait()
        diag_group(i, query, key, value, acc, stats, later)
        return carry

    lax.fori_loop(0, HEADS // GROUP, one_group, 0)


def diag_group(i, query, key, value, acc, stats, later):
    half = later.shape[0]

    def there(g):
        return pl.ds(pl.multiple_of(i * STEP + g * WIDTH, WIDTH), WIDTH)

    def unit(g):
        at = there(g)

        def score():
            q, k = query[at], key[at]
            return scores(k[:, :half], q), scores(k[:, half:], q[:, half:])

        def top(score):
            first, last = score
            corner, last = jnp.where(later, NEG, first[:, :half]), jnp.where(later, NEG, last)
            right = first[:, half:]
            top_a, top_b = top_of(fold_max(corner)), top_of(jnp.maximum(fold_max(right), fold_max(last)))
            return corner, right, last, top_a, top_b

        def weight(score, top):
            corner, right, last, top_a, top_b = top
            upper = jnp.concatenate([weights(corner, top_a), weights(right, top_b)], axis=1)
            lower = jnp.concatenate([jnp.zeros((half, half), jnp.bfloat16), weights(last, top_b)], axis=1)
            return jnp.concatenate([upper, lower], axis=0)

        def product(score, top, weight):
            return jnp.dot(with_ones(value[at]), weight, preferred_element_type=jnp.float32)

        return score, top, weight, product

    done = pipelined([unit(g) for g in range(GROUP)])
    for g in range(GROUP):
        acc[there(g)] = done[g][3][:WIDTH]
    totals = [d[3][WIDTH : WIDTH + 1] for d in done]
    tops = [jnp.concatenate(d[1][3:], axis=1) for d in done]
    stats[i] = jnp.concatenate([stack_rows(tops, 8), stack_rows(totals, 8)], axis=0)


def mix(a, b):
    (acc_a, total_a, top_a), (acc_b, total_b, top_b) = a, b
    top = jnp.maximum(top_a, top_b)
    factor_a, factor_b = jnp.exp2(top_a - top), jnp.exp2(top_b - top)
    total = total_a * factor_a + total_b * factor_b
    return acc_a * (factor_a / total) + acc_b * (factor_b / total), top + jnp.log2(total)


def attend_kernel(first, flags, q_own, k_own, v_own, acc_d, stats_d, q_mate, r1, r3, y1, y3, part, part_lse, msg):
    even, ok_x, ok_z, is0 = [flags[i] > 0 for i in range(4)]
    rows = q_own.shape[1]

    def one_group(i, carry):
        def here(g):
            return pl.ds(pl.multiple_of(i * STEP + g * WIDTH, WIDTH), WIDTH)

        def there(g):
            return pl.ds(pl.multiple_of((first + i) * STEP + g * WIDTH, WIDTH), WIDTH)

        def unit(score, value, ok):
            def top(s):
                return top_of(fold_max(s))

            def weight(s, top):
                return weights(s, top)

            def product(s, top, weight):
                acc = jnp.dot(with_ones(value()), weight, preferred_element_type=jnp.float32)
                return acc[:WIDTH], acc[WIDTH : WIDTH + 1], jnp.where(ok, top, NEG)

            return score, top, weight, product

        def unit_x(g):
            def score():
                key = jnp.where(is0, r3[here(g)], r1[here(g)])
                return scores(key, jnp.concatenate([q_own[there(g)], q_mate[there(g)]], axis=1))

            return unit(score, lambda: jnp.where(is0, y3[here(g)], r3[here(g)]), ok_x)

        def unit_z(g):
            def score():
                return scores(jnp.where(even, k_own[there(g)], y1[here(g)]), q_mate[there(g)])

            return unit(score, lambda: jnp.where(even, v_own[there(g)], y3[here(g)]), ok_z)

        done = pipelined([u(g) for g in range(GROUP) for u in (unit_x, unit_z)])
        stats = stats_d[first + i]
        own, mate = [], []
        for g in range(GROUP):
            x, z = done[2 * g][3], done[2 * g + 1][3]
            d = acc_d[there(g)], stats[8 + g : 9 + g], stats[g : g + 1]
            own.append(mix(d, [e[:, :rows] for e in x]))
            mate.append(mix(z, [e[:, rows:] for e in x]))
        for g in range(GROUP):
            part[here(g)] = own[g][0]
            msg[pl.ds(pl.multiple_of(i * MSG + g * WIDTH, 16), WIDTH)] = mate[g][0].astype(jnp.bfloat16)
        part_lse[i] = stack_rows([lse for _, lse in own], 8)
        stat = jnp.concatenate([lse for _, lse in mate], axis=0)
        high = stat.astype(jnp.bfloat16).astype(jnp.float32)
        mid = (stat - high).astype(jnp.bfloat16).astype(jnp.float32)
        stat = stack_rows([high, mid, stat - high - mid, jnp.zeros((1, rows), jnp.float32)], 4)
        msg[pl.ds(pl.multiple_of(i * MSG + STEP, 16), STAT)] = stat.astype(jnp.bfloat16)
        return carry

    lax.fori_loop(0, part_lse.shape[0], one_group, 0)


VMEM = pl.BlockSpec(memory_space=pltpu.VMEM)
ANY = pl.BlockSpec(memory_space=pl.ANY)


def diag(q, k, v):
    size, rows = q.shape
    groups = HEADS // GROUP
    return pl.pallas_call(
        diag_kernel,
        in_specs=[ANY] * 3,
        out_specs=[VMEM] * 5,
        out_shape=[
            *[jax.ShapeDtypeStruct((size, rows), jnp.bfloat16)] * 3,
            jax.ShapeDtypeStruct((size, rows), jnp.float32),
            jax.ShapeDtypeStruct((groups, 16, rows), jnp.float32),
        ],
        scratch_shapes=[pltpu.SemaphoreType.DMA((groups, 3))],
        compiler_params=pltpu.CompilerParams(vmem_limit_bytes=24 * 2**20),
        cost_estimate=pl.CostEstimate(
            flops=HEADS * 4 * rows * rows * WIDTH, bytes_accessed=size * rows * 10, transcendentals=HEADS * rows * rows
        ),
        name="diag",
    )(q, k, v)


def attend(flags, diagonal, q_mate, r1, r3, y1, y3, first):
    size, rows = r1.shape
    heads, groups = size // WIDTH, size // STEP
    return pl.pallas_call(
        lambda *refs: attend_kernel(first, *refs),
        in_specs=[pl.BlockSpec(memory_space=pltpu.SMEM)] + [VMEM] * 10,
        out_specs=[VMEM] * 3,
        out_shape=[
            jax.ShapeDtypeStruct((size, rows), jnp.float32),
            jax.ShapeDtypeStruct((groups, 8, rows), jnp.float32),
            jax.ShapeDtypeStruct((groups * MSG, rows), jnp.bfloat16),
        ],
        compiler_params=pltpu.CompilerParams(vmem_limit_bytes=24 * 2**20),
        cost_estimate=pl.CostEstimate(
            flops=heads * 3 * 4 * rows * rows * WIDTH,
            bytes_accessed=heads * WIDTH * rows * 24,
            transcendentals=heads * 3 * rows * rows,
        ),
        name="attend",
    )(flags, *diagonal, q_mate, r1, r3, y1, y3)


def merge_kernel(part, part_lse, msg, *rest):
    out = rest[-1]
    at = 0
    if len(rest) > 1:
        at = rest[0].shape[0]
        out[:at] = rest[0][...]
    for i in range(part_lse.shape[0]):
        stat = msg[pl.ds(i * MSG + STEP, STAT)].astype(jnp.float32)
        lse = stat[:GROUP] + stat[GROUP : 2 * GROUP] + stat[2 * GROUP : 3 * GROUP]
        gap = lse - part_lse[i, :GROUP]
        mine, theirs = 1.0 / (1.0 + jnp.exp2(gap)), 1.0 / (1.0 + jnp.exp2(-gap))
        for g in range(GROUP):
            row, src = i * STEP + g * WIDTH, pl.ds(i * MSG + g * WIDTH, WIDTH)
            both = part[pl.ds(row, WIDTH)] * mine[g : g + 1] + msg[src].astype(jnp.float32) * theirs[g : g + 1]
            out[pl.ds(at + row, WIDTH)] = both.astype(jnp.bfloat16)


def merge(part, part_lse, msg, *before):
    size, rows = part.shape
    done = sum(b.shape[0] for b in before)
    return pl.pallas_call(
        merge_kernel,
        in_specs=[VMEM] * (3 + len(before)),
        out_specs=VMEM,
        out_shape=jax.ShapeDtypeStruct((done + size, rows), jnp.bfloat16),
        compiler_params=pltpu.CompilerParams(vmem_limit_bytes=24 * 2**20),
        cost_estimate=pl.CostEstimate(flops=size * rows * 4, bytes_accessed=size * rows * 8, transcendentals=0),
        name="merge",
    )(part, part_lse, msg, *before)


def shards(queries, keys, values):
    length = lax.axis_size("seq")
    position = lax.axis_index("seq")
    column = position % 4
    even = column % 2 == 0
    q, k, v = queries.T, keys.T, values.T
    swap = [(i, i ^ 1) for i in range(length)]
    to_x = [(i, i + (3, 1, 3, -3)[i % 4]) for i in range(length)]
    to_x = [(i, j) for i, j in to_x if j < length]
    to_y = [(i, i + 4) for i in range(length - 4) if i % 2]
    to_y0 = [(i, i + 4) for i in range(length - 4) if i % 4 != 2]

    cut = CHUNKS[0] * STEP
    y_1, y_2 = k[:cut], k[cut:]
    x_1, x_2 = jnp.where(column == 3, v[:cut], y_1), jnp.where(column == 3, v[cut:], y_2)
    r1, y1 = lax.ppermute(x_1, "seq", to_x), lax.ppermute(y_1, "seq", to_y)
    r2, y2 = lax.ppermute(x_2, "seq", to_x), lax.ppermute(y_2, "seq", to_y)
    q_mate = lax.ppermute(q, "seq", swap)
    r1, y1, *diagonal = lax.optimization_barrier((r1, y1, *diag(q, k, v)))
    value = diagonal[2]

    def send_on(r, y, at):
        return jnp.where(column == 3, y, value[at]), jnp.where(column == 0, r, value[at])

    to_send = send_on(r1, y1, slice(0, cut))
    r3, y3 = lax.ppermute(to_send[0], "seq", to_x), lax.ppermute(to_send[1], "seq", to_y0)
    r2, y2 = lax.optimization_barrier((r2, y2, *to_send))[:2]
    to_send = send_on(r2, y2, slice(cut, None))
    r4, y4 = lax.ppermute(to_send[0], "seq", to_x), lax.ppermute(to_send[1], "seq", to_y0)
    ok_x = jnp.where(even, position >= 1, position >= 3)
    ok_z = jnp.where(even, position >= 0, position >= 4)
    flags = jnp.stack([even, ok_x, ok_z, column == 0]).astype(jnp.int32)
    part1, lse1, msg1 = attend(flags, diagonal, q_mate, r1, r3, y1, y3, 0)
    flags, msg1 = lax.optimization_barrier((flags, msg1))
    msg1 = lax.ppermute(msg1, "seq", swap)
    part2, lse2, msg2 = attend(flags, diagonal, q_mate, r2, r4, y2, y4, CHUNKS[0])
    msg2 = lax.ppermute(msg2, "seq", swap)
    return merge(part2, lse2, msg2, merge(part1, lse1, msg1)).T


def solution(mesh):
    return jax.shard_map(
        shards,
        mesh=mesh,
        in_specs=(P(("hist", "seq"), None), P(("hist", "seq"), None), P(("hist", "seq"), None)),
        out_specs=P(("hist", "seq"), None),
        check_vma=False,
    )
```

time: 77.1 us -> 83.7 us (1.086)
  the two profiles are of different devices: /device:TPU:250 before, /device:TPU:184 now
where the time goes in v2:
time: 83.7 us; the launch traced here: 83 us
  starting transfers between devices  42.5 us (51%)
  Pallas kernels  17 us (20%)
  waiting for transfers between devices  10 us (12%)
  other arithmetic  8.62 us (10%)
  local copies, waits for them, and re-layouts  4.58 us (5%)
    ppermute x2, starting transfers between devices, shards(): r1, y1 = (lax.ppermute(x_1, 'seq', to_x), lax.ppermute(y_1, 'seq', to_y))  11.3 us
    ppermute x2, starting transfers between devices, shards(): lax.ppermute(to_send[1], 'seq', to_y0)  9.85 us
    pallas_call x2, Pallas kernels, attend(): pl.pallas_call(lambda *refs: attend_kernel(first, *refs), in_specs=[pl.Bl...  9.82 us
    ppermute x2, starting transfers between devices, shards(): lax.ppermute(to_send[0], 'seq', to_x)  7.62 us
    ppermute x1, waiting for transfers between devices, shards(): msg1 = lax.ppermute(msg1, 'seq', swap)  6.54 us
    ppermute x2, starting transfers between devices, shards(): r2, y2 = (lax.ppermute(x_2, 'seq', to_x), lax.ppermute(y_2, 'seq', to_y))  5.96 us
    pallas_call x1, Pallas kernels, diag(): pl.pallas_call(diag_kernel, in_specs=[ANY] * 3, out_specs=[VMEM] * 5, out...  5.92 us
    unnamed x12, local copies, waits for them, and re-layouts  4.58 us
  transfers between devices with their start and end apart: 11, of which 2 were waited for; matrix products, arithmetic and copies ran while one was open for 8% of the time, Pallas kernels for 19%

profile of v2, /device:TPU:184, one launch (start us, length us, event | category | flops | bytes accessed | tf_op | source)
XLA Modules:
  0.0 83.0 jit_solution(10977949835812762753)
XLA Ops:
  0.0 2.2 %fusion.1 = (bf16[960,256]{1,0:T(8,128)(2,1)}, bf16[960,256]{1,0:T(8,128)(2,1)}) fusion(bf16[1600,256]{1,0:T(8,128)(2,1)} %bitcast.8, bf16[1600,256]{1,0:T(8,128)(2,1)} %bitcast.11, pred[]{:T(512)S(6)} %eq.19), kind=kLoop, calls=%fused_computation.8 | loop fusion | flops 245760 | bytes 1966081 | tf_op jit(solution)/shard_map/slice | solution.py:275
  2.2 1.4 %collective-permute-start.1 = (bf16[960,256]{1,0:T(8,128)(2,1)}, bf16[960,256]{1,0:T(8,128)(2,1)}, u32[]{:S(2)}, u32[]{:S(2)}) collective-permute-start(bf16[960,256]{1,0:T(8,128)(2,1)} %get-tuple-element.55), channel_id=1, source_target_pairs={{1,5},{3,7},{5,9},{7,11},{9,13},{11,15},{13,17},{15,19},{17,21},{1... | collective-permute-start | bytes 1474568 | tf_op jit(solution)/shard_map/ppermute | solution.py:277
  3.6 9.9 %collective-permute-start = (bf16[960,256]{1,0:T(8,128)(2,1)}, bf16[960,256]{1,0:T(8,128)(2,1)}, u32[]{:S(2)}, u32[]{:S(2)}) collective-permute-start(bf16[960,256]{1,0:T(8,128)(2,1)} %get-tuple-element.56), channel_id=1, source_target_pairs={{0,3},{1,2},{2,5},{3,0},{4,7},{5,6},{6,9},{7,4},{8,11},{9,10},{10,... | collective-permute-start | bytes 1474568 | tf_op jit(solution)/shard_map/ppermute | solution.py:277
  13.5 1.9 %collective-permute-start.2 = (bf16[1600,256]{1,0:T(8,128)(2,1)}, bf16[1600,256]{1,0:T(8,128)(2,1)S(1)}, u32[]{:S(2)}, u32[]{:S(2)}) collective-permute-start(bf16[1600,256]{1,0:T(8,128)(2,1)} %bitcast.6.q_any), channel_id=1, source_target_pairs={{0,1},{1,0},{2,3},{3,2},{4,5},{5,4},{6,7},{7,6},{8,9},{9,8},{10,11... | collective-permute-start | bytes 2457608 | tf_op jit(solution)/shard_map/ppermute | solution.py:279
  15.5 2.0 %fusion = (bf16[640,256]{1,0:T(8,128)(2,1)}, bf16[640,256]{1,0:T(8,128)(2,1)}) fusion(bf16[1600,256]{1,0:T(8,128)(2,1)} %bitcast.9, bf16[1600,256]{1,0:T(8,128)(2,1)} %bitcast.12, pred[]{:T(512)S(6)} %eq.19), kind=kLoop, calls=%fused_computation.7 | loop fusion | flops 163840 | bytes 1310721 | tf_op jit(solution)/shard_map/slice | solution.py:275
  17.4 1.4 %collective-permute-start.6 = (bf16[640,256]{1,0:T(8,128)(2,1)}, bf16[640,256]{1,0:T(8,128)(2,1)}, u32[]{:S(2)}, u32[]{:S(2)}) collective-permute-start(bf16[640,256]{1,0:T(8,128)(2,1)} %get-tuple-element.51), channel_id=1, source_target_pairs={{1,5},{3,7},{5,9},{7,11},{9,13},{11,15},{13,17},{15,19},{17,21},{1... | collective-permute-start | bytes 983048 | tf_op jit(solution)/shard_map/ppermute | solution.py:278
  18.8 4.6 %collective-permute-start.5 = (bf16[640,256]{1,0:T(8,128)(2,1)}, bf16[640,256]{1,0:T(8,128)(2,1)}, u32[]{:S(2)}, u32[]{:S(2)}) collective-permute-start(bf16[640,256]{1,0:T(8,128)(2,1)} %get-tuple-element.52), channel_id=1, source_target_pairs={{0,3},{1,2},{2,5},{3,0},{4,7},{5,6},{6,9},{7,4},{8,11},{9,10},{10,... | collective-permute-start | bytes 983048 | tf_op jit(solution)/shard_map/ppermute | solution.py:278
  23.4 0.0 copy-start.4
  23.4 1.1 %copy-done.4 = bf16[256,1600]{0,1:T(8,128)(2,1)S(1)} copy-done((bf16[256,1600]{0,1:T(8,128)(2,1)S(1)}, bf16[256,1600]{0,1:T(8,128)(2,1)}, u32[]{:S(2)}) %copy-start.4) | copy-done | bytes 819224
  24.5 1.1 %copy-done.5 = bf16[256,1600]{0,1:T(8,128)(2,1)S(1)} copy-done((bf16[256,1600]{0,1:T(8,128)(2,1)S(1)}, bf16[256,1600]{0,1:T(8,128)(2,1)}, u32[]{:S(2)}) %copy-start.5) | copy-done | bytes 819224
  25.7 5.9 %diag.1 = (bf16[1600,256]{1,0:T(8,128)(2,1)S(1)}, bf16[1600,256]{1,0:T(8,128)(2,1)S(1)}, bf16[1600,256]{1,0:T(8,128)(2,1)S(1)}, f32[1600,256]{1,0:T(8,128)S(1)}, f32[5,16,256]{2,1,0:T(8,128)S(1)}) custom-call(bf16[1600,256]{1,0:T(8,128)(2,1)} %bitcast.6.q_any, bf16[1600,256]{1,0:T(8,128)(2,1)S(1)} %bitcast.10, bf16[1600,256]{1,0:T(8,128)(2,1)S(1)} %bitcast.13), custom_call_target="tpu_custom_call" | custom-call | flops 419430400 | bytes 4096000 | tf_op jit(solution)/shard_map/diag/pallas_call | solution.py:191
  31.6 0.0 copy-start
  31.6 0.0 collective-permute-done.refs_7_
  31.6 2.5 %broadcast_select_fusion = (bf16[960,256]{1,0:T(8,128)(2,1)}, bf16[960,256]{1,0:T(8,128)(2,1)}) fusion(bf16[960,256]{1,0:T(8,128)(2,1)} %collective-permute-done.refs_7_, pred[]{:T(512)} %eq.18, bf16[1600,256]{1,0:T(8,128)(2,1)S(1)} %get-tuple-element.34.refs_3_, bf16[960,256]{1,0:T(8,128)(2,1)} %collective-permute-done.1.refs_9_, pred[]{:T(512)S(6)} %eq.19), kind=kLoop, calls=%fused_computation.1 | loop fusion | flops 491520 | bytes 2457602 | tf_op jit(solution)/shard_map/jit(_where)/select_n | solution.py:284
  34.1 2.6 %collective-permute-start.4 = (bf16[960,256]{1,0:T(8,128)(2,1)}, bf16[960,256]{1,0:T(8,128)(2,1)}, u32[]{:S(2)}, u32[]{:S(2)}) collective-permute-start(bf16[960,256]{1,0:T(8,128)(2,1)} %get-tuple-element.53), channel_id=1, source_target_pairs={{0,4},{1,5},{3,7},{4,8},{5,9},{7,11},{8,12},{9,13},{11,15},{12,16}... | collective-permute-start | bytes 1474568 | tf_op jit(solution)/shard_map/ppermute | solution.py:287
  36.7 2.5 %collective-permute-start.3 = (bf16[960,256]{1,0:T(8,128)(2,1)}, bf16[960,256]{1,0:T(8,128)(2,1)}, u32[]{:S(2)}, u32[]{:S(2)}) collective-permute-start(bf16[960,256]{1,0:T(8,128)(2,1)} %get-tuple-element.54), channel_id=1, source_target_pairs={{0,3},{1,2},{2,5},{3,0},{4,7},{5,6},{6,9},{7,4},{8,11},{9,10},{10,... | collective-permute-start | bytes 1474568 | tf_op jit(solution)/shard_map/ppermute | solution.py:287
  39.2 0.0 collective-permute-done.6.refs_9_
  39.2 1.9 %broadcast_select_fusion.2 = (bf16[640,256]{1,0:T(8,128)(2,1)}, bf16[640,256]{1,0:T(8,128)(2,1)}) fusion(bf16[640,256]{1,0:T(8,128)(2,1)} %collective-permute-done.5.refs_7_, pred[]{:T(512)} %eq.18, bf16[1600,256]{1,0:T(8,128)(2,1)S(1)} %get-tuple-element.34.refs_3_, bf16[640,256]{1,0:T(8,128)(2,1)} %collective-permute-done.6.refs_9_, pred[]{:T(512)S(6)} %eq.19), kind=kLoop, calls=%fused_computation.4 | loop fusion | flops 327680 | bytes 1638402 | tf_op jit(solution)/shard_map/jit(_where)/select_n | solution.py:284
  41.1 7.3 %collective-permute-start.8 = (bf16[640,256]{1,0:T(8,128)(2,1)}, bf16[640,256]{1,0:T(8,128)(2,1)}, u32[]{:S(2)}, u32[]{:S(2)}) collective-permute-start(bf16[640,256]{1,0:T(8,128)(2,1)} %get-tuple-element.49), channel_id=1, source_target_pairs={{0,4},{1,5},{3,7},{4,8},{5,9},{7,11},{8,12},{9,13},{11,15},{12,16}... | collective-permute-start | bytes 983048 | tf_op jit(solution)/shard_map/ppermute | solution.py:290
  48.4 5.1 %collective-permute-start.7 = (bf16[640,256]{1,0:T(8,128)(2,1)}, bf16[640,256]{1,0:T(8,128)(2,1)}, u32[]{:S(2)}, u32[]{:S(2)}) collective-permute-start(bf16[640,256]{1,0:T(8,128)(2,1)} %get-tuple-element.50), channel_id=1, source_target_pairs={{0,3},{1,2},{2,5},{3,0},{4,7},{5,6},{6,9},{7,4},{8,11},{9,10},{10,... | collective-permute-start | bytes 983048 | tf_op jit(solution)/shard_map/ppermute | solution.py:290
  53.6 0.1 add_convert_fusion.refs_0_
  53.7 0.0 copy-start.1
  53.7 1.1 %copy-done.1 = bf16[1600,256]{1,0:T(8,128)(2,1)S(1)} copy-done((bf16[1600,256]{1,0:T(8,128)(2,1)S(1)}, bf16[1600,256]{1,0:T(8,128)(2,1)}, u32[]{:S(2)}) %copy-start.1) | copy-done | bytes 819224
  54.8 1.1 %copy-done.3 = bf16[1600,256]{1,0:T(8,128)(2,1)S(1)} copy-done((bf16[1600,256]{1,0:T(8,128)(2,1)S(1)}, bf16[1600,256]{1,0:T(8,128)(2,1)}, u32[]{:S(2)}) %copy-start.3) | copy-done | bytes 819224
  56.0 5.7 %attend.2 = (f32[960,256]{1,0:T(8,128)S(1)}, f32[3,8,256]{2,1,0:T(8,128)S(1)}, bf16[1008,256]{1,0:T(8,128)(2,1)S(1)}) custom-call(s32[4]{0:T(128)S(1)} %add_convert_fusion.refs_0_, bf16[1600,256]{1,0:T(8,128)(2,1)S(1)} %copy-done.1, bf16[1600,256]{1,0:T(8,128)(2,1)S(1)} %copy-done.3, bf16[1600,256]{1,0:T(8,128)(2,1)S(1)} %get-tuple-element.34.refs_3_, ...), custom_call_target="tpu_custom_call" | custom-call | flops 754974720 | bytes 5898240 | tf_op jit(solution)/shard_map/attend/pallas_call | solution.py:212
  61.7 1.9 %collective-permute-start.10 = (bf16[1008,256]{1,0:T(8,128)(2,1)S(1)}, bf16[1008,256]{1,0:T(8,128)(2,1)S(1)}, u32[]{:S(2)}, u32[]{:S(2)}) collective-permute-start(bf16[1008,256]{1,0:T(8,128)(2,1)S(1)} %get-tuple-element.48), channel_id=1, source_target_pairs={{0,1},{1,0},{2,3},{3,2},{4,5},{5,4},{6,7},{7,6},{8,9},{9,8},{10,11... | collective-permute-start | bytes 1548296 | tf_op jit(solution)/shard_map/ppermute | solution.py:296
  63.6 4.1 %attend.3 = (f32[640,256]{1,0:T(8,128)S(1)}, f32[2,8,256]{2,1,0:T(8,128)S(1)}, bf16[672,256]{1,0:T(8,128)(2,1)S(1)}) custom-call(s32[4]{0:T(128)S(1)} %add_convert_fusion.refs_0_, bf16[1600,256]{1,0:T(8,128)(2,1)S(1)} %copy-done.1, bf16[1600,256]{1,0:T(8,128)(2,1)S(1)} %copy-done.3, bf16[1600,256]{1,0:T(8,128)(2,1)S(1)} %get-tuple-element.34.refs_3_, ...), custom_call_target="tpu_custom_call" | custom-call | flops 503316480 | bytes 3932160 | tf_op jit(solution)/shard_map/attend/pallas_call | solution.py:212
  67.7 3.9 %collective-permute-start.9 = (bf16[672,256]{1,0:T(8,128)(2,1)S(1)}, bf16[672,256]{1,0:T(8,128)(2,1)S(1)}, u32[]{:S(2)}, u32[]{:S(2)}) collective-permute-start(bf16[672,256]{1,0:T(8,128)(2,1)S(1)} %get-tuple-element.45), channel_id=1, source_target_pairs={{0,1},{1,0},{2,3},{3,2},{4,5},{5,4},{6,7},{7,6},{8,9},{9,8},{10,11... | collective-permute-start | bytes 1032200 | tf_op jit(solution)/shard_map/ppermute | solution.py:298
  71.7 6.5 %collective-permute-done.10.msg = bf16[1008,256]{1,0:T(8,128)(2,1)S(1)} collective-permute-done((bf16[1008,256]{1,0:T(8,128)(2,1)S(1)}, bf16[1008,256]{1,0:T(8,128)(2,1)S(1)}, u32[]{:S(2)}, u32[]{:S(2)}) %collective-permute-start.10) | collective-permute-done | bytes 516128 | tf_op jit(solution)/shard_map/ppermute | solution.py:296
  78.2 0.2 merge.2.rest_0_
  78.4 3.5 %collective-permute-done.9.msg = bf16[672,256]{1,0:T(8,128)(2,1)S(1)} collective-permute-done((bf16[672,256]{1,0:T(8,128)(2,1)S(1)}, bf16[672,256]{1,0:T(8,128)(2,1)S(1)}, u32[]{:S(2)}, u32[]{:S(2)}) %collective-permute-start.9) | collective-permute-done | bytes 344096 | tf_op jit(solution)/shard_map/ppermute | solution.py:298
  81.9 1.1 %merge.3 = bf16[1600,256]{1,0:T(8,128)(2,1)} custom-call(f32[640,256]{1,0:T(8,128)S(1)} %get-tuple-element.43.part, f32[2,8,256]{2,1,0:T(8,128)S(1)} %get-tuple-element.44.part_lse, bf16[672,256]{1,0:T(8,128)(2,1)S(1)} %collective-permute-done.9.msg, bf16[960,256]{1,0:T(8,128)(2,1)S(1)} %merge.2.rest_0_), custom_call_target="tpu_custom_call" | custom-call | flops 655360 | bytes 1310720 | tf_op jit(solution)/shard_map/merge/pallas_call | solution.py:251
  (12 shorter events, 0.0 us)
Async XLA Ops:
  2.2 29.4 %collective-permute-start.1 = (bf16[960,256]{1,0:T(8,128)(2,1)}, bf16[960,256]{1,0:T(8,128)(2,1)}, u32[]{:S(2)}, u32[]{:S(2)}) collective-permute-start(bf16[960,256]{1,0:T(8,128)(2,1)} %get-tuple-element.55), channel_id=1, source_target_pairs={{1,5},{3,7},{5,9},{7,11},{9,13},{11,15},{13,17},{15,19},{17,21},{1... | collective-permute-start | bytes 1474568 | tf_op jit(solution)/shard_map/ppermute | solution.py:277
  3.6 28.0 %collective-permute-start = (bf16[960,256]{1,0:T(8,128)(2,1)}, bf16[960,256]{1,0:T(8,128)(2,1)}, u32[]{:S(2)}, u32[]{:S(2)}) collective-permute-start(bf16[960,256]{1,0:T(8,128)(2,1)} %get-tuple-element.56), channel_id=1, source_target_pairs={{0,3},{1,2},{2,5},{3,0},{4,7},{5,6},{6,9},{7,4},{8,11},{9,10},{10,... | collective-permute-start | bytes 1474568 | tf_op jit(solution)/shard_map/ppermute | solution.py:277
  13.5 40.1 %collective-permute-start.2 = (bf16[1600,256]{1,0:T(8,128)(2,1)}, bf16[1600,256]{1,0:T(8,128)(2,1)S(1)}, u32[]{:S(2)}, u32[]{:S(2)}) collective-permute-start(bf16[1600,256]{1,0:T(8,128)(2,1)} %bitcast.6.q_any), channel_id=1, source_target_pairs={{0,1},{1,0},{2,3},{3,2},{4,5},{5,4},{6,7},{7,6},{8,9},{9,8},{10,11... | collective-permute-start | bytes 2457608 | tf_op jit(solution)/shard_map/ppermute | solution.py:279
  17.4 21.8 %collective-permute-start.6 = (bf16[640,256]{1,0:T(8,128)(2,1)}, bf16[640,256]{1,0:T(8,128)(2,1)}, u32[]{:S(2)}, u32[]{:S(2)}) collective-permute-start(bf16[640,256]{1,0:T(8,128)(2,1)} %get-tuple-element.51), channel_id=1, source_target_pairs={{1,5},{3,7},{5,9},{7,11},{9,13},{11,15},{13,17},{15,19},{17,21},{1... | collective-permute-start | bytes 983048 | tf_op jit(solution)/shard_map/ppermute | solution.py:278
  18.8 20.4 %collective-permute-start.5 = (bf16[640,256]{1,0:T(8,128)(2,1)}, bf16[640,256]{1,0:T(8,128)(2,1)}, u32[]{:S(2)}, u32[]{:S(2)}) collective-permute-start(bf16[640,256]{1,0:T(8,128)(2,1)} %get-tuple-element.52), channel_id=1, source_target_pairs={{0,3},{1,2},{2,5},{3,0},{4,7},{5,6},{6,9},{7,4},{8,11},{9,10},{10,... | collective-permute-start | bytes 983048 | tf_op jit(solution)/shard_map/ppermute | solution.py:278
  23.4 1.1 %copy-start.4 = (bf16[256,1600]{0,1:T(8,128)(2,1)S(1)}, bf16[256,1600]{0,1:T(8,128)(2,1)}, u32[]{:S(2)}) copy-start(bf16[256,1600]{0,1:T(8,128)(2,1)} %param.4) | copy-start | bytes 2457604
  24.5 1.1 %copy-start.5 = (bf16[256,1600]{0,1:T(8,128)(2,1)S(1)}, bf16[256,1600]{0,1:T(8,128)(2,1)}, u32[]{:S(2)}) copy-start(bf16[256,1600]{0,1:T(8,128)(2,1)} %param.5) | copy-start | bytes 2457604
  31.6 9.5 %copy-start = (bf16[1600,256]{1,0:T(8,128)(2,1)}, bf16[1600,256]{1,0:T(8,128)(2,1)S(1)}, u32[]{:S(2)}) copy-start(bf16[1600,256]{1,0:T(8,128)(2,1)S(1)} %get-tuple-element.32.refs_1_) | copy-start | bytes 2457604
  31.6 9.5 %copy-start.2 = (bf16[1600,256]{1,0:T(8,128)(2,1)}, bf16[1600,256]{1,0:T(8,128)(2,1)S(1)}, u32[]{:S(2)}) copy-start(bf16[1600,256]{1,0:T(8,128)(2,1)S(1)} %get-tuple-element.33.refs_2_) | copy-start | bytes 2457604
  34.1 19.6 %collective-permute-start.4 = (bf16[960,256]{1,0:T(8,128)(2,1)}, bf16[960,256]{1,0:T(8,128)(2,1)}, u32[]{:S(2)}, u32[]{:S(2)}) collective-permute-start(bf16[960,256]{1,0:T(8,128)(2,1)} %get-tuple-element.53), channel_id=1, source_target_pairs={{0,4},{1,5},{3,7},{4,8},{5,9},{7,11},{8,12},{9,13},{11,15},{12,16}... | collective-permute-start | bytes 1474568 | tf_op jit(solution)/shard_map/ppermute | solution.py:287
  36.7 17.0 %collective-permute-start.3 = (bf16[960,256]{1,0:T(8,128)(2,1)}, bf16[960,256]{1,0:T(8,128)(2,1)}, u32[]{:S(2)}, u32[]{:S(2)}) collective-permute-start(bf16[960,256]{1,0:T(8,128)(2,1)} %get-tuple-element.54), channel_id=1, source_target_pairs={{0,3},{1,2},{2,5},{3,0},{4,7},{5,6},{6,9},{7,4},{8,11},{9,10},{10,... | collective-permute-start | bytes 1474568 | tf_op jit(solution)/shard_map/ppermute | solution.py:287
  41.1 22.5 %collective-permute-start.8 = (bf16[640,256]{1,0:T(8,128)(2,1)}, bf16[640,256]{1,0:T(8,128)(2,1)}, u32[]{:S(2)}, u32[]{:S(2)}) collective-permute-start(bf16[640,256]{1,0:T(8,128)(2,1)} %get-tuple-element.49), channel_id=1, source_target_pairs={{0,4},{1,5},{3,7},{4,8},{5,9},{7,11},{8,12},{9,13},{11,15},{12,16}... | collective-permute-start | bytes 983048 | tf_op jit(solution)/shard_map/ppermute | solution.py:290
  48.4 15.2 %collective-permute-start.7 = (bf16[640,256]{1,0:T(8,128)(2,1)}, bf16[640,256]{1,0:T(8,128)(2,1)}, u32[]{:S(2)}, u32[]{:S(2)}) collective-permute-start(bf16[640,256]{1,0:T(8,128)(2,1)} %get-tuple-element.50), channel_id=1, source_target_pairs={{0,3},{1,2},{2,5},{3,0},{4,7},{5,6},{6,9},{7,4},{8,11},{9,10},{10,... | collective-permute-start | bytes 983048 | tf_op jit(solution)/shard_map/ppermute | solution.py:290
  53.7 1.1 %copy-start.1 = (bf16[1600,256]{1,0:T(8,128)(2,1)S(1)}, bf16[1600,256]{1,0:T(8,128)(2,1)}, u32[]{:S(2)}) copy-start(bf16[1600,256]{1,0:T(8,128)(2,1)} %copy-done) | copy-start | bytes 2457604
  54.8 1.1 %copy-start.3 = (bf16[1600,256]{1,0:T(8,128)(2,1)S(1)}, bf16[1600,256]{1,0:T(8,128)(2,1)}, u32[]{:S(2)}) copy-start(bf16[1600,256]{1,0:T(8,128)(2,1)} %copy-done.2) | copy-start | bytes 2457604
  61.7 16.5 %collective-permute-start.10 = (bf16[1008,256]{1,0:T(8,128)(2,1)S(1)}, bf16[1008,256]{1,0:T(8,128)(2,1)S(1)}, u32[]{:S(2)}, u32[]{:S(2)}) collective-permute-start(bf16[1008,256]{1,0:T(8,128)(2,1)S(1)} %get-tuple-element.48), channel_id=1, source_target_pairs={{0,1},{1,0},{2,3},{3,2},{4,5},{5,4},{6,7},{7,6},{8,9},{9,8},{10,11... | collective-permute-start | bytes 1548296 | tf_op jit(solution)/shard_map/ppermute | solution.py:296
  67.7 14.2 %collective-permute-start.9 = (bf16[672,256]{1,0:T(8,128)(2,1)S(1)}, bf16[672,256]{1,0:T(8,128)(2,1)S(1)}, u32[]{:S(2)}, u32[]{:S(2)}) collective-permute-start(bf16[672,256]{1,0:T(8,128)(2,1)S(1)} %get-tuple-element.45), channel_id=1, source_target_pairs={{0,1},{1,0},{2,3},{3,2},{4,5},{5,4},{6,7},{7,6},{8,9},{9,8},{10,11... | collective-permute-start | bytes 1032200 | tf_op jit(solution)/shard_map/ppermute | solution.py:298

commit v3 on v2

v3 whole, which is shorter than its diff:
```python
import jax
import jax.numpy as jnp
from jax import lax
from jax.experimental import pallas as pl
from jax.experimental.pallas import tpu as pltpu
from jax.sharding import PartitionSpec as P

HEADS = 25
WIDTH = 64
GROUP = 5
HALVES = (2, 3)
CHUNKS = (2, 2, 1)
STEP = GROUP * WIDTH
ONES = 16
STAT = 16
MSG = STEP + STAT
SCALE = WIDTH ** -0.5 * 1.4426950408889634
NEG = -1e30


def scores(key_cols, query_cols):
    return lax.dot_general(key_cols, query_cols, (((0,), (0,)), ((), ())), preferred_element_type=jnp.float32)


def fold_max(tile):
    return jnp.max(tile.reshape(tile.shape[0] // 8, 8, tile.shape[1]), axis=0)


def top_of(folded):
    return jnp.max(folded, axis=0, keepdims=True) * SCALE


def with_ones(value):
    return jnp.concatenate([value, jnp.ones((ONES, value.shape[1]), value.dtype)], axis=0)


def weights(score, top):
    return jnp.exp2(score * SCALE - top).astype(jnp.bfloat16)


def pipelined(units):
    results, depth = [[] for _ in units], len(units[0])
    for i in range(len(units) + depth - 1):
        for stage in range(depth):
            if 0 <= i - stage < len(units):
                done = results[i - stage]
                done.append(units[i - stage][stage](*done))
    return results


def stack_rows(rows, size):
    fill = [jnp.zeros_like(rows[0])] * (size - len(rows))
    return jnp.concatenate(list(rows) + fill, axis=0)


def mix(a, b):
    (acc_a, total_a, top_a), (acc_b, total_b, top_b) = a, b
    top = jnp.maximum(top_a, top_b)
    factor_a, factor_b = jnp.exp2(top_a - top), jnp.exp2(top_b - top)
    total = total_a * factor_a + total_b * factor_b
    return acc_a * (factor_a / total) + acc_b * (factor_b / total), top + jnp.log2(total)


def attend_kernel(first, skip, q_own, q_mate, k_own, v_own, r1, r3, y1, y3, part, part_lse, msg):
    position = lax.axis_index("seq")
    even, is0 = position % 2 == 0, position % 4 == 0
    ok_x, ok_z = (position >= 3) | (even & (position >= 1)), even | (position >= 4)
    rows = q_own.shape[1]
    half = rows // 2
    later = lax.broadcasted_iota(jnp.int32, (half, half), 0) > lax.broadcasted_iota(jnp.int32, (half, half), 1)

    def one_group(i, carry):
        def rows_at(group, g, step=STEP):
            return pl.ds(pl.multiple_of(group * step + g * WIDTH, 16), WIDTH)

        def here(g):
            return rows_at(skip + i, g)

        def there(g):
            return rows_at(first + i, g)

        def unit(score, value, ok):
            def top(s):
                return top_of(fold_max(s))

            def weight(s, top):
                return weights(s, top)

            def product(s, top, weight):
                acc = jnp.dot(with_ones(value()), weight, preferred_element_type=jnp.float32)
                return acc[:WIDTH], acc[WIDTH : WIDTH + 1], jnp.where(ok, top, NEG)

            return score, top, weight, product

        def unit_x(g):
            def score():
                key = jnp.where(is0, y3[here(g)], r1[there(g)])
                return scores(key, jnp.concatenate([q_own[there(g)], q_mate[there(g)]], axis=1))

            return unit(score, lambda: r3[here(g)], ok_x)

        def unit_z(g):
            def score():
                return scores(jnp.where(even, k_own[there(g)], y3[here(g)]), q_mate[there(g)])

            return unit(score, lambda: jnp.where(even, v_own[there(g)], y1[here(g)]), ok_z)

        def unit_d(g):
            def score():
                q, k = q_own[there(g)], k_own[there(g)]
                return scores(k[:, :half], q), scores(k[:, half:], q[:, half:])

            def top(score):
                first, last = score
                corner, last = jnp.where(later, NEG, first[:, :half]), jnp.where(later, NEG, last)
                right = first[:, half:]
                top_a, top_b = top_of(fold_max(corner)), top_of(jnp.maximum(fold_max(right), fold_max(last)))
                return corner, right, last, top_a, top_b

            def weight(score, top):
                corner, right, last, top_a, top_b = top
                upper = jnp.concatenate([weights(corner, top_a), weights(right, top_b)], axis=1)
                lower = jnp.concatenate([jnp.zeros((half, half), jnp.bfloat16), weights(last, top_b)], axis=1)
                return jnp.concatenate([upper, lower], axis=0)

            def product(score, top, weight):
                acc = jnp.dot(with_ones(v_own[there(g)]), weight, preferred_element_type=jnp.float32)
                return acc[:WIDTH], acc[WIDTH : WIDTH + 1], jnp.concatenate(top[3:], axis=1)

            return score, top, weight, product

        done = pipelined([u(g) for g in range(GROUP) for u in (unit_x, unit_z, unit_d)])
        own, mate = [], []
        for g in range(GROUP):
            x, z, d = [done[3 * g + j][3] for j in range(3)]
            own.append(mix(d, [e[:, :rows] for e in x]))
            mate.append(mix(z, [e[:, rows:] for e in x]))
        for g in range(GROUP):
            part[rows_at(i, g)] = own[g][0]
            msg[rows_at(i, g, MSG)] = mate[g][0].astype(jnp.bfloat16)
        part_lse[i] = stack_rows([lse for _, lse in own], 8)
        stat = jnp.concatenate([lse for _, lse in mate], axis=0)
        high = stat.astype(jnp.bfloat16).astype(jnp.float32)
        mid = (stat - high).astype(jnp.bfloat16).astype(jnp.float32)
        stat = stack_rows([high, mid, stat - high - mid, jnp.zeros((1, rows), jnp.float32)], 4)
        msg[pl.ds(pl.multiple_of(i * MSG + STEP, 16), STAT)] = stat.astype(jnp.bfloat16)
        return carry

    lax.fori_loop(0, part_lse.shape[0], one_group, 0)


VMEM = pl.BlockSpec(memory_space=pltpu.VMEM)


def attend(arguments, q_mate, came, first, skip, groups):
    rows = q_mate.shape[1]
    size, heads = groups * STEP, groups * GROUP
    q, k, v = arguments
    return pl.pallas_call(
        lambda *refs: attend_kernel(first, skip, *refs),
        in_specs=[VMEM] * 8,
        out_specs=[VMEM] * 3,
        out_shape=[
            jax.ShapeDtypeStruct((size, rows), jnp.float32),
            jax.ShapeDtypeStruct((groups, 8, rows), jnp.float32),
            jax.ShapeDtypeStruct((groups * MSG, rows), jnp.bfloat16),
        ],
        compiler_params=pltpu.CompilerParams(vmem_limit_bytes=12 * 2**20),
        cost_estimate=pl.CostEstimate(
            flops=heads * 4 * 4 * 4 * rows * rows * WIDTH,
            bytes_accessed=heads * WIDTH * rows * 24,
            transcendentals=heads * 4 * rows * rows,
        ),
        name="attend",
    )(q, q_mate, k, v, *came)


def merge_kernel(part, part_lse, msg, *rest):
    out = rest[-1]
    at = 0
    for before in rest[:-1]:
        out[pl.ds(at, before.shape[0])] = before[...]
        at += before.shape[0]
    for i in range(part_lse.shape[0]):
        stat = msg[pl.ds(i * MSG + STEP, STAT)].astype(jnp.float32)
        lse = stat[:GROUP] + stat[GROUP : 2 * GROUP] + stat[2 * GROUP : 3 * GROUP]
        gap = lse - part_lse[i, :GROUP]
        mine, theirs = 1.0 / (1.0 + jnp.exp2(gap)), 1.0 / (1.0 + jnp.exp2(-gap))
        for g in range(GROUP):
            row, src = i * STEP + g * WIDTH, pl.ds(i * MSG + g * WIDTH, WIDTH)
            both = part[pl.ds(row, WIDTH)] * mine[g : g + 1] + msg[src].astype(jnp.float32) * theirs[g : g + 1]
            out[pl.ds(at + row, WIDTH)] = both.astype(jnp.bfloat16)


def merge(part, part_lse, msg, *before):
    size, rows = part.shape
    done = sum(b.shape[0] for b in before)
    return pl.pallas_call(
        merge_kernel,
        in_specs=[VMEM] * (3 + len(before)),
        out_specs=VMEM,
        out_shape=jax.ShapeDtypeStruct((done + size, rows), jnp.bfloat16),
        compiler_params=pltpu.CompilerParams(vmem_limit_bytes=12 * 2**20),
        cost_estimate=pl.CostEstimate(flops=size * rows * 4, bytes_accessed=size * rows * 8, transcendentals=0),
        name="merge",
    )(part, part_lse, msg, *before)


def shards(queries, keys, values):
    length = lax.axis_size("seq")
    position = lax.axis_index("seq")
    column = position % 4
    q, k, v = queries.T, keys.T, values.T
    swap = [(i, i ^ 1) for i in range(length)]
    to_x = [(i, i + (3, 1, 3, -3)[i % 4]) for i in range(length)]
    to_x = [(i, j) for i, j in to_x if j < length]
    to_y = [(i, i + 4) for i in range(length - 4) if i % 2]
    to_y0 = [(i, i + 4) for i in range(length - 4) if i % 4 != 2]

    cut = HALVES[0] * STEP
    k1, k2, v1, v2 = k[:cut], k[cut:], v[:cut], v[cut:]
    r1 = lax.ppermute(k, "seq", to_x)
    y1, y2 = lax.ppermute(v1, "seq", to_y), lax.ppermute(v2, "seq", to_y)
    q_mate = lax.ppermute(q, "seq", swap)
    send = jnp.where(column == 3, y1, v1)
    r3 = lax.ppermute(send, "seq", to_x)
    r1 = lax.optimization_barrier((r1, send))[0]
    send = jnp.where(column == 0, r1[:cut], k1)
    y3 = lax.ppermute(send, "seq", to_y0)
    r1, y2 = lax.optimization_barrier((r1, y2, send))[:2]
    send = jnp.where(column == 0, r1[cut:], k2)
    y4 = lax.ppermute(send, "seq", to_y0)
    r4 = lax.ppermute(jnp.where(column == 3, y2, v2), "seq", to_x)
    halves, arguments = ((r1, r3, y1, y3), (r1, r4, y2, y4)), (q, k, v)
    results, first = [], 0
    for groups in CHUNKS:
        half = int(first >= HALVES[0])
        part, lse, msg = attend(arguments, q_mate, halves[half], first, first - half * HALVES[0], groups)
        q_mate, msg = lax.optimization_barrier((q_mate, msg))
        results.append((part, lse, lax.ppermute(msg, "seq", swap)))
        first += groups
    before = [merge(*result) for result in results[:-1]]
    return merge(*results[-1], *before).T


def solution(mesh):
    return jax.shard_map(
        shards,
        mesh=mesh,
        in_specs=(P(("hist", "seq"), None), P(("hist", "seq"), None), P(("hist", "seq"), None)),
        out_specs=P(("hist", "seq"), None),
        check_vma=False,
    )
```

time: 83.7 us -> 73.5 us (0.88)
  the two profiles are of different devices: /device:TPU:184 before, /device:TPU:248 now
where the time goes in v3:
time: 73.5 us; the launch traced here: 73 us
  starting transfers between devices  48.5 us (66%)
  Pallas kernels  14.1 us (19%)
  waiting for transfers between devices  6.3 us (9%)
  local copies, waits for them, and re-layouts  3.64 us (5%)
    pallas_call x3, Pallas kernels, attend(): pl.pallas_call(lambda *refs: attend_kernel(first, skip, *refs), in_specs=...  12.8 us
    ppermute x1, starting transfers between devices, shards(): q_mate = lax.ppermute(q, 'seq', swap)  11.2 us
    ppermute x3, starting transfers between devices, shards(): results.append((part, lse, lax.ppermute(msg, 'seq', swap)))  9.83 us
    ppermute x1, starting transfers between devices, shards(): y3 = lax.ppermute(send, 'seq', to_y0)  8.19 us
    ppermute x1, starting transfers between devices, shards(): r4 = lax.ppermute(jnp.where(column == 3, y2, v2), 'seq', to_x)  7.01 us
    ppermute x3, waiting for transfers between devices, shards(): results.append((part, lse, lax.ppermute(msg, 'seq', swap)))  5.08 us
    ppermute x1, starting transfers between devices, shards(): r1 = lax.ppermute(k, 'seq', to_x)  4.66 us
    ppermute x1, starting transfers between devices, shards(): r3 = lax.ppermute(send, 'seq', to_x)  4.23 us
  transfers between devices with their start and end apart: 11, of which 3 were waited for; matrix products, arithmetic and copies ran while one was open for 5% of the time, Pallas kernels for 18%

profile of v3, /device:TPU:248, one launch (start us, length us, event | category | flops | bytes accessed | tf_op | source)
XLA Modules:
  0.0 73.0 jit_solution(3399991366071850413)
XLA Ops:
  0.0 4.7 %collective-permute-start.1 = (bf16[1600,256]{1,0:T(8,128)(2,1)}, bf16[1600,256]{1,0:T(8,128)(2,1)S(1)}, u32[]{:S(2)}, u32[]{:S(2)}) collective-permute-start(bf16[1600,256]{1,0:T(8,128)(2,1)} %bitcast.11), channel_id=1, source_target_pairs={{0,3},{1,2},{2,5},{3,0},{4,7},{5,6},{6,9},{7,4},{8,11},{9,10},{10,... | collective-permute-start | bytes 2457608 | tf_op jit(solution)/shard_map/ppermute | solution.py:222
  4.7 0.0 copy-start
  4.7 1.8 %slice.24 = bf16[640,256]{1,0:T(8,128)(2,1)} slice(bf16[1600,256]{1,0:T(8,128)(2,1)} %bitcast.4), slice={[0:640], [0:256]} | slice | bytes 655360 | tf_op jit(solution)/shard_map/slice | solution.py:221
  6.5 0.8 %collective-permute-start.2 = (bf16[640,256]{1,0:T(8,128)(2,1)}, bf16[640,256]{1,0:T(8,128)(2,1)S(1)}, u32[]{:S(2)}, u32[]{:S(2)}) collective-permute-start(bf16[640,256]{1,0:T(8,128)(2,1)} %slice.24), channel_id=1, source_target_pairs={{1,5},{3,7},{5,9},{7,11},{9,13},{11,15},{13,17},{15,19},{17,21},{1... | collective-permute-start | bytes 983048 | tf_op jit(solution)/shard_map/ppermute | solution.py:223
  7.3 1.8 %slice.25 = bf16[960,256]{1,0:T(8,128)(2,1)} slice(bf16[1600,256]{1,0:T(8,128)(2,1)} %bitcast.5), slice={[640:1600], [0:256]} | slice | bytes 983040 | tf_op jit(solution)/shard_map/slice | solution.py:221
  9.1 0.7 collective-permute-start.3
  9.8 11.2 %collective-permute-start = (bf16[1600,256]{1,0:T(8,128)(2,1)}, bf16[1600,256]{1,0:T(8,128)(2,1)}, u32[]{:S(2)}, u32[]{:S(2)}) collective-permute-start(bf16[1600,256]{1,0:T(8,128)(2,1)} %bitcast.refs_0_), channel_id=1, source_target_pairs={{0,1},{1,0},{2,3},{3,2},{4,5},{5,4},{6,7},{7,6},{8,9},{9,8},{10,11... | collective-permute-start | bytes 2457608 | tf_op jit(solution)/shard_map/ppermute | solution.py:224
  21.0 0.0 collective-permute-done.2.refs_6_
  21.1 4.2 %collective-permute-start.4 = (bf16[640,256]{1,0:T(8,128)(2,1)S(1)}, bf16[640,256]{1,0:T(8,128)(2,1)S(1)}, u32[]{:S(2)}, u32[]{:S(2)}) collective-permute-start(bf16[640,256]{1,0:T(8,128)(2,1)S(1)} %broadcast_select_fusion.1), channel_id=1, source_target_pairs={{0,3},{1,2},{2,5},{3,0},{4,7},{5,6},{6,9},{7,4},{8,11},{9,10},{10,... | collective-permute-start | bytes 983048 | tf_op jit(solution)/shard_map/ppermute | solution.py:226
  25.3 0.0 collective-permute-done.1.refs_4_
  25.4 8.2 %collective-permute-start.5 = (bf16[640,256]{1,0:T(8,128)(2,1)S(1)}, bf16[640,256]{1,0:T(8,128)(2,1)S(1)}, u32[]{:S(2)}, u32[]{:S(2)}) collective-permute-start(bf16[640,256]{1,0:T(8,128)(2,1)S(1)} %slice_select_fusion.1), channel_id=1, source_target_pairs={{0,4},{1,5},{3,7},{4,8},{5,9},{7,11},{8,12},{9,13},{11,15},{12,16}... | collective-permute-start | bytes 983048 | tf_op jit(solution)/shard_map/ppermute | solution.py:229
  33.6 0.0 collective-permute-done.3.refs_6_
  33.6 0.1 broadcast_select_fusion
  33.7 0.1 slice_select_fusion
  33.7 1.9 %collective-permute-start.7 = (bf16[960,256]{1,0:T(8,128)(2,1)S(1)}, bf16[960,256]{1,0:T(8,128)(2,1)S(1)}, u32[]{:S(2)}, u32[]{:S(2)}) collective-permute-start(bf16[960,256]{1,0:T(8,128)(2,1)S(1)} %slice_select_fusion), channel_id=1, source_target_pairs={{0,4},{1,5},{3,7},{4,8},{5,9},{7,11},{8,12},{9,13},{11,15},{12,16}... | collective-permute-start | bytes 1474568 | tf_op jit(solution)/shard_map/ppermute | solution.py:232
  35.7 7.0 %collective-permute-start.6 = (bf16[960,256]{1,0:T(8,128)(2,1)S(1)}, bf16[960,256]{1,0:T(8,128)(2,1)S(1)}, u32[]{:S(2)}, u32[]{:S(2)}) collective-permute-start(bf16[960,256]{1,0:T(8,128)(2,1)S(1)} %broadcast_select_fusion), channel_id=1, source_target_pairs={{0,3},{1,2},{2,5},{3,0},{4,7},{5,6},{6,9},{7,4},{8,11},{9,10},{10,... | collective-permute-start | bytes 1474568 | tf_op jit(solution)/shard_map/ppermute | solution.py:233
  42.7 0.0 collective-permute-done.4.refs_5_
  42.7 0.0 collective-permute-done.refs_1_
  42.7 0.0 collective-permute-done.5.refs_7_
  42.7 4.9 %attend.3 = (f32[640,256]{1,0:T(8,128)S(1)}, f32[2,8,256]{2,1,0:T(8,128)S(1)}, bf16[672,256]{1,0:T(8,128)(2,1)S(1)}) custom-call(bf16[1600,256]{1,0:T(8,128)(2,1)} %bitcast.refs_0_, bf16[1600,256]{1,0:T(8,128)(2,1)} %collective-permute-done.refs_1_, bf16[1600,256]{1,0:T(8,128)(2,1)S(1)} %bitcast.14, bf16[1600,256]{1,0:T(8,128)(2,1)S(1)} %bitcast.8, ...), custom_call_target="tpu_custom_call" | custom-call | flops 2684354560 | bytes 3932160 | tf_op jit(solution)/shard_map/attend/pallas_call | solution.py:159
  47.6 3.6 %collective-permute-start.9 = (bf16[672,256]{1,0:T(8,128)(2,1)S(1)}, bf16[672,256]{1,0:T(8,128)(2,1)S(1)}, u32[]{:S(2)}, u32[]{:S(2)}) collective-permute-start(bf16[672,256]{1,0:T(8,128)(2,1)S(1)} %get-tuple-element.35), channel_id=1, source_target_pairs={{0,1},{1,0},{2,3},{3,2},{4,5},{5,4},{6,7},{7,6},{8,9},{9,8},{10,11... | collective-permute-start | bytes 1032200 | tf_op jit(solution)/shard_map/ppermute | solution.py:240
  51.2 0.0 collective-permute-done.7.refs_7_
  51.2 1.2 %collective-permute-done.6.refs_5_ = bf16[960,256]{1,0:T(8,128)(2,1)S(1)} collective-permute-done((bf16[960,256]{1,0:T(8,128)(2,1)S(1)}, bf16[960,256]{1,0:T(8,128)(2,1)S(1)}, u32[]{:S(2)}, u32[]{:S(2)}) %collective-permute-start.6) | collective-permute-done | bytes 491552 | tf_op jit(solution)/shard_map/ppermute | solution.py:233
  52.4 4.8 %attend.4 = (f32[640,256]{1,0:T(8,128)S(1)}, f32[2,8,256]{2,1,0:T(8,128)S(1)}, bf16[672,256]{1,0:T(8,128)(2,1)S(1)}) custom-call(bf16[1600,256]{1,0:T(8,128)(2,1)} %bitcast.refs_0_, bf16[1600,256]{1,0:T(8,128)(2,1)} %collective-permute-done.refs_1_, bf16[1600,256]{1,0:T(8,128)(2,1)S(1)} %bitcast.15, bf16[1600,256]{1,0:T(8,128)(2,1)S(1)} %bitcast.9, ...), custom_call_target="tpu_custom_call" | custom-call | flops 2684354560 | bytes 3932160 | tf_op jit(solution)/shard_map/attend/pallas_call | solution.py:159
  57.3 4.3 %collective-permute-start.10 = (bf16[672,256]{1,0:T(8,128)(2,1)S(1)}, bf16[672,256]{1,0:T(8,128)(2,1)S(1)}, u32[]{:S(2)}, u32[]{:S(2)}) collective-permute-start(bf16[672,256]{1,0:T(8,128)(2,1)S(1)} %get-tuple-element.38), channel_id=1, source_target_pairs={{0,1},{1,0},{2,3},{3,2},{4,5},{5,4},{6,7},{7,6},{8,9},{9,8},{10,11... | collective-permute-start | bytes 1032200 | tf_op jit(solution)/shard_map/ppermute | solution.py:240
  61.6 3.1 %attend.5 = (f32[320,256]{1,0:T(8,128)S(1)}, f32[1,8,256]{2,1,0:T(8,128)S(1)}, bf16[336,256]{1,0:T(8,128)(2,1)S(1)}) custom-call(bf16[1600,256]{1,0:T(8,128)(2,1)} %bitcast.refs_0_, bf16[1600,256]{1,0:T(8,128)(2,1)} %collective-permute-done.refs_1_, bf16[1600,256]{1,0:T(8,128)(2,1)S(1)} %bitcast.16, bf16[1600,256]{1,0:T(8,128)(2,1)S(1)} %bitcast.10, ...), custom_call_target="tpu_custom_call" | custom-call | flops 1342177280 | bytes 1966080 | tf_op jit(solution)/shard_map/attend/pallas_call | solution.py:159
  64.7 1.9 %collective-permute-start.8 = (bf16[336,256]{1,0:T(8,128)(2,1)S(1)}, bf16[336,256]{1,0:T(8,128)(2,1)S(1)}, u32[]{:S(2)}, u32[]{:S(2)}) collective-permute-start(bf16[336,256]{1,0:T(8,128)(2,1)S(1)} %get-tuple-element.32), channel_id=1, source_target_pairs={{0,1},{1,0},{2,3},{3,2},{4,5},{5,4},{6,7},{7,6},{8,9},{9,8},{10,11... | collective-permute-start | bytes 516104 | tf_op jit(solution)/shard_map/ppermute | solution.py:240
  66.6 0.1 merge.3.rest_0_
  66.8 1.5 %collective-permute-done.10.msg = bf16[672,256]{1,0:T(8,128)(2,1)S(1)} collective-permute-done((bf16[672,256]{1,0:T(8,128)(2,1)S(1)}, bf16[672,256]{1,0:T(8,128)(2,1)S(1)}, u32[]{:S(2)}, u32[]{:S(2)}) %collective-permute-start.10) | collective-permute-done | bytes 344096 | tf_op jit(solution)/shard_map/ppermute | solution.py:240
  68.3 0.1 merge.4.rest_1_
  68.4 3.5 %collective-permute-done.8.msg = bf16[336,256]{1,0:T(8,128)(2,1)S(1)} collective-permute-done((bf16[336,256]{1,0:T(8,128)(2,1)S(1)}, bf16[336,256]{1,0:T(8,128)(2,1)S(1)}, u32[]{:S(2)}, u32[]{:S(2)}) %collective-permute-start.8) | collective-permute-done | bytes 172064 | tf_op jit(solution)/shard_map/ppermute | solution.py:240
  72.0 1.0 %merge.5 = bf16[1600,256]{1,0:T(8,128)(2,1)} custom-call(f32[320,256]{1,0:T(8,128)S(1)} %get-tuple-element.29.part, f32[1,8,256]{2,1,0:T(8,128)S(1)} %get-tuple-element.30.part_lse, bf16[336,256]{1,0:T(8,128)(2,1)S(1)} %collective-permute-done.8.msg, bf16[640,256]{1,0:T(8,128)(2,1)S(1)} %merge.3.rest_0_, bf16[640,256]{1,0:T(8,128)(2,1)S(1)} %merge.4.rest_1_), custom_call_target="tpu_custom_call" | custom-call | flops 327680 | bytes 655360 | tf_op jit(solution)/shard_map/merge/pallas_call | solution.py:198
  (6 shorter events, 0.1 us)
Async XLA Ops:
  0.0 25.3 %collective-permute-start.1 = (bf16[1600,256]{1,0:T(8,128)(2,1)}, bf16[1600,256]{1,0:T(8,128)(2,1)S(1)}, u32[]{:S(2)}, u32[]{:S(2)}) collective-permute-start(bf16[1600,256]{1,0:T(8,128)(2,1)} %bitcast.11), channel_id=1, source_target_pairs={{0,3},{1,2},{2,5},{3,0},{4,7},{5,6},{6,9},{7,4},{8,11},{9,10},{10,... | collective-permute-start | bytes 2457608 | tf_op jit(solution)/shard_map/ppermute | solution.py:222
  4.7 16.4 %copy-start = (bf16[256,1600]{0,1:T(8,128)(2,1)S(1)}, bf16[256,1600]{0,1:T(8,128)(2,1)}, u32[]{:S(2)}) copy-start(bf16[256,1600]{0,1:T(8,128)(2,1)} %param.5) | copy-start | bytes 2457604
  6.5 18.9 %copy-start.1 = (bf16[256,1600]{0,1:T(8,128)(2,1)S(1)}, bf16[256,1600]{0,1:T(8,128)(2,1)}, u32[]{:S(2)}) copy-start(bf16[256,1600]{0,1:T(8,128)(2,1)} %param.4) | copy-start | bytes 2457604
  6.5 14.6 %collective-permute-start.2 = (bf16[640,256]{1,0:T(8,128)(2,1)}, bf16[640,256]{1,0:T(8,128)(2,1)S(1)}, u32[]{:S(2)}, u32[]{:S(2)}) collective-permute-start(bf16[640,256]{1,0:T(8,128)(2,1)} %slice.24), channel_id=1, source_target_pairs={{1,5},{3,7},{5,9},{7,11},{9,13},{11,15},{13,17},{15,19},{17,21},{1... | collective-permute-start | bytes 983048 | tf_op jit(solution)/shard_map/ppermute | solution.py:223
  9.1 24.5 %collective-permute-start.3 = (bf16[960,256]{1,0:T(8,128)(2,1)}, bf16[960,256]{1,0:T(8,128)(2,1)S(1)}, u32[]{:S(2)}, u32[]{:S(2)}) collective-permute-start(bf16[960,256]{1,0:T(8,128)(2,1)} %slice.25), channel_id=1, source_target_pairs={{1,5},{3,7},{5,9},{7,11},{9,13},{11,15},{13,17},{15,19},{17,21},{1... | collective-permute-start | bytes 1474568 | tf_op jit(solution)/shard_map/ppermute | solution.py:223
  9.8 32.9 %collective-permute-start = (bf16[1600,256]{1,0:T(8,128)(2,1)}, bf16[1600,256]{1,0:T(8,128)(2,1)}, u32[]{:S(2)}, u32[]{:S(2)}) collective-permute-start(bf16[1600,256]{1,0:T(8,128)(2,1)} %bitcast.refs_0_), channel_id=1, source_target_pairs={{0,1},{1,0},{2,3},{3,2},{4,5},{5,4},{6,7},{7,6},{8,9},{9,8},{10,11... | collective-permute-start | bytes 2457608 | tf_op jit(solution)/shard_map/ppermute | solution.py:224
  21.1 21.6 %collective-permute-start.4 = (bf16[640,256]{1,0:T(8,128)(2,1)S(1)}, bf16[640,256]{1,0:T(8,128)(2,1)S(1)}, u32[]{:S(2)}, u32[]{:S(2)}) collective-permute-start(bf16[640,256]{1,0:T(8,128)(2,1)S(1)} %broadcast_select_fusion.1), channel_id=1, source_target_pairs={{0,3},{1,2},{2,5},{3,0},{4,7},{5,6},{6,9},{7,4},{8,11},{9,10},{10,... | collective-permute-start | bytes 983048 | tf_op jit(solution)/shard_map/ppermute | solution.py:226
  25.4 17.3 %collective-permute-start.5 = (bf16[640,256]{1,0:T(8,128)(2,1)S(1)}, bf16[640,256]{1,0:T(8,128)(2,1)S(1)}, u32[]{:S(2)}, u32[]{:S(2)}) collective-permute-start(bf16[640,256]{1,0:T(8,128)(2,1)S(1)} %slice_select_fusion.1), channel_id=1, source_target_pairs={{0,4},{1,5},{3,7},{4,8},{5,9},{7,11},{8,12},{9,13},{11,15},{12,16}... | collective-permute-start | bytes 983048 | tf_op jit(solution)/shard_map/ppermute | solution.py:229
  33.7 17.5 %collective-permute-start.7 = (bf16[960,256]{1,0:T(8,128)(2,1)S(1)}, bf16[960,256]{1,0:T(8,128)(2,1)S(1)}, u32[]{:S(2)}, u32[]{:S(2)}) collective-permute-start(bf16[960,256]{1,0:T(8,128)(2,1)S(1)} %slice_select_fusion), channel_id=1, source_target_pairs={{0,4},{1,5},{3,7},{4,8},{5,9},{7,11},{8,12},{9,13},{11,15},{12,16}... | collective-permute-start | bytes 1474568 | tf_op jit(solution)/shard_map/ppermute | solution.py:232
  35.7 16.8 %collective-permute-start.6 = (bf16[960,256]{1,0:T(8,128)(2,1)S(1)}, bf16[960,256]{1,0:T(8,128)(2,1)S(1)}, u32[]{:S(2)}, u32[]{:S(2)}) collective-permute-start(bf16[960,256]{1,0:T(8,128)(2,1)S(1)} %broadcast_select_fusion), channel_id=1, source_target_pairs={{0,3},{1,2},{2,5},{3,0},{4,7},{5,6},{6,9},{7,4},{8,11},{9,10},{10,... | collective-permute-start | bytes 1474568 | tf_op jit(solution)/shard_map/ppermute | solution.py:233
  47.6 19.0 %collective-permute-start.9 = (bf16[672,256]{1,0:T(8,128)(2,1)S(1)}, bf16[672,256]{1,0:T(8,128)(2,1)S(1)}, u32[]{:S(2)}, u32[]{:S(2)}) collective-permute-start(bf16[672,256]{1,0:T(8,128)(2,1)S(1)} %get-tuple-element.35), channel_id=1, source_target_pairs={{0,1},{1,0},{2,3},{3,2},{4,5},{5,4},{6,7},{7,6},{8,9},{9,8},{10,11... | collective-permute-start | bytes 1032200 | tf_op jit(solution)/shard_map/ppermute | solution.py:240
  57.3 11.0 %collective-permute-start.10 = (bf16[672,256]{1,0:T(8,128)(2,1)S(1)}, bf16[672,256]{1,0:T(8,128)(2,1)S(1)}, u32[]{:S(2)}, u32[]{:S(2)}) collective-permute-start(bf16[672,256]{1,0:T(8,128)(2,1)S(1)} %get-tuple-element.38), channel_id=1, source_target_pairs={{0,1},{1,0},{2,3},{3,2},{4,5},{5,4},{6,7},{7,6},{8,9},{9,8},{10,11... | collective-permute-start | bytes 1032200 | tf_op jit(solution)/shard_map/ppermute | solution.py:240
  64.7 7.3 %collective-permute-start.8 = (bf16[336,256]{1,0:T(8,128)(2,1)S(1)}, bf16[336,256]{1,0:T(8,128)(2,1)S(1)}, u32[]{:S(2)}, u32[]{:S(2)}) collective-permute-start(bf16[336,256]{1,0:T(8,128)(2,1)S(1)} %get-tuple-element.32), channel_id=1, source_target_pairs={{0,1},{1,0},{2,3},{3,2},{4,5},{5,4},{6,7},{7,6},{8,9},{9,8},{10,11... | collective-permute-start | bytes 516104 | tf_op jit(solution)/shard_map/ppermute | solution.py:240

commit v4 on v3

--- a/solution.py
+++ b/solution.py
@@ -61,7 +61,7 @@
     return acc_a * (factor_a / total) + acc_b * (factor_b / total), top + jnp.log2(total)
 
 
-def attend_kernel(first, skip, q_own, q_mate, k_own, v_own, r1, r3, y1, y3, part, part_lse, msg):
+def attend_kernel(first, skip, q_any, qm_any, k_own, v_own, r1, r3, y1, y3, part, part_lse, msg, q_own, q_mate, sems):
     position = lax.axis_index("seq")
     even, is0 = position % 2 == 0, position % 4 == 0
     ok_x, ok_z = (position >= 3) | (even & (position >= 1)), even | (position >= 4)
@@ -69,7 +69,20 @@
     half = rows // 2
     later = lax.broadcasted_iota(jnp.int32, (half, half), 0) > lax.broadcasted_iota(jnp.int32, (half, half), 1)
 
+    def copies(i):
+        src = pl.ds(pl.multiple_of((first + i) * STEP, STEP), STEP)
+        dst = pl.ds(pl.multiple_of(i * STEP, STEP), STEP)
+        pairs = (q_any, q_own), (qm_any, q_mate)
+        return [pltpu.make_async_copy(a.at[src], b.at[dst], sems.at[i, j]) for j, (a, b) in enumerate(pairs)]
+
+    for i in range(part_lse.shape[0]):
+        for copy in copies(i):
+            copy.start()
+
     def one_group(i, carry):
+        for copy in copies(i):
+            copy.wait()
+
         def rows_at(group, g, step=STEP):
             return pl.ds(pl.multiple_of(group * step + g * WIDTH, 16), WIDTH)
 
@@ -95,19 +108,19 @@
         def unit_x(g):
             def score():
                 key = jnp.where(is0, y3[here(g)], r1[there(g)])
-                return scores(key, jnp.concatenate([q_own[there(g)], q_mate[there(g)]], axis=1))
+                return scores(key, jnp.concatenate([q_own[rows_at(i, g)], q_mate[rows_at(i, g)]], axis=1))
 
             return unit(score, lambda: r3[here(g)], ok_x)
 
         def unit_z(g):
             def score():
-                return scores(jnp.where(even, k_own[there(g)], y3[here(g)]), q_mate[there(g)])
+                return scores(jnp.where(even, k_own[there(g)], y3[here(g)]), q_mate[rows_at(i, g)])
 
             return unit(score, lambda: jnp.where(even, v_own[there(g)], y1[here(g)]), ok_z)
 
         def unit_d(g):
             def score():
-                q, k = q_own[there(g)], k_own[there(g)]
+                q, k = q_own[rows_at(i, g)], k_own[there(g)]
                 return scores(k[:, :half], q), scores(k[:, half:], q[:, half:])
 
             def top(score):
@@ -150,6 +163,7 @@
 
 
 VMEM = pl.BlockSpec(memory_space=pltpu.VMEM)
+ANY = pl.BlockSpec(memory_space=pl.ANY)
 
 
 def attend(arguments, q_mate, came, first, skip, groups):
@@ -158,13 +172,14 @@
     q, k, v = arguments
     return pl.pallas_call(
         lambda *refs: attend_kernel(first, skip, *refs),
-        in_specs=[VMEM] * 8,
+        in_specs=[ANY] * 2 + [VMEM] * 6,
         out_specs=[VMEM] * 3,
         out_shape=[
             jax.ShapeDtypeStruct((size, rows), jnp.float32),
             jax.ShapeDtypeStruct((groups, 8, rows), jnp.float32),
             jax.ShapeDtypeStruct((groups * MSG, rows), jnp.bfloat16),
         ],
+        scratch_shapes=[pltpu.VMEM((size, rows), jnp.bfloat16)] * 2 + [pltpu.SemaphoreType.DMA((groups, 2))],
         compiler_params=pltpu.CompilerParams(vmem_limit_bytes=12 * 2**20),
         cost_estimate=pl.CostEstimate(
             flops=heads * 4 * 4 * 4 * rows * rows * WIDTH,

time: 73.5 us -> 72.7 us (0.989)
  Pallas kernels: 14.1 us -> 13 us
    pallas_call x3, Pallas kernels: 12.8 us -> 11.7 us  [attend(): pl.pallas_call(lambda *refs: attend_kernel(first, skip, *refs), in_specs=...]
  transfers between devices with their start and end apart: 11 -> 11, of which waited for: 3 -> 3; matrix products, arithmetic and copies ran while one was open for 5% -> 5% of each run, Pallas kernels for 18% -> 17%
where the time goes in v4:
time: 72.7 us; the launch traced here: 72.2 us
  starting transfers between devices  48.5 us (67%)
  Pallas kernels  13 us (18%)
  waiting for transfers between devices  6.67 us (9%)
  local copies, waits for them, and re-layouts  3.64 us (5%)
    pallas_call x3, Pallas kernels, attend(): pl.pallas_call(lambda *refs: attend_kernel(first, skip, *refs), in_specs=...  11.7 us
    ppermute x1, starting transfers between devices, shards(): q_mate = lax.ppermute(q, 'seq', swap)  11.2 us
    ppermute x3, starting transfers between devices, shards(): results.append((part, lse, lax.ppermute(msg, 'seq', swap)))  9.82 us
    ppermute x1, starting transfers between devices, shards(): y3 = lax.ppermute(send, 'seq', to_y0)  8.19 us
    ppermute x1, starting transfers between devices, shards(): r4 = lax.ppermute(jnp.where(column == 3, y2, v2), 'seq', to_x)  7.01 us
    ppermute x3, waiting for transfers between devices, shards(): results.append((part, lse, lax.ppermute(msg, 'seq', swap)))  5.08 us
    ppermute x1, starting transfers between devices, shards(): r1 = lax.ppermute(k, 'seq', to_x)  4.66 us
    ppermute x1, starting transfers between devices, shards(): r3 = lax.ppermute(send, 'seq', to_x)  4.23 us
  transfers between devices with their start and end apart: 11, of which 3 were waited for; matrix products, arithmetic and copies ran while one was open for 5% of the time, Pallas kernels for 17%

profile of v4, /device:TPU:248, one launch (start us, length us, event | category | flops | bytes accessed | tf_op | source)
XLA Modules:
  0.0 72.2 jit_solution(123858847133719578)
XLA Ops:
  0.0 4.7 %collective-permute-start.1 = (bf16[1600,256]{1,0:T(8,128)(2,1)}, bf16[1600,256]{1,0:T(8,128)(2,1)S(1)}, u32[]{:S(2)}, u32[]{:S(2)}) collective-permute-start(bf16[1600,256]{1,0:T(8,128)(2,1)} %bitcast.11), channel_id=1, source_target_pairs={{0,3},{1,2},{2,5},{3,0},{4,7},{5,6},{6,9},{7,4},{8,11},{9,10},{10,... | collective-permute-start | bytes 2457608 | tf_op jit(solution)/shard_map/ppermute | solution.py:237
  4.7 0.0 copy-start
  4.7 1.8 %slice.24 = bf16[640,256]{1,0:T(8,128)(2,1)} slice(bf16[1600,256]{1,0:T(8,128)(2,1)} %bitcast.4), slice={[0:640], [0:256]} | slice | bytes 655360 | tf_op jit(solution)/shard_map/slice | solution.py:236
  6.5 0.8 %collective-permute-start.2 = (bf16[640,256]{1,0:T(8,128)(2,1)}, bf16[640,256]{1,0:T(8,128)(2,1)S(1)}, u32[]{:S(2)}, u32[]{:S(2)}) collective-permute-start(bf16[640,256]{1,0:T(8,128)(2,1)} %slice.24), channel_id=1, source_target_pairs={{1,5},{3,7},{5,9},{7,11},{9,13},{11,15},{13,17},{15,19},{17,21},{1... | collective-permute-start | bytes 983048 | tf_op jit(solution)/shard_map/ppermute | solution.py:238
  7.3 1.8 %slice.25 = bf16[960,256]{1,0:T(8,128)(2,1)} slice(bf16[1600,256]{1,0:T(8,128)(2,1)} %bitcast.5), slice={[640:1600], [0:256]} | slice | bytes 983040 | tf_op jit(solution)/shard_map/slice | solution.py:236
  9.1 0.7 collective-permute-start.3
  9.8 11.2 %collective-permute-start = (bf16[1600,256]{1,0:T(8,128)(2,1)}, bf16[1600,256]{1,0:T(8,128)(2,1)}, u32[]{:S(2)}, u32[]{:S(2)}) collective-permute-start(bf16[1600,256]{1,0:T(8,128)(2,1)} %bitcast.refs_0_), channel_id=1, source_target_pairs={{0,1},{1,0},{2,3},{3,2},{4,5},{5,4},{6,7},{7,6},{8,9},{9,8},{10,11... | collective-permute-start | bytes 2457608 | tf_op jit(solution)/shard_map/ppermute | solution.py:239
  21.0 0.0 collective-permute-done.2.refs_6_
  21.1 4.2 %collective-permute-start.4 = (bf16[640,256]{1,0:T(8,128)(2,1)S(1)}, bf16[640,256]{1,0:T(8,128)(2,1)S(1)}, u32[]{:S(2)}, u32[]{:S(2)}) collective-permute-start(bf16[640,256]{1,0:T(8,128)(2,1)S(1)} %broadcast_select_fusion.1), channel_id=1, source_target_pairs={{0,3},{1,2},{2,5},{3,0},{4,7},{5,6},{6,9},{7,4},{8,11},{9,10},{10,... | collective-permute-start | bytes 983048 | tf_op jit(solution)/shard_map/ppermute | solution.py:241
  25.3 0.0 collective-permute-done.1.refs_4_
  25.4 8.2 %collective-permute-start.5 = (bf16[640,256]{1,0:T(8,128)(2,1)S(1)}, bf16[640,256]{1,0:T(8,128)(2,1)S(1)}, u32[]{:S(2)}, u32[]{:S(2)}) collective-permute-start(bf16[640,256]{1,0:T(8,128)(2,1)S(1)} %slice_select_fusion.1), channel_id=1, source_target_pairs={{0,4},{1,5},{3,7},{4,8},{5,9},{7,11},{8,12},{9,13},{11,15},{12,16}... | collective-permute-start | bytes 983048 | tf_op jit(solution)/shard_map/ppermute | solution.py:244
  33.6 0.0 collective-permute-done.3.refs_6_
  33.6 0.1 broadcast_select_fusion
  33.7 0.1 slice_select_fusion
  33.7 1.9 %collective-permute-start.7 = (bf16[960,256]{1,0:T(8,128)(2,1)S(1)}, bf16[960,256]{1,0:T(8,128)(2,1)S(1)}, u32[]{:S(2)}, u32[]{:S(2)}) collective-permute-start(bf16[960,256]{1,0:T(8,128)(2,1)S(1)} %slice_select_fusion), channel_id=1, source_target_pairs={{0,4},{1,5},{3,7},{4,8},{5,9},{7,11},{8,12},{9,13},{11,15},{12,16}... | collective-permute-start | bytes 1474568 | tf_op jit(solution)/shard_map/ppermute | solution.py:247
  35.7 7.0 %collective-permute-start.6 = (bf16[960,256]{1,0:T(8,128)(2,1)S(1)}, bf16[960,256]{1,0:T(8,128)(2,1)S(1)}, u32[]{:S(2)}, u32[]{:S(2)}) collective-permute-start(bf16[960,256]{1,0:T(8,128)(2,1)S(1)} %broadcast_select_fusion), channel_id=1, source_target_pairs={{0,3},{1,2},{2,5},{3,0},{4,7},{5,6},{6,9},{7,4},{8,11},{9,10},{10,... | collective-permute-start | bytes 1474568 | tf_op jit(solution)/shard_map/ppermute | solution.py:248
  42.7 0.0 collective-permute-done.refs_1_
  42.7 0.0 collective-permute-done.5.refs_7_
  42.7 4.5 %attend.3 = (f32[640,256]{1,0:T(8,128)S(1)}, f32[2,8,256]{2,1,0:T(8,128)S(1)}, bf16[672,256]{1,0:T(8,128)(2,1)S(1)}) custom-call(bf16[1600,256]{1,0:T(8,128)(2,1)} %bitcast.refs_0_, bf16[1600,256]{1,0:T(8,128)(2,1)} %collective-permute-done.refs_1_, bf16[1600,256]{1,0:T(8,128)(2,1)S(1)} %bitcast.14, bf16[1600,256]{1,0:T(8,128)(2,1)S(1)} %bitcast.8, ...), custom_call_target="tpu_custom_call" | custom-call | flops 2684354560 | bytes 3932160 | tf_op jit(solution)/shard_map/attend/pallas_call | solution.py:173
  47.2 3.6 %collective-permute-start.9 = (bf16[672,256]{1,0:T(8,128)(2,1)S(1)}, bf16[672,256]{1,0:T(8,128)(2,1)S(1)}, u32[]{:S(2)}, u32[]{:S(2)}) collective-permute-start(bf16[672,256]{1,0:T(8,128)(2,1)S(1)} %get-tuple-element.35), channel_id=1, source_target_pairs={{0,1},{1,0},{2,3},{3,2},{4,5},{5,4},{6,7},{7,6},{8,9},{9,8},{10,11... | collective-permute-start | bytes 1032200 | tf_op jit(solution)/shard_map/ppermute | solution.py:255
  50.8 0.0 collective-permute-done.7.refs_7_
  50.8 1.6 %collective-permute-done.6.refs_5_ = bf16[960,256]{1,0:T(8,128)(2,1)S(1)} collective-permute-done((bf16[960,256]{1,0:T(8,128)(2,1)S(1)}, bf16[960,256]{1,0:T(8,128)(2,1)S(1)}, u32[]{:S(2)}, u32[]{:S(2)}) %collective-permute-start.6) | collective-permute-done | bytes 491552 | tf_op jit(solution)/shard_map/ppermute | solution.py:248
  52.4 4.5 %attend.4 = (f32[640,256]{1,0:T(8,128)S(1)}, f32[2,8,256]{2,1,0:T(8,128)S(1)}, bf16[672,256]{1,0:T(8,128)(2,1)S(1)}) custom-call(bf16[1600,256]{1,0:T(8,128)(2,1)} %bitcast.refs_0_, bf16[1600,256]{1,0:T(8,128)(2,1)} %collective-permute-done.refs_1_, bf16[1600,256]{1,0:T(8,128)(2,1)S(1)} %bitcast.15, bf16[1600,256]{1,0:T(8,128)(2,1)S(1)} %bitcast.9, ...), custom_call_target="tpu_custom_call" | custom-call | flops 2684354560 | bytes 3932160 | tf_op jit(solution)/shard_map/attend/pallas_call | solution.py:173
  56.9 4.3 %collective-permute-start.10 = (bf16[672,256]{1,0:T(8,128)(2,1)S(1)}, bf16[672,256]{1,0:T(8,128)(2,1)S(1)}, u32[]{:S(2)}, u32[]{:S(2)}) collective-permute-start(bf16[672,256]{1,0:T(8,128)(2,1)S(1)} %get-tuple-element.38), channel_id=1, source_target_pairs={{0,1},{1,0},{2,3},{3,2},{4,5},{5,4},{6,7},{7,6},{8,9},{9,8},{10,11... | collective-permute-start | bytes 1032200 | tf_op jit(solution)/shard_map/ppermute | solution.py:255
  61.2 2.7 %attend.5 = (f32[320,256]{1,0:T(8,128)S(1)}, f32[1,8,256]{2,1,0:T(8,128)S(1)}, bf16[336,256]{1,0:T(8,128)(2,1)S(1)}) custom-call(bf16[1600,256]{1,0:T(8,128)(2,1)} %bitcast.refs_0_, bf16[1600,256]{1,0:T(8,128)(2,1)} %collective-permute-done.refs_1_, bf16[1600,256]{1,0:T(8,128)(2,1)S(1)} %bitcast.16, bf16[1600,256]{1,0:T(8,128)(2,1)S(1)} %bitcast.10, ...), custom_call_target="tpu_custom_call" | custom-call | flops 1342177280 | bytes 1966080 | tf_op jit(solution)/shard_map/attend/pallas_call | solution.py:173
  63.9 1.9 %collective-permute-start.8 = (bf16[336,256]{1,0:T(8,128)(2,1)S(1)}, bf16[336,256]{1,0:T(8,128)(2,1)S(1)}, u32[]{:S(2)}, u32[]{:S(2)}) collective-permute-start(bf16[336,256]{1,0:T(8,128)(2,1)S(1)} %get-tuple-element.32), channel_id=1, source_target_pairs={{0,1},{1,0},{2,3},{3,2},{4,5},{5,4},{6,7},{7,6},{8,9},{9,8},{10,11... | collective-permute-start | bytes 516104 | tf_op jit(solution)/shard_map/ppermute | solution.py:255
  65.9 0.0 collective-permute-done.9.msg
  65.9 0.1 merge.3.rest_0_
  66.0 2.0 %collective-permute-done.10.msg = bf16[672,256]{1,0:T(8,128)(2,1)S(1)} collective-permute-done((bf16[672,256]{1,0:T(8,128)(2,1)S(1)}, bf16[672,256]{1,0:T(8,128)(2,1)S(1)}, u32[]{:S(2)}, u32[]{:S(2)}) %collective-permute-start.10) | collective-permute-done | bytes 344096 | tf_op jit(solution)/shard_map/ppermute | solution.py:255
  68.0 0.1 merge.4.rest_1_
  68.2 3.0 %collective-permute-done.8.msg = bf16[336,256]{1,0:T(8,128)(2,1)S(1)} collective-permute-done((bf16[336,256]{1,0:T(8,128)(2,1)S(1)}, bf16[336,256]{1,0:T(8,128)(2,1)S(1)}, u32[]{:S(2)}, u32[]{:S(2)}) %collective-permute-start.8) | collective-permute-done | bytes 172064 | tf_op jit(solution)/shard_map/ppermute | solution.py:255
  71.2 1.0 %merge.5 = bf16[1600,256]{1,0:T(8,128)(2,1)} custom-call(f32[320,256]{1,0:T(8,128)S(1)} %get-tuple-element.29.part, f32[1,8,256]{2,1,0:T(8,128)S(1)} %get-tuple-element.30.part_lse, bf16[336,256]{1,0:T(8,128)(2,1)S(1)} %collective-permute-done.8.msg, bf16[640,256]{1,0:T(8,128)(2,1)S(1)} %merge.3.rest_0_, bf16[640,256]{1,0:T(8,128)(2,1)S(1)} %merge.4.rest_1_), custom_call_target="tpu_custom_call" | custom-call | flops 327680 | bytes 655360 | tf_op jit(solution)/shard_map/merge/pallas_call | solution.py:213
  (6 shorter events, 0.1 us)
Async XLA Ops:
  0.0 25.3 %collective-permute-start.1 = (bf16[1600,256]{1,0:T(8,128)(2,1)}, bf16[1600,256]{1,0:T(8,128)(2,1)S(1)}, u32[]{:S(2)}, u32[]{:S(2)}) collective-permute-start(bf16[1600,256]{1,0:T(8,128)(2,1)} %bitcast.11), channel_id=1, source_target_pairs={{0,3},{1,2},{2,5},{3,0},{4,7},{5,6},{6,9},{7,4},{8,11},{9,10},{10,... | collective-permute-start | bytes 2457608 | tf_op jit(solution)/shard_map/ppermute | solution.py:237
  4.7 16.4 %copy-start = (bf16[256,1600]{0,1:T(8,128)(2,1)S(1)}, bf16[256,1600]{0,1:T(8,128)(2,1)}, u32[]{:S(2)}) copy-start(bf16[256,1600]{0,1:T(8,128)(2,1)} %param.5) | copy-start | bytes 2457604
  6.5 18.9 %copy-start.1 = (bf16[256,1600]{0,1:T(8,128)(2,1)S(1)}, bf16[256,1600]{0,1:T(8,128)(2,1)}, u32[]{:S(2)}) copy-start(bf16[256,1600]{0,1:T(8,128)(2,1)} %param.4) | copy-start | bytes 2457604
  6.5 14.6 %collective-permute-start.2 = (bf16[640,256]{1,0:T(8,128)(2,1)}, bf16[640,256]{1,0:T(8,128)(2,1)S(1)}, u32[]{:S(2)}, u32[]{:S(2)}) collective-permute-start(bf16[640,256]{1,0:T(8,128)(2,1)} %slice.24), channel_id=1, source_target_pairs={{1,5},{3,7},{5,9},{7,11},{9,13},{11,15},{13,17},{15,19},{17,21},{1... | collective-permute-start | bytes 983048 | tf_op jit(solution)/shard_map/ppermute | solution.py:238
  9.1 24.5 %collective-permute-start.3 = (bf16[960,256]{1,0:T(8,128)(2,1)}, bf16[960,256]{1,0:T(8,128)(2,1)S(1)}, u32[]{:S(2)}, u32[]{:S(2)}) collective-permute-start(bf16[960,256]{1,0:T(8,128)(2,1)} %slice.25), channel_id=1, source_target_pairs={{1,5},{3,7},{5,9},{7,11},{9,13},{11,15},{13,17},{15,19},{17,21},{1... | collective-permute-start | bytes 1474568 | tf_op jit(solution)/shard_map/ppermute | solution.py:238
  9.8 32.9 %collective-permute-start = (bf16[1600,256]{1,0:T(8,128)(2,1)}, bf16[1600,256]{1,0:T(8,128)(2,1)}, u32[]{:S(2)}, u32[]{:S(2)}) collective-permute-start(bf16[1600,256]{1,0:T(8,128)(2,1)} %bitcast.refs_0_), channel_id=1, source_target_pairs={{0,1},{1,0},{2,3},{3,2},{4,5},{5,4},{6,7},{7,6},{8,9},{9,8},{10,11... | collective-permute-start | bytes 2457608 | tf_op jit(solution)/shard_map/ppermute | solution.py:239
  21.1 21.6 %collective-permute-start.4 = (bf16[640,256]{1,0:T(8,128)(2,1)S(1)}, bf16[640,256]{1,0:T(8,128)(2,1)S(1)}, u32[]{:S(2)}, u32[]{:S(2)}) collective-permute-start(bf16[640,256]{1,0:T(8,128)(2,1)S(1)} %broadcast_select_fusion.1), channel_id=1, source_target_pairs={{0,3},{1,2},{2,5},{3,0},{4,7},{5,6},{6,9},{7,4},{8,11},{9,10},{10,... | collective-permute-start | bytes 983048 | tf_op jit(solution)/shard_map/ppermute | solution.py:241
  25.4 17.3 %collective-permute-start.5 = (bf16[640,256]{1,0:T(8,128)(2,1)S(1)}, bf16[640,256]{1,0:T(8,128)(2,1)S(1)}, u32[]{:S(2)}, u32[]{:S(2)}) collective-permute-start(bf16[640,256]{1,0:T(8,128)(2,1)S(1)} %slice_select_fusion.1), channel_id=1, source_target_pairs={{0,4},{1,5},{3,7},{4,8},{5,9},{7,11},{8,12},{9,13},{11,15},{12,16}... | collective-permute-start | bytes 983048 | tf_op jit(solution)/shard_map/ppermute | solution.py:244
  33.7 17.1 %collective-permute-start.7 = (bf16[960,256]{1,0:T(8,128)(2,1)S(1)}, bf16[960,256]{1,0:T(8,128)(2,1)S(1)}, u32[]{:S(2)}, u32[]{:S(2)}) collective-permute-start(bf16[960,256]{1,0:T(8,128)(2,1)S(1)} %slice_select_fusion), channel_id=1, source_target_pairs={{0,4},{1,5},{3,7},{4,8},{5,9},{7,11},{8,12},{9,13},{11,15},{12,16}... | collective-permute-start | bytes 1474568 | tf_op jit(solution)/shard_map/ppermute | solution.py:247
  35.7 16.8 %collective-permute-start.6 = (bf16[960,256]{1,0:T(8,128)(2,1)S(1)}, bf16[960,256]{1,0:T(8,128)(2,1)S(1)}, u32[]{:S(2)}, u32[]{:S(2)}) collective-permute-start(bf16[960,256]{1,0:T(8,128)(2,1)S(1)} %broadcast_select_fusion), channel_id=1, source_target_pairs={{0,3},{1,2},{2,5},{3,0},{4,7},{5,6},{6,9},{7,4},{8,11},{9,10},{10,... | collective-permute-start | bytes 1474568 | tf_op jit(solution)/shard_map/ppermute | solution.py:248
  47.2 18.7 %collective-permute-start.9 = (bf16[672,256]{1,0:T(8,128)(2,1)S(1)}, bf16[672,256]{1,0:T(8,128)(2,1)S(1)}, u32[]{:S(2)}, u32[]{:S(2)}) collective-permute-start(bf16[672,256]{1,0:T(8,128)(2,1)S(1)} %get-tuple-element.35), channel_id=1, source_target_pairs={{0,1},{1,0},{2,3},{3,2},{4,5},{5,4},{6,7},{7,6},{8,9},{9,8},{10,11... | collective-permute-start | bytes 1032200 | tf_op jit(solution)/shard_map/ppermute | solution.py:255
  56.9 11.1 %collective-permute-start.10 = (bf16[672,256]{1,0:T(8,128)(2,1)S(1)}, bf16[672,256]{1,0:T(8,128)(2,1)S(1)}, u32[]{:S(2)}, u32[]{:S(2)}) collective-permute-start(bf16[672,256]{1,0:T(8,128)(2,1)S(1)} %get-tuple-element.38), channel_id=1, source_target_pairs={{0,1},{1,0},{2,3},{3,2},{4,5},{5,4},{6,7},{7,6},{8,9},{9,8},{10,11... | collective-permute-start | bytes 1032200 | tf_op jit(solution)/shard_map/ppermute | solution.py:255
  63.9 7.3 %collective-permute-start.8 = (bf16[336,256]{1,0:T(8,128)(2,1)S(1)}, bf16[336,256]{1,0:T(8,128)(2,1)S(1)}, u32[]{:S(2)}, u32[]{:S(2)}) collective-permute-start(bf16[336,256]{1,0:T(8,128)(2,1)S(1)} %get-tuple-element.32), channel_id=1, source_target_pairs={{0,1},{1,0},{2,3},{3,2},{4,5},{5,4},{6,7},{7,6},{8,9},{9,8},{10,11... | collective-permute-start | bytes 516104 | tf_op jit(solution)/shard_map/ppermute | solution.py:255

commit v5 on v3

--- a/solution.py
+++ b/solution.py
@@ -94,16 +94,16 @@
 
         def unit_x(g):
             def score():
-                key = jnp.where(is0, y3[here(g)], r1[there(g)])
+                key = jnp.where(is0, r3[here(g)], r1[here(g)])
                 return scores(key, jnp.concatenate([q_own[there(g)], q_mate[there(g)]], axis=1))
 
-            return unit(score, lambda: r3[here(g)], ok_x)
+            return unit(score, lambda: jnp.where(is0, y3[here(g)], r3[here(g)]), ok_x)
 
         def unit_z(g):
             def score():
-                return scores(jnp.where(even, k_own[there(g)], y3[here(g)]), q_mate[there(g)])
-
-            return unit(score, lambda: jnp.where(even, v_own[there(g)], y1[here(g)]), ok_z)
+                return scores(jnp.where(even, k_own[there(g)], y1[here(g)]), q_mate[there(g)])
+
+            return unit(score, lambda: jnp.where(even, v_own[there(g)], y3[here(g)]), ok_z)
 
         def unit_d(g):
             def score():
@@ -165,7 +165,7 @@
             jax.ShapeDtypeStruct((groups, 8, rows), jnp.float32),
             jax.ShapeDtypeStruct((groups * MSG, rows), jnp.bfloat16),
         ],
-        compiler_params=pltpu.CompilerParams(vmem_limit_bytes=12 * 2**20),
+        compiler_params=pltpu.CompilerParams(vmem_limit_bytes=24 * 2**20),
         cost_estimate=pl.CostEstimate(
             flops=heads * 4 * 4 * 4 * rows * rows * WIDTH,
             bytes_accessed=heads * WIDTH * rows * 24,
@@ -200,7 +200,7 @@
         in_specs=[VMEM] * (3 + len(before)),
         out_specs=VMEM,
         out_shape=jax.ShapeDtypeStruct((done + size, rows), jnp.bfloat16),
-        compiler_params=pltpu.CompilerParams(vmem_limit_bytes=12 * 2**20),
+        compiler_params=pltpu.CompilerParams(vmem_limit_bytes=24 * 2**20),
         cost_estimate=pl.CostEstimate(flops=size * rows * 4, bytes_accessed=size * rows * 8, transcendentals=0),
         name="merge",
     )(part, part_lse, msg, *before)
@@ -219,19 +219,17 @@
 
     cut = HALVES[0] * STEP
     k1, k2, v1, v2 = k[:cut], k[cut:], v[:cut], v[cut:]
-    r1 = lax.ppermute(k, "seq", to_x)
-    y1, y2 = lax.ppermute(v1, "seq", to_y), lax.ppermute(v2, "seq", to_y)
+
+    r1, y1 = lax.ppermute(jnp.where(column == 3, v1, k1), "seq", to_x), lax.ppermute(k1, "seq", to_y)
+    r2, y2 = lax.ppermute(jnp.where(column == 3, v2, k2), "seq", to_x), lax.ppermute(k2, "seq", to_y)
     q_mate = lax.ppermute(q, "seq", swap)
-    send = jnp.where(column == 3, y1, v1)
-    r3 = lax.ppermute(send, "seq", to_x)
-    r1 = lax.optimization_barrier((r1, send))[0]
-    send = jnp.where(column == 0, r1[:cut], k1)
-    y3 = lax.ppermute(send, "seq", to_y0)
-    r1, y2 = lax.optimization_barrier((r1, y2, send))[:2]
-    send = jnp.where(column == 0, r1[cut:], k2)
-    y4 = lax.ppermute(send, "seq", to_y0)
-    r4 = lax.ppermute(jnp.where(column == 3, y2, v2), "seq", to_x)
-    halves, arguments = ((r1, r3, y1, y3), (r1, r4, y2, y4)), (q, k, v)
+    to_send = jnp.where(column == 3, y1, v1), jnp.where(column == 0, r1, v1)
+    y1, r1 = lax.optimization_barrier((y1, r1))
+    r3, y3 = lax.ppermute(to_send[0], "seq", to_x), lax.ppermute(to_send[1], "seq", to_y0)
+    r2, y2 = lax.optimization_barrier((r2, y2, *to_send))[:2]
+    to_send = jnp.where(column == 3, y2, v2), jnp.where(column == 0, r2, v2)
+    r4, y4 = lax.ppermute(to_send[0], "seq", to_x), lax.ppermute(to_send[1], "seq", to_y0)
+    halves, arguments = ((r1, r3, y1, y3), (r2, r4, y2, y4)), (q, k, v)
     results, first = [], 0
     for groups in CHUNKS:
         half = int(first >= HALVES[0])

time: 73.5 us -> 71.1 us (0.967)
  the two profiles are of different devices: /device:TPU:248 before, /device:TPU:256 now
where the time goes in v5:
time: 71.1 us; the launch traced here: 70.5 us
  starting transfers between devices  48.3 us (68%)
  Pallas kernels  11 us (15%)
  waiting for transfers between devices  5.67 us (8%)
  other arithmetic  5.22 us (7%)
    ppermute x3, starting transfers between devices, shards(): results.append((part, lse, lax.ppermute(msg, 'seq', swap)))  15.3 us
    ppermute x2, starting transfers between devices, shards(): lax.ppermute(to_send[0], 'seq', to_x)  10 us
    pallas_call x3, Pallas kernels, attend(): pl.pallas_call(lambda *refs: attend_kernel(first, skip, *refs), in_specs=...  9.74 us
    ppermute x1, starting transfers between devices, shards(): lax.ppermute(jnp.where(column == 3, v2, k2), 'seq', to_x)  7.28 us
    ppermute x2, starting transfers between devices, shards(): lax.ppermute(to_send[1], 'seq', to_y0)  6.97 us
    ppermute x3, waiting for transfers between devices, shards(): results.append((part, lse, lax.ppermute(msg, 'seq', swap)))  5.08 us
    ppermute x1, starting transfers between devices, shards(): lax.ppermute(jnp.where(column == 3, v1, k1), 'seq', to_x)  4.66 us
    select_n x1, other arithmetic, shards(): jnp.where(column == 3, v1, k1)  2.05 us
  transfers between devices with their start and end apart: 12, of which 3 were waited for; matrix products, arithmetic and copies ran while one was open for 4% of the time, Pallas kernels for 14%

profile of v5, /device:TPU:256, one launch (start us, length us, event | category | flops | bytes accessed | tf_op | source)
XLA Modules:
  0.0 70.5 jit_solution(10824016742649856660)
XLA Ops:
  0.0 2.1 %broadcast_select_fusion.5 = (bf16[640,256]{1,0:T(8,128)(2,1)}, bf16[640,256]{1,0:T(8,128)(2,1)}) fusion(pred[]{:T(512)S(6)} %eq.6, bf16[1600,256]{1,0:T(8,128)(2,1)} %bitcast.4, bf16[1600,256]{1,0:T(8,128)(2,1)} %bitcast.11), kind=kLoop, calls=%fused_computation.5 | loop fusion | flops 163840 | bytes 1310721 | tf_op jit(solution)/shard_map/jit(_where)/select_n | solution.py:223
  2.1 4.7 %collective-permute-start.2 = (bf16[640,256]{1,0:T(8,128)(2,1)}, bf16[640,256]{1,0:T(8,128)(2,1)}, u32[]{:S(2)}, u32[]{:S(2)}) collective-permute-start(bf16[640,256]{1,0:T(8,128)(2,1)} %get-tuple-element.47), channel_id=1, source_target_pairs={{0,3},{1,2},{2,5},{3,0},{4,7},{5,6},{6,9},{7,4},{8,11},{9,10},{10,... | collective-permute-start | bytes 983048 | tf_op jit(solution)/shard_map/ppermute | solution.py:223
  6.7 0.0 copy-start.2
  6.7 1.5 %collective-permute-start.1 = (bf16[640,256]{1,0:T(8,128)(2,1)}, bf16[640,256]{1,0:T(8,128)(2,1)}, u32[]{:S(2)}, u32[]{:S(2)}) collective-permute-start(bf16[640,256]{1,0:T(8,128)(2,1)} %get-tuple-element.48), channel_id=1, source_target_pairs={{1,5},{3,7},{5,9},{7,11},{9,13},{11,15},{13,17},{15,19},{17,21},{1... | collective-permute-start | bytes 983048 | tf_op jit(solution)/shard_map/ppermute | solution.py:223
  8.3 2.0 %fusion = (bf16[960,256]{1,0:T(8,128)(2,1)}, bf16[960,256]{1,0:T(8,128)(2,1)}) fusion(bf16[1600,256]{1,0:T(8,128)(2,1)} %bitcast.12, bf16[1600,256]{1,0:T(8,128)(2,1)S(1)} %bitcast.5, pred[]{:T(512)S(6)} %eq.6), kind=kLoop, calls=%fused_computation.6 | loop fusion | flops 245760 | bytes 1966081 | tf_op jit(solution)/shard_map/slice | solution.py:221
  10.3 0.7 collective-permute-start.6
  11.0 7.3 %collective-permute-start.5 = (bf16[960,256]{1,0:T(8,128)(2,1)}, bf16[960,256]{1,0:T(8,128)(2,1)S(1)}, u32[]{:S(2)}, u32[]{:S(2)}) collective-permute-start(bf16[960,256]{1,0:T(8,128)(2,1)} %get-tuple-element.44), channel_id=1, source_target_pairs={{0,3},{1,2},{2,5},{3,0},{4,7},{5,6},{6,9},{7,4},{8,11},{9,10},{10,... | collective-permute-start | bytes 1474568 | tf_op jit(solution)/shard_map/ppermute | solution.py:224
  18.3 1.9 %collective-permute-start = (bf16[1600,256]{1,0:T(8,128)(2,1)S(1)}, bf16[1600,256]{1,0:T(8,128)(2,1)S(1)}, u32[]{:S(2)}, u32[]{:S(2)}) collective-permute-start(bf16[1600,256]{1,0:T(8,128)(2,1)S(1)} %bitcast.16), channel_id=1, source_target_pairs={{0,1},{1,0},{2,3},{3,2},{4,5},{5,4},{6,7},{7,6},{8,9},{9,8},{10,11... | collective-permute-start | bytes 2457608 | tf_op jit(solution)/shard_map/ppermute | solution.py:225
  20.2 0.0 collective-permute-done.1.refs_6_
  20.3 1.0 %broadcast_select_fusion.3 = (bf16[640,256]{1,0:T(8,128)(2,1)S(1)}, bf16[640,256]{1,0:T(8,128)(2,1)S(1)}) fusion(bf16[640,256]{1,0:T(8,128)(2,1)} %collective-permute-done.2.refs_4_, pred[]{:T(512)S(6)} %eq.7, bf16[1600,256]{1,0:T(8,128)(2,1)S(1)} %bitcast.6, bf16[640,256]{1,0:T(8,128)(2,1)} %collective-permute-done.1.refs_6_, pred[]{:T(512)S(6)} %eq.6), kind=kLoop, calls=%fused_computation.3 | loop fusion | flops 327680 | bytes 1638402 | tf_op jit(solution)/shard_map/jit(_where)/select_n | solution.py:226
  21.3 3.5 %collective-permute-start.4 = (bf16[640,256]{1,0:T(8,128)(2,1)S(1)}, bf16[640,256]{1,0:T(8,128)(2,1)S(1)}, u32[]{:S(2)}, u32[]{:S(2)}) collective-permute-start(bf16[640,256]{1,0:T(8,128)(2,1)S(1)} %get-tuple-element.45), channel_id=1, source_target_pairs={{0,4},{1,5},{3,7},{4,8},{5,9},{7,11},{8,12},{9,13},{11,15},{12,16}... | collective-permute-start | bytes 983048 | tf_op jit(solution)/shard_map/ppermute | solution.py:228
  24.8 0.0 copy-start.1
  24.8 5.0 %collective-permute-start.3 = (bf16[640,256]{1,0:T(8,128)(2,1)S(1)}, bf16[640,256]{1,0:T(8,128)(2,1)S(1)}, u32[]{:S(2)}, u32[]{:S(2)}) collective-permute-start(bf16[640,256]{1,0:T(8,128)(2,1)S(1)} %get-tuple-element.46), channel_id=1, source_target_pairs={{0,3},{1,2},{2,5},{3,0},{4,7},{5,6},{6,9},{7,4},{8,11},{9,10},{10,... | collective-permute-start | bytes 983048 | tf_op jit(solution)/shard_map/ppermute | solution.py:228
  29.8 0.0 collective-permute-done.6.refs_6_
  29.8 0.0 collective-permute-done.5.refs_4_
  29.8 0.1 broadcast_select_fusion
  29.9 3.5 %collective-permute-start.8 = (bf16[960,256]{1,0:T(8,128)(2,1)S(1)}, bf16[960,256]{1,0:T(8,128)(2,1)S(1)}, u32[]{:S(2)}, u32[]{:S(2)}) collective-permute-start(bf16[960,256]{1,0:T(8,128)(2,1)S(1)} %get-tuple-element.41), channel_id=1, source_target_pairs={{0,4},{1,5},{3,7},{4,8},{5,9},{7,11},{8,12},{9,13},{11,15},{12,16}... | collective-permute-start | bytes 1474568 | tf_op jit(solution)/shard_map/ppermute | solution.py:231
  33.4 5.1 %collective-permute-start.7 = (bf16[960,256]{1,0:T(8,128)(2,1)S(1)}, bf16[960,256]{1,0:T(8,128)(2,1)S(1)}, u32[]{:S(2)}, u32[]{:S(2)}) collective-permute-start(bf16[960,256]{1,0:T(8,128)(2,1)S(1)} %get-tuple-element.42), channel_id=1, source_target_pairs={{0,3},{1,2},{2,5},{3,0},{4,7},{5,6},{6,9},{7,4},{8,11},{9,10},{10,... | collective-permute-start | bytes 1474568 | tf_op jit(solution)/shard_map/ppermute | solution.py:231
  38.5 0.0 collective-permute-done.3.refs_5_
  38.5 0.6 collective-permute-done.refs_1_
  39.1 4.5 %attend.3 = (f32[640,256]{1,0:T(8,128)S(1)}, f32[2,8,256]{2,1,0:T(8,128)S(1)}, bf16[672,256]{1,0:T(8,128)(2,1)S(1)}) custom-call(bf16[1600,256]{1,0:T(8,128)(2,1)S(1)} %bitcast.17, bf16[1600,256]{1,0:T(8,128)(2,1)S(1)} %collective-permute-done.refs_1_, bf16[1600,256]{1,0:T(8,128)(2,1)S(1)} %bitcast.13, bf16[1600,256]{1,0:T(8,128)(2,1)S(1)} %bitcast.8, ...), custom_call_target="tpu_custom_call" | custom-call | flops 2684354560 | bytes 3932160 | tf_op jit(solution)/shard_map/attend/pallas_call | solution.py:159
  43.6 5.0 %collective-permute-start.10 = (bf16[672,256]{1,0:T(8,128)(2,1)S(1)}, bf16[672,256]{1,0:T(8,128)(2,1)S(1)}, u32[]{:S(2)}, u32[]{:S(2)}) collective-permute-start(bf16[672,256]{1,0:T(8,128)(2,1)S(1)} %get-tuple-element.37), channel_id=1, source_target_pairs={{0,1},{1,0},{2,3},{3,2},{4,5},{5,4},{6,7},{7,6},{8,9},{9,8},{10,11... | collective-permute-start | bytes 1032200 | tf_op jit(solution)/shard_map/ppermute | solution.py:238
  48.6 3.5 %attend.4 = (f32[640,256]{1,0:T(8,128)S(1)}, f32[2,8,256]{2,1,0:T(8,128)S(1)}, bf16[672,256]{1,0:T(8,128)(2,1)S(1)}) custom-call(bf16[1600,256]{1,0:T(8,128)(2,1)S(1)} %bitcast.18, bf16[1600,256]{1,0:T(8,128)(2,1)S(1)} %collective-permute-done.refs_1_, bf16[1600,256]{1,0:T(8,128)(2,1)S(1)} %bitcast.14, bf16[1600,256]{1,0:T(8,128)(2,1)S(1)} %bitcast.9, ...), custom_call_target="tpu_custom_call" | custom-call | flops 2684354560 | bytes 3932160 | tf_op jit(solution)/shard_map/attend/pallas_call | solution.py:159
  52.1 8.3 %collective-permute-start.11 = (bf16[672,256]{1,0:T(8,128)(2,1)S(1)}, bf16[672,256]{1,0:T(8,128)(2,1)S(1)}, u32[]{:S(2)}, u32[]{:S(2)}) collective-permute-start(bf16[672,256]{1,0:T(8,128)(2,1)S(1)} %get-tuple-element.40), channel_id=1, source_target_pairs={{0,1},{1,0},{2,3},{3,2},{4,5},{5,4},{6,7},{7,6},{8,9},{9,8},{10,11... | collective-permute-start | bytes 1032200 | tf_op jit(solution)/shard_map/ppermute | solution.py:238
  60.5 1.8 %attend.5 = (f32[320,256]{1,0:T(8,128)S(1)}, f32[1,8,256]{2,1,0:T(8,128)S(1)}, bf16[336,256]{1,0:T(8,128)(2,1)S(1)}) custom-call(bf16[1600,256]{1,0:T(8,128)(2,1)S(1)} %bitcast.19, bf16[1600,256]{1,0:T(8,128)(2,1)S(1)} %collective-permute-done.refs_1_, bf16[1600,256]{1,0:T(8,128)(2,1)S(1)} %bitcast.15, bf16[1600,256]{1,0:T(8,128)(2,1)S(1)} %bitcast.10, ...), custom_call_target="tpu_custom_call" | custom-call | flops 1342177280 | bytes 1966080 | tf_op jit(solution)/shard_map/attend/pallas_call | solution.py:159
  62.2 1.9 %collective-permute-start.9 = (bf16[336,256]{1,0:T(8,128)(2,1)S(1)}, bf16[336,256]{1,0:T(8,128)(2,1)S(1)}, u32[]{:S(2)}, u32[]{:S(2)}) collective-permute-start(bf16[336,256]{1,0:T(8,128)(2,1)S(1)} %get-tuple-element.34), channel_id=1, source_target_pairs={{0,1},{1,0},{2,3},{3,2},{4,5},{5,4},{6,7},{7,6},{8,9},{9,8},{10,11... | collective-permute-start | bytes 516104 | tf_op jit(solution)/shard_map/ppermute | solution.py:238
  64.1 0.0 collective-permute-done.10.msg
  64.2 0.1 merge.3.rest_0_
  64.3 3.2 %collective-permute-done.11.msg = bf16[672,256]{1,0:T(8,128)(2,1)S(1)} collective-permute-done((bf16[672,256]{1,0:T(8,128)(2,1)S(1)}, bf16[672,256]{1,0:T(8,128)(2,1)S(1)}, u32[]{:S(2)}, u32[]{:S(2)}) %collective-permute-start.11) | collective-permute-done | bytes 344096 | tf_op jit(solution)/shard_map/ppermute | solution.py:238
  67.4 0.1 merge.4.rest_1_
  67.6 1.9 %collective-permute-done.9.msg = bf16[336,256]{1,0:T(8,128)(2,1)S(1)} collective-permute-done((bf16[336,256]{1,0:T(8,128)(2,1)S(1)}, bf16[336,256]{1,0:T(8,128)(2,1)S(1)}, u32[]{:S(2)}, u32[]{:S(2)}) %collective-permute-start.9) | collective-permute-done | bytes 172064 | tf_op jit(solution)/shard_map/ppermute | solution.py:238
  69.5 1.0 %merge.5 = bf16[1600,256]{1,0:T(8,128)(2,1)} custom-call(f32[320,256]{1,0:T(8,128)S(1)} %get-tuple-element.31.part, f32[1,8,256]{2,1,0:T(8,128)S(1)} %get-tuple-element.32.part_lse, bf16[336,256]{1,0:T(8,128)(2,1)S(1)} %collective-permute-done.9.msg, bf16[640,256]{1,0:T(8,128)(2,1)S(1)} %merge.3.rest_0_, bf16[640,256]{1,0:T(8,128)(2,1)S(1)} %merge.4.rest_1_), custom_call_target="tpu_custom_call" | custom-call | flops 327680 | bytes 655360 | tf_op jit(solution)/shard_map/merge/pallas_call | solution.py:198
  (8 shorter events, 0.0 us)
Async XLA Ops:
  0.0 8.3 %copy-start = (bf16[256,1600]{0,1:T(8,128)(2,1)S(1)}, bf16[256,1600]{0,1:T(8,128)(2,1)}, u32[]{:S(2)}) copy-start(bf16[256,1600]{0,1:T(8,128)(2,1)} %param.5) | copy-start | bytes 2457604
  2.1 18.2 %collective-permute-start.2 = (bf16[640,256]{1,0:T(8,128)(2,1)}, bf16[640,256]{1,0:T(8,128)(2,1)}, u32[]{:S(2)}, u32[]{:S(2)}) collective-permute-start(bf16[640,256]{1,0:T(8,128)(2,1)} %get-tuple-element.47), channel_id=1, source_target_pairs={{0,3},{1,2},{2,5},{3,0},{4,7},{5,6},{6,9},{7,4},{8,11},{9,10},{10,... | collective-permute-start | bytes 983048 | tf_op jit(solution)/shard_map/ppermute | solution.py:223
  6.7 11.6 %copy-start.2 = (bf16[256,1600]{0,1:T(8,128)(2,1)S(1)}, bf16[256,1600]{0,1:T(8,128)(2,1)}, u32[]{:S(2)}) copy-start(bf16[256,1600]{0,1:T(8,128)(2,1)} %param.3) | copy-start | bytes 2457604
  6.7 13.5 %collective-permute-start.1 = (bf16[640,256]{1,0:T(8,128)(2,1)}, bf16[640,256]{1,0:T(8,128)(2,1)}, u32[]{:S(2)}, u32[]{:S(2)}) collective-permute-start(bf16[640,256]{1,0:T(8,128)(2,1)} %get-tuple-element.48), channel_id=1, source_target_pairs={{1,5},{3,7},{5,9},{7,11},{9,13},{11,15},{13,17},{15,19},{17,21},{1... | collective-permute-start | bytes 983048 | tf_op jit(solution)/shard_map/ppermute | solution.py:223
  10.3 19.5 %collective-permute-start.6 = (bf16[960,256]{1,0:T(8,128)(2,1)}, bf16[960,256]{1,0:T(8,128)(2,1)S(1)}, u32[]{:S(2)}, u32[]{:S(2)}) collective-permute-start(bf16[960,256]{1,0:T(8,128)(2,1)} %get-tuple-element.43), channel_id=1, source_target_pairs={{1,5},{3,7},{5,9},{7,11},{9,13},{11,15},{13,17},{15,19},{17,21},{1... | collective-permute-start | bytes 1474568 | tf_op jit(solution)/shard_map/ppermute | solution.py:224
  11.0 18.8 %collective-permute-start.5 = (bf16[960,256]{1,0:T(8,128)(2,1)}, bf16[960,256]{1,0:T(8,128)(2,1)S(1)}, u32[]{:S(2)}, u32[]{:S(2)}) collective-permute-start(bf16[960,256]{1,0:T(8,128)(2,1)} %get-tuple-element.44), channel_id=1, source_target_pairs={{0,3},{1,2},{2,5},{3,0},{4,7},{5,6},{6,9},{7,4},{8,11},{9,10},{10,... | collective-permute-start | bytes 1474568 | tf_op jit(solution)/shard_map/ppermute | solution.py:224
  18.3 20.8 %collective-permute-start = (bf16[1600,256]{1,0:T(8,128)(2,1)S(1)}, bf16[1600,256]{1,0:T(8,128)(2,1)S(1)}, u32[]{:S(2)}, u32[]{:S(2)}) collective-permute-start(bf16[1600,256]{1,0:T(8,128)(2,1)S(1)} %bitcast.16), channel_id=1, source_target_pairs={{0,1},{1,0},{2,3},{3,2},{4,5},{5,4},{6,7},{7,6},{8,9},{9,8},{10,11... | collective-permute-start | bytes 2457608 | tf_op jit(solution)/shard_map/ppermute | solution.py:225
  21.3 17.2 %collective-permute-start.4 = (bf16[640,256]{1,0:T(8,128)(2,1)S(1)}, bf16[640,256]{1,0:T(8,128)(2,1)S(1)}, u32[]{:S(2)}, u32[]{:S(2)}) collective-permute-start(bf16[640,256]{1,0:T(8,128)(2,1)S(1)} %get-tuple-element.45), channel_id=1, source_target_pairs={{0,4},{1,5},{3,7},{4,8},{5,9},{7,11},{8,12},{9,13},{11,15},{12,16}... | collective-permute-start | bytes 983048 | tf_op jit(solution)/shard_map/ppermute | solution.py:228
  24.8 14.3 %copy-start.1 = (bf16[256,1600]{0,1:T(8,128)(2,1)S(1)}, bf16[256,1600]{0,1:T(8,128)(2,1)}, u32[]{:S(2)}) copy-start(bf16[256,1600]{0,1:T(8,128)(2,1)} %param.4) | copy-start | bytes 2457604
  24.8 13.7 %collective-permute-start.3 = (bf16[640,256]{1,0:T(8,128)(2,1)S(1)}, bf16[640,256]{1,0:T(8,128)(2,1)S(1)}, u32[]{:S(2)}, u32[]{:S(2)}) collective-permute-start(bf16[640,256]{1,0:T(8,128)(2,1)S(1)} %get-tuple-element.46), channel_id=1, source_target_pairs={{0,3},{1,2},{2,5},{3,0},{4,7},{5,6},{6,9},{7,4},{8,11},{9,10},{10,... | collective-permute-start | bytes 983048 | tf_op jit(solution)/shard_map/ppermute | solution.py:228
  29.9 18.7 %collective-permute-start.8 = (bf16[960,256]{1,0:T(8,128)(2,1)S(1)}, bf16[960,256]{1,0:T(8,128)(2,1)S(1)}, u32[]{:S(2)}, u32[]{:S(2)}) collective-permute-start(bf16[960,256]{1,0:T(8,128)(2,1)S(1)} %get-tuple-element.41), channel_id=1, source_target_pairs={{0,4},{1,5},{3,7},{4,8},{5,9},{7,11},{8,12},{9,13},{11,15},{12,16}... | collective-permute-start | bytes 1474568 | tf_op jit(solution)/shard_map/ppermute | solution.py:231
  33.4 15.2 %collective-permute-start.7 = (bf16[960,256]{1,0:T(8,128)(2,1)S(1)}, bf16[960,256]{1,0:T(8,128)(2,1)S(1)}, u32[]{:S(2)}, u32[]{:S(2)}) collective-permute-start(bf16[960,256]{1,0:T(8,128)(2,1)S(1)} %get-tuple-element.42), channel_id=1, source_target_pairs={{0,3},{1,2},{2,5},{3,0},{4,7},{5,6},{6,9},{7,4},{8,11},{9,10},{10,... | collective-permute-start | bytes 1474568 | tf_op jit(solution)/shard_map/ppermute | solution.py:231
  43.6 20.6 %collective-permute-start.10 = (bf16[672,256]{1,0:T(8,128)(2,1)S(1)}, bf16[672,256]{1,0:T(8,128)(2,1)S(1)}, u32[]{:S(2)}, u32[]{:S(2)}) collective-permute-start(bf16[672,256]{1,0:T(8,128)(2,1)S(1)} %get-tuple-element.37), channel_id=1, source_target_pairs={{0,1},{1,0},{2,3},{3,2},{4,5},{5,4},{6,7},{7,6},{8,9},{9,8},{10,11... | collective-permute-start | bytes 1032200 | tf_op jit(solution)/shard_map/ppermute | solution.py:238
  52.1 15.3 %collective-permute-start.11 = (bf16[672,256]{1,0:T(8,128)(2,1)S(1)}, bf16[672,256]{1,0:T(8,128)(2,1)S(1)}, u32[]{:S(2)}, u32[]{:S(2)}) collective-permute-start(bf16[672,256]{1,0:T(8,128)(2,1)S(1)} %get-tuple-element.40), channel_id=1, source_target_pairs={{0,1},{1,0},{2,3},{3,2},{4,5},{5,4},{6,7},{7,6},{8,9},{9,8},{10,11... | collective-permute-start | bytes 1032200 | tf_op jit(solution)/shard_map/ppermute | solution.py:238
  62.2 7.3 %collective-permute-start.9 = (bf16[336,256]{1,0:T(8,128)(2,1)S(1)}, bf16[336,256]{1,0:T(8,128)(2,1)S(1)}, u32[]{:S(2)}, u32[]{:S(2)}) collective-permute-start(bf16[336,256]{1,0:T(8,128)(2,1)S(1)} %get-tuple-element.34), channel_id=1, source_target_pairs={{0,1},{1,0},{2,3},{3,2},{4,5},{5,4},{6,7},{7,6},{8,9},{9,8},{10,11... | collective-permute-start | bytes 516104 | tf_op jit(solution)/shard_map/ppermute | solution.py:238

commit v6 on v5

--- a/solution.py
+++ b/solution.py
@@ -61,11 +61,11 @@
     return acc_a * (factor_a / total) + acc_b * (factor_b / total), top + jnp.log2(total)
 
 
-def attend_kernel(first, skip, q_own, q_mate, k_own, v_own, r1, r3, y1, y3, part, part_lse, msg):
+def attend_kernel(for_mate, first, skip, query, k_own, v_own, r1, r3, y1, y3, out, *out_lse):
     position = lax.axis_index("seq")
     even, is0 = position % 2 == 0, position % 4 == 0
     ok_x, ok_z = (position >= 3) | (even & (position >= 1)), even | (position >= 4)
-    rows = q_own.shape[1]
+    rows = query.shape[1]
     half = rows // 2
     later = lax.broadcasted_iota(jnp.int32, (half, half), 0) > lax.broadcasted_iota(jnp.int32, (half, half), 1)
 
@@ -95,19 +95,19 @@
         def unit_x(g):
             def score():
                 key = jnp.where(is0, r3[here(g)], r1[here(g)])
-                return scores(key, jnp.concatenate([q_own[there(g)], q_mate[there(g)]], axis=1))
+                return scores(key, query[there(g)])
 
             return unit(score, lambda: jnp.where(is0, y3[here(g)], r3[here(g)]), ok_x)
 
         def unit_z(g):
             def score():
-                return scores(jnp.where(even, k_own[there(g)], y1[here(g)]), q_mate[there(g)])
+                return scores(jnp.where(even, k_own[there(g)], y1[here(g)]), query[there(g)])
 
             return unit(score, lambda: jnp.where(even, v_own[there(g)], y3[here(g)]), ok_z)
 
         def unit_d(g):
             def score():
-                q, k = q_own[there(g)], k_own[there(g)]
+                q, k = query[there(g)], k_own[there(g)]
                 return scores(k[:, :half], q), scores(k[:, half:], q[:, half:])
 
             def top(score):
@@ -129,50 +129,50 @@
 
             return score, top, weight, product
 
-        done = pipelined([u(g) for g in range(GROUP) for u in (unit_x, unit_z, unit_d)])
-        own, mate = [], []
+        done = pipelined([u(g) for g in range(GROUP) for u in (unit_x, unit_z if for_mate else unit_d)])
+        mixed = [mix(done[2 * g + 1][3], done[2 * g][3]) for g in range(GROUP)]
+        if not for_mate:
+            for g in range(GROUP):
+                out[rows_at(i, g)] = mixed[g][0]
+            out_lse[0][i] = stack_rows([lse for _, lse in mixed], 8)
+            return carry
         for g in range(GROUP):
-            x, z, d = [done[3 * g + j][3] for j in range(3)]
-            own.append(mix(d, [e[:, :rows] for e in x]))
-            mate.append(mix(z, [e[:, rows:] for e in x]))
-        for g in range(GROUP):
-            part[rows_at(i, g)] = own[g][0]
-            msg[rows_at(i, g, MSG)] = mate[g][0].astype(jnp.bfloat16)
-        part_lse[i] = stack_rows([lse for _, lse in own], 8)
-        stat = jnp.concatenate([lse for _, lse in mate], axis=0)
+            out[rows_at(i, g, MSG)] = mixed[g][0].astype(jnp.bfloat16)
+        stat = jnp.concatenate([lse for _, lse in mixed], axis=0)
         high = stat.astype(jnp.bfloat16).astype(jnp.float32)
         mid = (stat - high).astype(jnp.bfloat16).astype(jnp.float32)
         stat = stack_rows([high, mid, stat - high - mid, jnp.zeros((1, rows), jnp.float32)], 4)
-        msg[pl.ds(pl.multiple_of(i * MSG + STEP, 16), STAT)] = stat.astype(jnp.bfloat16)
+        out[pl.ds(pl.multiple_of(i * MSG + STEP, 16), STAT)] = stat.astype(jnp.bfloat16)
         return carry
 
-    lax.fori_loop(0, part_lse.shape[0], one_group, 0)
+    lax.fori_loop(0, out.shape[0] // (MSG if for_mate else STEP), one_group, 0)
 
 
 VMEM = pl.BlockSpec(memory_space=pltpu.VMEM)
 
 
-def attend(arguments, q_mate, came, first, skip, groups):
-    rows = q_mate.shape[1]
+def attend(for_mate, query, k, v, came, first, skip, groups):
+    rows = query.shape[1]
     size, heads = groups * STEP, groups * GROUP
-    q, k, v = arguments
+    shapes = [
+        jax.ShapeDtypeStruct((size, rows), jnp.float32),
+        jax.ShapeDtypeStruct((groups, 8, rows), jnp.float32),
+    ]
+    if for_mate:
+        shapes = [jax.ShapeDtypeStruct((groups * MSG, rows), jnp.bfloat16)]
     return pl.pallas_call(
-        lambda *refs: attend_kernel(first, skip, *refs),
-        in_specs=[VMEM] * 8,
-        out_specs=[VMEM] * 3,
-        out_shape=[
-            jax.ShapeDtypeStruct((size, rows), jnp.float32),
-            jax.ShapeDtypeStruct((groups, 8, rows), jnp.float32),
-            jax.ShapeDtypeStruct((groups * MSG, rows), jnp.bfloat16),
-        ],
+        lambda *refs: attend_kernel(for_mate, first, skip, *refs),
+        in_specs=[VMEM] * 7,
+        out_specs=[VMEM] * len(shapes),
+        out_shape=shapes,
         compiler_params=pltpu.CompilerParams(vmem_limit_bytes=24 * 2**20),
         cost_estimate=pl.CostEstimate(
-            flops=heads * 4 * 4 * 4 * rows * rows * WIDTH,
-            bytes_accessed=heads * WIDTH * rows * 24,
-            transcendentals=heads * 4 * rows * rows,
+            flops=heads * 6 * 2 * 4 * rows * rows * WIDTH,
+            bytes_accessed=heads * WIDTH * rows * 12,
+            transcendentals=heads * 2 * rows * rows,
         ),
-        name="attend",
-    )(q, q_mate, k, v, *came)
+        name="mate" if for_mate else "own",
+    )(query, k, v, *came)
 
 
 def merge_kernel(part, part_lse, msg, *rest):
@@ -229,13 +229,14 @@
     r2, y2 = lax.optimization_barrier((r2, y2, *to_send))[:2]
     to_send = jnp.where(column == 3, y2, v2), jnp.where(column == 0, r2, v2)
     r4, y4 = lax.ppermute(to_send[0], "seq", to_x), lax.ppermute(to_send[1], "seq", to_y0)
-    halves, arguments = ((r1, r3, y1, y3), (r2, r4, y2, y4)), (q, k, v)
+    halves = (r1, r3, y1, y3), (r2, r4, y2, y4)
     results, first = [], 0
     for groups in CHUNKS:
         half = int(first >= HALVES[0])
-        part, lse, msg = attend(arguments, q_mate, halves[half], first, first - half * HALVES[0], groups)
-        q_mate, msg = lax.optimization_barrier((q_mate, msg))
-        results.append((part, lse, lax.ppermute(msg, "seq", swap)))
+        place = halves[half], first, first - half * HALVES[0], groups
+        (msg,) = attend(True, q_mate, k, v, *place)
+        q_mate, q, msg = lax.optimization_barrier((q_mate, q, msg))
+        results.append((*attend(False, q, k, v, *place), lax.ppermute(msg, "seq", swap)))
         first += groups
     before = [merge(*result) for result in results[:-1]]
     return merge(*results[-1], *before).T

time: 71.1 us -> 69.9 us (0.983)
  the two profiles are of different devices: /device:TPU:256 before, /device:TPU:248 now
where the time goes in v6:
time: 69.9 us; the launch traced here: 69.4 us
  starting transfers between devices  46.8 us (67%)
  Pallas kernels  14.9 us (21%)
  other arithmetic  5.22 us (7%)
  waiting for transfers between devices  2.21 us (3%)
    ppermute x2, starting transfers between devices, shards(): lax.ppermute(to_send[0], 'seq', to_x)  14.3 us
    pallas_call x6, Pallas kernels, attend(): pl.pallas_call(lambda *refs: attend_kernel(for_mate, first, skip, *refs),...  13.6 us
    ppermute x1, starting transfers between devices, shards(): lax.ppermute(jnp.where(column == 3, v2, k2), 'seq', to_x)  10.7 us
    ppermute x3, starting transfers between devices, shards(): lax.ppermute(msg, 'seq', swap)  7.77 us
    ppermute x2, starting transfers between devices, shards(): lax.ppermute(to_send[1], 'seq', to_y0)  5.18 us
    ppermute x1, starting transfers between devices, shards(): lax.ppermute(jnp.where(column == 3, v1, k1), 'seq', to_x)  4.66 us
    ppermute x3, waiting for transfers between devices, shards(): lax.ppermute(msg, 'seq', swap)  2.19 us
    select_n x1, other arithmetic, shards(): jnp.where(column == 3, v1, k1)  2.05 us
  transfers between devices with their start and end apart: 12, of which 2 were waited for; matrix products, arithmetic and copies ran while one was open for 5% of the time, Pallas kernels for 20%

profile of v6, /device:TPU:248, one launch (start us, length us, event | category | flops | bytes accessed | tf_op | source)
XLA Modules:
  0.0 69.4 jit_solution(6693542441093236570)
XLA Ops:
  0.0 2.1 %broadcast_select_fusion.5 = (bf16[640,256]{1,0:T(8,128)(2,1)}, bf16[640,256]{1,0:T(8,128)(2,1)}) fusion(pred[]{:T(512)S(6)} %eq.6, bf16[1600,256]{1,0:T(8,128)(2,1)} %bitcast.4, bf16[1600,256]{1,0:T(8,128)(2,1)} %bitcast.14), kind=kLoop, calls=%fused_computation.5 | loop fusion | flops 163840 | bytes 1310721 | tf_op jit(solution)/shard_map/jit(_where)/select_n | solution.py:223
  2.1 4.7 %collective-permute-start.2 = (bf16[640,256]{1,0:T(8,128)(2,1)}, bf16[640,256]{1,0:T(8,128)(2,1)}, u32[]{:S(2)}, u32[]{:S(2)}) collective-permute-start(bf16[640,256]{1,0:T(8,128)(2,1)} %get-tuple-element.47), channel_id=1, source_target_pairs={{0,3},{1,2},{2,5},{3,0},{4,7},{5,6},{6,9},{7,4},{8,11},{9,10},{10,... | collective-permute-start | bytes 983048 | tf_op jit(solution)/shard_map/ppermute | solution.py:223
  6.7 0.0 copy-start.2
  6.7 1.5 %collective-permute-start.1 = (bf16[640,256]{1,0:T(8,128)(2,1)}, bf16[640,256]{1,0:T(8,128)(2,1)}, u32[]{:S(2)}, u32[]{:S(2)}) collective-permute-start(bf16[640,256]{1,0:T(8,128)(2,1)} %get-tuple-element.48), channel_id=1, source_target_pairs={{1,5},{3,7},{5,9},{7,11},{9,13},{11,15},{13,17},{15,19},{17,21},{1... | collective-permute-start | bytes 983048 | tf_op jit(solution)/shard_map/ppermute | solution.py:223
  8.3 2.0 %fusion = (bf16[960,256]{1,0:T(8,128)(2,1)}, bf16[960,256]{1,0:T(8,128)(2,1)}) fusion(bf16[1600,256]{1,0:T(8,128)(2,1)} %bitcast.15, bf16[1600,256]{1,0:T(8,128)(2,1)S(1)} %bitcast.5, pred[]{:T(512)S(6)} %eq.6), kind=kLoop, calls=%fused_computation.6 | loop fusion | flops 245760 | bytes 1966081 | tf_op jit(solution)/shard_map/slice | solution.py:221
  10.3 0.7 collective-permute-start.6
  11.0 10.7 %collective-permute-start.5 = (bf16[960,256]{1,0:T(8,128)(2,1)}, bf16[960,256]{1,0:T(8,128)(2,1)S(1)}, u32[]{:S(2)}, u32[]{:S(2)}) collective-permute-start(bf16[960,256]{1,0:T(8,128)(2,1)} %get-tuple-element.44), channel_id=1, source_target_pairs={{0,3},{1,2},{2,5},{3,0},{4,7},{5,6},{6,9},{7,4},{8,11},{9,10},{10,... | collective-permute-start | bytes 1474568 | tf_op jit(solution)/shard_map/ppermute | solution.py:224
  21.8 1.9 %collective-permute-start = (bf16[1600,256]{1,0:T(8,128)(2,1)S(1)}, bf16[1600,256]{1,0:T(8,128)(2,1)S(1)}, u32[]{:S(2)}, u32[]{:S(2)}) collective-permute-start(bf16[1600,256]{1,0:T(8,128)(2,1)S(1)} %bitcast.22), channel_id=1, source_target_pairs={{0,1},{1,0},{2,3},{3,2},{4,5},{5,4},{6,7},{7,6},{8,9},{9,8},{10,11... | collective-permute-start | bytes 2457608 | tf_op jit(solution)/shard_map/ppermute | solution.py:225
  23.7 1.0 %broadcast_select_fusion.3 = (bf16[640,256]{1,0:T(8,128)(2,1)S(1)}, bf16[640,256]{1,0:T(8,128)(2,1)S(1)}) fusion(bf16[640,256]{1,0:T(8,128)(2,1)} %collective-permute-done.2.refs_3_, pred[]{:T(512)S(6)} %eq.7, bf16[1600,256]{1,0:T(8,128)(2,1)S(1)} %bitcast.6, bf16[640,256]{1,0:T(8,128)(2,1)} %collective-permute-done.1.refs_5_, pred[]{:T(512)S(6)} %eq.6), kind=kLoop, calls=%fused_computation.3 | loop fusion | flops 327680 | bytes 1638402 | tf_op jit(solution)/shard_map/jit(_where)/select_n | solution.py:226
  24.8 2.6 %collective-permute-start.4 = (bf16[640,256]{1,0:T(8,128)(2,1)S(1)}, bf16[640,256]{1,0:T(8,128)(2,1)S(1)}, u32[]{:S(2)}, u32[]{:S(2)}) collective-permute-start(bf16[640,256]{1,0:T(8,128)(2,1)S(1)} %get-tuple-element.45), channel_id=1, source_target_pairs={{0,4},{1,5},{3,7},{4,8},{5,9},{7,11},{8,12},{9,13},{11,15},{12,16}... | collective-permute-start | bytes 983048 | tf_op jit(solution)/shard_map/ppermute | solution.py:228
  27.4 0.0 copy-start.1
  27.4 7.7 %collective-permute-start.3 = (bf16[640,256]{1,0:T(8,128)(2,1)S(1)}, bf16[640,256]{1,0:T(8,128)(2,1)S(1)}, u32[]{:S(2)}, u32[]{:S(2)}) collective-permute-start(bf16[640,256]{1,0:T(8,128)(2,1)S(1)} %get-tuple-element.46), channel_id=1, source_target_pairs={{0,3},{1,2},{2,5},{3,0},{4,7},{5,6},{6,9},{7,4},{8,11},{9,10},{10,... | collective-permute-start | bytes 983048 | tf_op jit(solution)/shard_map/ppermute | solution.py:228
  35.0 0.0 collective-permute-done.6.refs_5_
  35.1 0.0 collective-permute-done.5.refs_3_
  35.1 0.1 broadcast_select_fusion
  35.2 2.6 %collective-permute-start.8 = (bf16[960,256]{1,0:T(8,128)(2,1)S(1)}, bf16[960,256]{1,0:T(8,128)(2,1)S(1)}, u32[]{:S(2)}, u32[]{:S(2)}) collective-permute-start(bf16[960,256]{1,0:T(8,128)(2,1)S(1)} %get-tuple-element.41), channel_id=1, source_target_pairs={{0,4},{1,5},{3,7},{4,8},{5,9},{7,11},{8,12},{9,13},{11,15},{12,16}... | collective-permute-start | bytes 1474568 | tf_op jit(solution)/shard_map/ppermute | solution.py:231
  37.8 6.6 %collective-permute-start.7 = (bf16[960,256]{1,0:T(8,128)(2,1)S(1)}, bf16[960,256]{1,0:T(8,128)(2,1)S(1)}, u32[]{:S(2)}, u32[]{:S(2)}) collective-permute-start(bf16[960,256]{1,0:T(8,128)(2,1)S(1)} %get-tuple-element.42), channel_id=1, source_target_pairs={{0,3},{1,2},{2,5},{3,0},{4,7},{5,6},{6,9},{7,4},{8,11},{9,10},{10,... | collective-permute-start | bytes 1474568 | tf_op jit(solution)/shard_map/ppermute | solution.py:231
  44.4 0.0 collective-permute-done.refs_0_
  44.4 3.5 %mate.3 = bf16[672,256]{1,0:T(8,128)(2,1)S(1)} custom-call(bf16[1600,256]{1,0:T(8,128)(2,1)S(1)} %collective-permute-done.refs_0_, bf16[1600,256]{1,0:T(8,128)(2,1)S(1)} %bitcast.16, bf16[1600,256]{1,0:T(8,128)(2,1)S(1)} %bitcast.8, bf16[640,256]{1,0:T(8,128)(2,1)} %collective-permute-done.2.refs_3_, bf16[640,256]{1,0:T(8,128)(2,1)S(1)} %collective-permute-done.3.refs_4_, ...), custom_call_target="tpu_custom_call" | custom-call | flops 2013265920 | bytes 1966080 | tf_op jit(solution)/shard_map/mate/pallas_call | solution.py:163
  47.9 1.9 %collective-permute-start.10 = (bf16[672,256]{1,0:T(8,128)(2,1)S(1)}, bf16[672,256]{1,0:T(8,128)(2,1)S(1)}, u32[]{:S(2)}, u32[]{:S(2)}) collective-permute-start(bf16[672,256]{1,0:T(8,128)(2,1)S(1)} %mate.3), channel_id=1, source_target_pairs={{0,1},{1,0},{2,3},{3,2},{4,5},{5,4},{6,7},{7,6},{8,9},{9,8},{10,11... | collective-permute-start | bytes 1032200 | tf_op jit(solution)/shard_map/ppermute | solution.py:239
  49.9 3.2 %own.4 = (f32[640,256]{1,0:T(8,128)S(1)}, f32[2,8,256]{2,1,0:T(8,128)S(1)}) custom-call(bf16[1600,256]{1,0:T(8,128)(2,1)S(1)} %bitcast.23, bf16[1600,256]{1,0:T(8,128)(2,1)S(1)} %bitcast.17, bf16[1600,256]{1,0:T(8,128)(2,1)S(1)} %bitcast.9, bf16[640,256]{1,0:T(8,128)(2,1)} %collective-permute-done.2.refs_3_, ...), custom_call_target="tpu_custom_call" | custom-call | flops 2013265920 | bytes 1966080 | tf_op jit(solution)/shard_map/own/pallas_call | solution.py:163
  53.1 2.4 %mate.4 = bf16[672,256]{1,0:T(8,128)(2,1)S(1)} custom-call(bf16[1600,256]{1,0:T(8,128)(2,1)S(1)} %collective-permute-done.refs_0_, bf16[1600,256]{1,0:T(8,128)(2,1)S(1)} %bitcast.18, bf16[1600,256]{1,0:T(8,128)(2,1)S(1)} %bitcast.10, bf16[960,256]{1,0:T(8,128)(2,1)S(1)} %collective-permute-done.5.refs_3_, ...), custom_call_target="tpu_custom_call" | custom-call | flops 2013265920 | bytes 1966080 | tf_op jit(solution)/shard_map/mate/pallas_call | solution.py:163
  55.6 3.9 %collective-permute-start.11 = (bf16[672,256]{1,0:T(8,128)(2,1)S(1)}, bf16[672,256]{1,0:T(8,128)(2,1)S(1)}, u32[]{:S(2)}, u32[]{:S(2)}) collective-permute-start(bf16[672,256]{1,0:T(8,128)(2,1)S(1)} %mate.4), channel_id=1, source_target_pairs={{0,1},{1,0},{2,3},{3,2},{4,5},{5,4},{6,7},{7,6},{8,9},{9,8},{10,11... | collective-permute-start | bytes 1032200 | tf_op jit(solution)/shard_map/ppermute | solution.py:239
  59.5 1.2 %mate.5 = bf16[336,256]{1,0:T(8,128)(2,1)S(1)} custom-call(bf16[1600,256]{1,0:T(8,128)(2,1)S(1)} %collective-permute-done.refs_0_, bf16[1600,256]{1,0:T(8,128)(2,1)S(1)} %bitcast.19, bf16[1600,256]{1,0:T(8,128)(2,1)S(1)} %bitcast.11, bf16[960,256]{1,0:T(8,128)(2,1)S(1)} %collective-permute-done.5.refs_3_, ...), custom_call_target="tpu_custom_call" | custom-call | flops 1006632960 | bytes 983040 | tf_op jit(solution)/shard_map/mate/pallas_call | solution.py:163
  60.7 1.9 %collective-permute-start.9 = (bf16[336,256]{1,0:T(8,128)(2,1)S(1)}, bf16[336,256]{1,0:T(8,128)(2,1)S(1)}, u32[]{:S(2)}, u32[]{:S(2)}) collective-permute-start(bf16[336,256]{1,0:T(8,128)(2,1)S(1)} %mate.5), channel_id=1, source_target_pairs={{0,1},{1,0},{2,3},{3,2},{4,5},{5,4},{6,7},{7,6},{8,9},{9,8},{10,11... | collective-permute-start | bytes 516104 | tf_op jit(solution)/shard_map/ppermute | solution.py:239
  62.6 1.1 %own.3 = (f32[320,256]{1,0:T(8,128)S(1)}, f32[1,8,256]{2,1,0:T(8,128)S(1)}) custom-call(bf16[1600,256]{1,0:T(8,128)(2,1)S(1)} %bitcast.24, bf16[1600,256]{1,0:T(8,128)(2,1)S(1)} %bitcast.20, bf16[1600,256]{1,0:T(8,128)(2,1)S(1)} %bitcast.12, bf16[960,256]{1,0:T(8,128)(2,1)S(1)} %collective-permute-done.5.refs_3_, ...), custom_call_target="tpu_custom_call" | custom-call | flops 1006632960 | bytes 983040 | tf_op jit(solution)/shard_map/own/pallas_call | solution.py:163
  63.7 2.2 %own.5 = (f32[640,256]{1,0:T(8,128)S(1)}, f32[2,8,256]{2,1,0:T(8,128)S(1)}) custom-call(bf16[1600,256]{1,0:T(8,128)(2,1)S(1)} %bitcast.25, bf16[1600,256]{1,0:T(8,128)(2,1)S(1)} %bitcast.21, bf16[1600,256]{1,0:T(8,128)(2,1)S(1)} %bitcast.13, bf16[960,256]{1,0:T(8,128)(2,1)S(1)} %collective-permute-done.5.refs_3_, ...), custom_call_target="tpu_custom_call" | custom-call | flops 2013265920 | bytes 1966080 | tf_op jit(solution)/shard_map/own/pallas_call | solution.py:163
  65.9 0.1 merge.3.rest_0_
  66.1 0.5 collective-permute-done.11.msg
  66.5 0.1 merge.4.rest_1_
  66.7 1.7 %collective-permute-done.9.msg = bf16[336,256]{1,0:T(8,128)(2,1)S(1)} collective-permute-done((bf16[336,256]{1,0:T(8,128)(2,1)S(1)}, bf16[336,256]{1,0:T(8,128)(2,1)S(1)}, u32[]{:S(2)}, u32[]{:S(2)}) %collective-permute-start.9) | collective-permute-done | bytes 172064 | tf_op jit(solution)/shard_map/ppermute | solution.py:239
  68.4 1.0 %merge.5 = bf16[1600,256]{1,0:T(8,128)(2,1)} custom-call(f32[320,256]{1,0:T(8,128)S(1)} %get-tuple-element.32.part, f32[1,8,256]{2,1,0:T(8,128)S(1)} %get-tuple-element.33.part_lse, bf16[336,256]{1,0:T(8,128)(2,1)S(1)} %collective-permute-done.9.msg, bf16[640,256]{1,0:T(8,128)(2,1)S(1)} %merge.3.rest_0_, bf16[640,256]{1,0:T(8,128)(2,1)S(1)} %merge.4.rest_1_), custom_call_target="tpu_custom_call" | custom-call | flops 327680 | bytes 655360 | tf_op jit(solution)/shard_map/merge/pallas_call | solution.py:198
  (11 shorter events, 0.0 us)
Async XLA Ops:
  0.0 8.3 %copy-start = (bf16[256,1600]{0,1:T(8,128)(2,1)S(1)}, bf16[256,1600]{0,1:T(8,128)(2,1)}, u32[]{:S(2)}) copy-start(bf16[256,1600]{0,1:T(8,128)(2,1)} %param.5) | copy-start | bytes 2457604
  2.1 21.6 %collective-permute-start.2 = (bf16[640,256]{1,0:T(8,128)(2,1)}, bf16[640,256]{1,0:T(8,128)(2,1)}, u32[]{:S(2)}, u32[]{:S(2)}) collective-permute-start(bf16[640,256]{1,0:T(8,128)(2,1)} %get-tuple-element.47), channel_id=1, source_target_pairs={{0,3},{1,2},{2,5},{3,0},{4,7},{5,6},{6,9},{7,4},{8,11},{9,10},{10,... | collective-permute-start | bytes 983048 | tf_op jit(solution)/shard_map/ppermute | solution.py:223
  6.7 15.0 %copy-start.2 = (bf16[256,1600]{0,1:T(8,128)(2,1)S(1)}, bf16[256,1600]{0,1:T(8,128)(2,1)}, u32[]{:S(2)}) copy-start(bf16[256,1600]{0,1:T(8,128)(2,1)} %param.3) | copy-start | bytes 2457604
  6.7 17.0 %collective-permute-start.1 = (bf16[640,256]{1,0:T(8,128)(2,1)}, bf16[640,256]{1,0:T(8,128)(2,1)}, u32[]{:S(2)}, u32[]{:S(2)}) collective-permute-start(bf16[640,256]{1,0:T(8,128)(2,1)} %get-tuple-element.48), channel_id=1, source_target_pairs={{1,5},{3,7},{5,9},{7,11},{9,13},{11,15},{13,17},{15,19},{17,21},{1... | collective-permute-start | bytes 983048 | tf_op jit(solution)/shard_map/ppermute | solution.py:223
  10.3 24.7 %collective-permute-start.6 = (bf16[960,256]{1,0:T(8,128)(2,1)}, bf16[960,256]{1,0:T(8,128)(2,1)S(1)}, u32[]{:S(2)}, u32[]{:S(2)}) collective-permute-start(bf16[960,256]{1,0:T(8,128)(2,1)} %get-tuple-element.43), channel_id=1, source_target_pairs={{1,5},{3,7},{5,9},{7,11},{9,13},{11,15},{13,17},{15,19},{17,21},{1... | collective-permute-start | bytes 1474568 | tf_op jit(solution)/shard_map/ppermute | solution.py:224
  11.0 24.1 %collective-permute-start.5 = (bf16[960,256]{1,0:T(8,128)(2,1)}, bf16[960,256]{1,0:T(8,128)(2,1)S(1)}, u32[]{:S(2)}, u32[]{:S(2)}) collective-permute-start(bf16[960,256]{1,0:T(8,128)(2,1)} %get-tuple-element.44), channel_id=1, source_target_pairs={{0,3},{1,2},{2,5},{3,0},{4,7},{5,6},{6,9},{7,4},{8,11},{9,10},{10,... | collective-permute-start | bytes 1474568 | tf_op jit(solution)/shard_map/ppermute | solution.py:224
  21.8 22.6 %collective-permute-start = (bf16[1600,256]{1,0:T(8,128)(2,1)S(1)}, bf16[1600,256]{1,0:T(8,128)(2,1)S(1)}, u32[]{:S(2)}, u32[]{:S(2)}) collective-permute-start(bf16[1600,256]{1,0:T(8,128)(2,1)S(1)} %bitcast.22), channel_id=1, source_target_pairs={{0,1},{1,0},{2,3},{3,2},{4,5},{5,4},{6,7},{7,6},{8,9},{9,8},{10,11... | collective-permute-start | bytes 2457608 | tf_op jit(solution)/shard_map/ppermute | solution.py:225
  24.8 19.6 %collective-permute-start.4 = (bf16[640,256]{1,0:T(8,128)(2,1)S(1)}, bf16[640,256]{1,0:T(8,128)(2,1)S(1)}, u32[]{:S(2)}, u32[]{:S(2)}) collective-permute-start(bf16[640,256]{1,0:T(8,128)(2,1)S(1)} %get-tuple-element.45), channel_id=1, source_target_pairs={{0,4},{1,5},{3,7},{4,8},{5,9},{7,11},{8,12},{9,13},{11,15},{12,16}... | collective-permute-start | bytes 983048 | tf_op jit(solution)/shard_map/ppermute | solution.py:228
  27.4 17.1 %copy-start.1 = (bf16[256,1600]{0,1:T(8,128)(2,1)S(1)}, bf16[256,1600]{0,1:T(8,128)(2,1)}, u32[]{:S(2)}) copy-start(bf16[256,1600]{0,1:T(8,128)(2,1)} %param.4) | copy-start | bytes 2457604
  27.4 17.0 %collective-permute-start.3 = (bf16[640,256]{1,0:T(8,128)(2,1)S(1)}, bf16[640,256]{1,0:T(8,128)(2,1)S(1)}, u32[]{:S(2)}, u32[]{:S(2)}) collective-permute-start(bf16[640,256]{1,0:T(8,128)(2,1)S(1)} %get-tuple-element.46), channel_id=1, source_target_pairs={{0,3},{1,2},{2,5},{3,0},{4,7},{5,6},{6,9},{7,4},{8,11},{9,10},{10,... | collective-permute-start | bytes 983048 | tf_op jit(solution)/shard_map/ppermute | solution.py:228
  35.2 17.9 %collective-permute-start.8 = (bf16[960,256]{1,0:T(8,128)(2,1)S(1)}, bf16[960,256]{1,0:T(8,128)(2,1)S(1)}, u32[]{:S(2)}, u32[]{:S(2)}) collective-permute-start(bf16[960,256]{1,0:T(8,128)(2,1)S(1)} %get-tuple-element.41), channel_id=1, source_target_pairs={{0,4},{1,5},{3,7},{4,8},{5,9},{7,11},{8,12},{9,13},{11,15},{12,16}... | collective-permute-start | bytes 1474568 | tf_op jit(solution)/shard_map/ppermute | solution.py:231
  37.8 15.3 %collective-permute-start.7 = (bf16[960,256]{1,0:T(8,128)(2,1)S(1)}, bf16[960,256]{1,0:T(8,128)(2,1)S(1)}, u32[]{:S(2)}, u32[]{:S(2)}) collective-permute-start(bf16[960,256]{1,0:T(8,128)(2,1)S(1)} %get-tuple-element.42), channel_id=1, source_target_pairs={{0,3},{1,2},{2,5},{3,0},{4,7},{5,6},{6,9},{7,4},{8,11},{9,10},{10,... | collective-permute-start | bytes 1474568 | tf_op jit(solution)/shard_map/ppermute | solution.py:231
  47.9 18.0 %collective-permute-start.10 = (bf16[672,256]{1,0:T(8,128)(2,1)S(1)}, bf16[672,256]{1,0:T(8,128)(2,1)S(1)}, u32[]{:S(2)}, u32[]{:S(2)}) collective-permute-start(bf16[672,256]{1,0:T(8,128)(2,1)S(1)} %mate.3), channel_id=1, source_target_pairs={{0,1},{1,0},{2,3},{3,2},{4,5},{5,4},{6,7},{7,6},{8,9},{9,8},{10,11... | collective-permute-start | bytes 1032200 | tf_op jit(solution)/shard_map/ppermute | solution.py:239
  55.6 11.0 %collective-permute-start.11 = (bf16[672,256]{1,0:T(8,128)(2,1)S(1)}, bf16[672,256]{1,0:T(8,128)(2,1)S(1)}, u32[]{:S(2)}, u32[]{:S(2)}) collective-permute-start(bf16[672,256]{1,0:T(8,128)(2,1)S(1)} %mate.4), channel_id=1, source_target_pairs={{0,1},{1,0},{2,3},{3,2},{4,5},{5,4},{6,7},{7,6},{8,9},{9,8},{10,11... | collective-permute-start | bytes 1032200 | tf_op jit(solution)/shard_map/ppermute | solution.py:239
  60.7 7.7 %collective-permute-start.9 = (bf16[336,256]{1,0:T(8,128)(2,1)S(1)}, bf16[336,256]{1,0:T(8,128)(2,1)S(1)}, u32[]{:S(2)}, u32[]{:S(2)}) collective-permute-start(bf16[336,256]{1,0:T(8,128)(2,1)S(1)} %mate.5), channel_id=1, source_target_pairs={{0,1},{1,0},{2,3},{3,2},{4,5},{5,4},{6,7},{7,6},{8,9},{9,8},{10,11... | collective-permute-start | bytes 516104 | tf_op jit(solution)/shard_map/ppermute | solution.py:239
